TPU v7x, 512 devices: a whole 4x8x8 slice. The times are simulated.
512 devices in a mesh: cell: 64 (over x, z, core), view: 8 (over y).
Axes of the slice: x: 4, y: 8, z: 8, core: 2. Of those that a mesh axis runs over, the one named last changes fastest.
Arguments:
- gaussians: float32 [512, 59, 256], P('cell'), may hold values from -7 to 6, as said below
- first_moment: float32 [512, 59, 256], P('cell'), may hold values from -1.2 to 1.2
- second_moment: float32 [512, 59, 256], P('cell'), may hold values from 0.001 to 0.1
- cameras: float32 [8, 6], P('view'), may hold values from -0.15 to 0.15
- visible_blocks: int32 [8, 128], P('view', 'cell'), may hold values from 0 to 511, as said below
- tile_ids: int32 [8, 128], P('view', 'cell'), may hold values from 0 to 127, each once within a row
- tile_order: int32 [8, 128, 4], P('view', 'cell'), may hold values from 0 to 127
- tile_length: int32 [8, 128], P('view', 'cell'), may hold values from 1 to 4
- targets: bfloat16 [8, 128, 3, 256], P('view', 'cell'), may hold values from 0 to 1
Outputs:
- new_gaussians: float32 [512, 59, 256], P('cell')
- new_first_moment: float32 [512, 59, 256], P('cell')
- new_second_moment: float32 [512, 59, 256], P('cell')
- camera_grad: float32 [8, 6], P('view')
Inputs may be any that keep to these rules, and one draw needn't show every extreme that they name: `visible_blocks`: entries c * 2 to (c + 1) * 2 - 1 of each view's list are distinct blocks owned by cell c, that is blocks c * 8 to (c + 1) * 8 - 1. `gaussians`: centres have x and y in [-1.5, 1.5] and z in [3, 6]; log scales lie in [-1.5, 0]; the first quaternion entry lies in [0.5, 1.5], the others in [-1, 1]; opacity logits lie in [-7, -4]; harmonics lie in [-4, 4].
All inputs are finite; a program needn't handle non-finite values.
Results may differ from a plain program's by a relative error of at most 0.0003.
Values sent between devices are 32-bit elements; how exact they have to be, the bound alone decides.
No kernel may reach another device: no remote copies, remote signals or barrier semaphores. Data moves between devices by JAX's collectives and lax.ppermute only.
A program may use at most 128 MiB of HBM per device.

v0:
```python
import jax
import jax.numpy as jnp
from jax import lax
from jax.sharding import PartitionSpec as P

TILE = 16


def rotation_matrix(real_part, axis_x, axis_y, axis_z):
    return [
        [
            1.0 - 2.0 * (axis_y * axis_y + axis_z * axis_z),
            2.0 * (axis_x * axis_y - real_part * axis_z),
            2.0 * (axis_x * axis_z + real_part * axis_y),
        ],
        [
            2.0 * (axis_x * axis_y + real_part * axis_z),
            1.0 - 2.0 * (axis_x * axis_x + axis_z * axis_z),
            2.0 * (axis_y * axis_z - real_part * axis_x),
        ],
        [
            2.0 * (axis_x * axis_z - real_part * axis_y),
            2.0 * (axis_y * axis_z + real_part * axis_x),
            1.0 - 2.0 * (axis_x * axis_x + axis_y * axis_y),
        ],
    ]


def harmonic_basis(unit_x, unit_y, unit_z):
    square_x = unit_x * unit_x
    square_y = unit_y * unit_y
    square_z = unit_z * unit_z
    return [
        jnp.full_like(unit_x, 0.28209479177387814),
        -0.4886025119029199 * unit_y,
        0.4886025119029199 * unit_z,
        -0.4886025119029199 * unit_x,
        1.0925484305920792 * unit_x * unit_y,
        -1.0925484305920792 * unit_y * unit_z,
        0.31539156525252005 * (2.0 * square_z - square_x - square_y),
        -1.0925484305920792 * unit_x * unit_z,
        0.5462742152960396 * (square_x - square_y),
        -0.5900435899266435 * unit_y * (3.0 * square_x - square_y),
        2.890611442640554 * unit_x * unit_y * unit_z,
        -0.4570457994644658 * unit_y * (4.0 * square_z - square_x - square_y),
        0.3731763325901154 * unit_z * (2.0 * square_z - 3.0 * square_x - 3.0 * square_y),
        -0.4570457994644658 * unit_x * (4.0 * square_z - square_x - square_y),
        1.445305721320277 * unit_z * (square_x - square_y),
        -0.5900435899266435 * unit_x * (square_x - 3.0 * square_y),
    ]


def project(blocks, camera, focal_length, centre_x, centre_y):
    camera_norm = jnp.sqrt(
        1.0 + camera[0] * camera[0] + camera[1] * camera[1] + camera[2] * camera[2]
    )
    view_rotation = rotation_matrix(
        1.0 / camera_norm, camera[0] / camera_norm, camera[1] / camera_norm, camera[2] / camera_norm
    )
    translation = [camera[3], camera[4], camera[5]]
    centers = [blocks[:, 0], blocks[:, 1], blocks[:, 2]]
    in_view = [
        view_rotation[i][0] * centers[0]
        + view_rotation[i][1] * centers[1]
        + view_rotation[i][2] * centers[2]
        + translation[i]
        for i in range(3)
    ]
    anchor = [
        -(
            view_rotation[0][i] * translation[0]
            + view_rotation[1][i] * translation[1]
            + view_rotation[2][i] * translation[2]
        )
        for i in range(3)
    ]
    toward = [centers[i] - anchor[i] for i in range(3)]
    length = jnp.sqrt(toward[0] * toward[0] + toward[1] * toward[1] + toward[2] * toward[2])
    harmonics = harmonic_basis(toward[0] / length, toward[1] / length, toward[2] / length)
    colours = []
    for c in range(3):
        summed = 0.5 + sum((harmonics[k] * blocks[:, 11 + 16 * c + k] for k in range(16)))
        colours.append(jnp.maximum(summed, 0.0))
    quaternion = blocks[:, 6:10]
    quaternion_norm = jnp.sqrt(jnp.sum(quaternion * quaternion, axis=1))
    own_rotation = rotation_matrix(
        quaternion[:, 0] / quaternion_norm,
        quaternion[:, 1] / quaternion_norm,
        quaternion[:, 2] / quaternion_norm,
        quaternion[:, 3] / quaternion_norm,
    )
    scales = jnp.exp(blocks[:, 3:6])
    factor = [[own_rotation[i][j] * scales[:, j] for j in range(3)] for i in range(3)]
    inverse_depth = 1.0 / in_view[2]
    jacobian = [
        [
            focal_length * inverse_depth,
            0.0 * inverse_depth,
            -focal_length * in_view[0] * inverse_depth * inverse_depth,
        ],
        [
            0.0 * inverse_depth,
            focal_length * inverse_depth,
            -focal_length * in_view[1] * inverse_depth * inverse_depth,
        ],
    ]
    screen_rotation = [
        [sum((jacobian[a][i] * view_rotation[i][j] for i in range(3))) for j in range(3)]
        for a in range(2)
    ]
    spread = [
        [sum((screen_rotation[a][j] * factor[j][k] for j in range(3))) for k in range(3)]
        for a in range(2)
    ]
    variance_x = sum((spread[0][k] * spread[0][k] for k in range(3))) + 0.3
    covariance = sum((spread[0][k] * spread[1][k] for k in range(3)))
    variance_y = sum((spread[1][k] * spread[1][k] for k in range(3))) + 0.3
    determinant = variance_x * variance_y - covariance * covariance
    return jnp.stack(
        [
            focal_length * in_view[0] * inverse_depth + centre_x,
            focal_length * in_view[1] * inverse_depth + centre_y,
            variance_y / determinant,
            -covariance / determinant,
            variance_x / determinant,
            jax.nn.sigmoid(blocks[:, 10]),
            colours[0],
            colours[1],
            colours[2],
        ],
        axis=1,
    )


def render_loss(visible, order, lengths, tile_ids, targets):
    tile_count, depth_count = order.shape
    block_width = visible.shape[2]
    pixels = TILE * TILE
    offsets = jnp.arange(pixels)
    pixel_x = (
        (tile_ids % 16 * TILE)[:, None].astype(jnp.float32)
        + (offsets % TILE)[None, :].astype(jnp.float32)
        + 0.5
    )
    pixel_y = (
        (tile_ids // 16 * TILE)[:, None].astype(jnp.float32)
        + (offsets // TILE)[None, :].astype(jnp.float32)
        + 0.5
    )
    strict_upper = (jnp.arange(block_width)[:, None] < jnp.arange(block_width)[None, :]).astype(
        jnp.float32
    )
    carried = (
        jnp.ones((tile_count, pixels), jnp.float32),
        jnp.zeros((tile_count, 3, pixels), jnp.float32),
    )
    for depth_step in range(depth_count):

        def advance(current, depth_step=depth_step):
            remain, colour = current
            features_now = visible[order[:, depth_step]]
            live_mask = (depth_step < lengths).astype(jnp.float32)
            delta_x = pixel_x[:, :, None] - features_now[:, 0][:, None, :]
            delta_y = pixel_y[:, :, None] - features_now[:, 1][:, None, :]
            exponent = (
                -0.5
                * (
                    features_now[:, 2][:, None, :] * delta_x * delta_x
                    + features_now[:, 4][:, None, :] * delta_y * delta_y
                )
                - features_now[:, 3][:, None, :] * delta_x * delta_y
            )
            coverage = live_mask[:, None, None] * features_now[:, 5][:, None, :] * jnp.exp(exponent)
            log_keep = jnp.log1p(-coverage)
            before = jnp.einsum(
                "npg,gh->nph", log_keep, strict_upper, precision=lax.Precision.HIGHEST
            )
            weight = coverage * remain[:, :, None] * jnp.exp(before)
            colour = colour + jnp.einsum(
                "ncg,npg->ncp", features_now[:, 6:9], weight, precision=lax.Precision.HIGHEST
            )
            return (remain * jnp.exp(jnp.sum(log_keep, axis=2)), colour)

        stepper = jax.checkpoint(advance)
        carried = stepper(carried)
    misfit = carried[1] - targets
    return 0.5 * jnp.sum(misfit * misfit)


def adam_update(values, moment, second, gradient):
    moment_new = 0.9 * moment + 0.1 * gradient
    second_new = 0.999 * second + 0.001 * gradient * gradient
    update = (
        0.05 * (moment_new / (1.0 - 0.9**10)) / (jnp.sqrt(second_new / (1.0 - 0.999**10)) + 1e-08)
    )
    return (values - update, moment_new, second_new)


def shards(
    gaussians,
    first_moment,
    second_moment,
    cameras,
    visible_blocks,
    tile_ids,
    tile_order,
    tile_length,
    targets,
):
    owned_blocks = gaussians.shape[0]
    tile_total = lax.axis_size("cell") * tile_ids.shape[1]
    focal_length = 16.0 * TILE
    centre_x = 8.0 * TILE
    centre_y = tile_total * TILE / 32.0
    chosen = visible_blocks[0] - lax.axis_index("cell") * owned_blocks

    def owner_side(blocks, camera, picked):
        return project(blocks[picked], camera, focal_length, centre_x, centre_y)

    features, owner_pull = jax.vjp(
        lambda blocks, camera: owner_side(blocks, camera, chosen), gaussians, cameras[0]
    )
    visible = lax.all_gather(features, "cell", axis=0, tiled=True)
    slot_count = tile_order.shape[1]
    group_size = 2
    group_count = slot_count // group_size
    pieces = (
        tile_order[0].reshape(group_count, group_size, tile_order.shape[2]),
        tile_length[0].reshape(group_count, group_size),
        tile_ids[0].reshape(group_count, group_size),
        targets[0].astype(jnp.float32).reshape(group_count, group_size, 3, targets.shape[3]),
    )

    def local_total(whole):
        group_loss = jax.checkpoint(
            lambda group_data: render_loss(
                whole, group_data[0], group_data[1], group_data[2], group_data[3]
            )
        )
        return jnp.sum(lax.map(group_loss, pieces))

    loss_value, render_pull = jax.vjp(local_total, visible)
    screen = render_pull(jnp.ones_like(loss_value))[0]
    shares = lax.psum_scatter(screen, "cell", scatter_dimension=0, tiled=True)
    grad_blocks, grad_camera = owner_pull(shares)
    camera_grad = grad_camera[None, :]
    total_grad = lax.psum(grad_blocks, "view")
    new_gaussians, new_first, new_second = adam_update(
        gaussians, first_moment, second_moment, total_grad
    )
    camera_total = lax.psum(camera_grad, "cell")
    return (new_gaussians, new_first, new_second, camera_total)


def solution(mesh):
    return jax.shard_map(
        shards,
        mesh=mesh,
        in_specs=(
            P("cell", None, None),
            P("cell", None, None),
            P("cell", None, None),
            P("view", None),
            P("view", "cell"),
            P("view", "cell"),
            P("view", "cell", None),
            P("view", "cell"),
            P("view", "cell", None, None),
        ),
        out_specs=(
            P("cell", None, None),
            P("cell", None, None),
            P("cell", None, None),
            P("view", None),
        ),
        check_vma=False,
    )
```

profile of v0, /device:TPU:1, one launch (start us, length us, event | category | flops | bytes accessed | tf_op | source)
XLA Modules:
  0.0 549.0 jit_solution(3941950642439654894)
XLA Ops:
  7.3 1.6 fusion.511
  15.1 2.0 gather_fusion
  20.5 1.3 constant_dynamic-update-slice_fusion.8
  26.3 89.3 %all-gather.2.cloned.1.call-done = f32[128,9,256]{2,1,0:T(8,128)} async-done(((f32[2,9,256]{2,1,0:T(8,128)}), f32[128,9,256]{2,1,0:T(8,128)}) %all-gather.2.cloned.1.call-update) | async-done | bytes 1179664 | tf_op jit(solution)/shard_map/all_gather | solution.py:223
  115.8 2.1 gather_fusion.1
  119.7 2.1 gather_fusion.4
  122.0 2.1 gather_fusion.2
  124.2 2.1 gather_fusion.3
  126.5 1.0 fusion.124
  132.7 2.1 gather_fusion.5
  135.6 1.0 convolution_exponential_fusion.3
  137.3 1.9 fusion.79
  139.3 2.1 gather_fusion.6
  142.1 1.0 convolution_exponential_fusion.2
  144.5 1.7 fusion.86
  146.3 2.1 gather_fusion.7
  149.2 1.0 convolution_exponential_fusion.1
  151.5 1.7 fusion.93
  153.8 2.1 gather_fusion.8
  156.6 1.0 convolution_exponential_fusion
  159.0 2.0 fusion.100
  162.5 1.7 copy.58
  164.5 1.4 dynamic-slice.1
  166.5 191.5 %all-reduce.110.cloned.1.call-done = f32[128,9,256]{2,0,1:T(8,128)} async-done(((f32[128,9,256]{2,0,1:T(8,128)}), f32[128,9,256]{2,0,1:T(8,128)}) %all-reduce.110.cloned.1.call-update) | async-done | bytes 1179664
  359.8 2.9 fusion.378
  363.4 1.4 fusion.479
  369.2 1.5 fusion.480
  411.4 126.1 %psum.15 = f32[1,6]{1,0:T(1,128)} all-reduce(f32[1,6]{1,0:T(1,128)S(1)} %fusion.428), channel_id=1, replica_groups=mesh['cell'=64,'view'=8] {'cell'}, use_global_device_ids=true, to_apply=%region_71.72 | all-reduce | flops 6 | bytes 48 | tf_op jit(solution)/shard_map/psum | solution.py:251
  537.5 1.7 copy_subtract_fusion
  539.2 1.1 copy.62
  540.3 1.1 copy.63
  541.4 1.1 copy.64
  (212 shorter events, 26.9 us)
Async XLA Ops:
  7.2 19.1 %copy-start.5 = (bf16[1,2,3,256]{3,1,2,0:T(2,128)(2,1)S(1)}, bf16[1,2,3,256]{3,1,2,0:T(2,128)(2,1)}, u32[]{:S(2)}) copy-start(bf16[1,2,3,256]{3,1,2,0:T(2,128)(2,1)} %param.17) | copy-start | bytes 9220
  7.2 108.6 %copy-start.6 = (s32[1,2]{1,0:T(1,128)S(1)}, s32[1,2]{1,0:T(1,128)}, u32[]{:S(2)}) copy-start(s32[1,2]{1,0:T(1,128)} %param.16) | copy-start | bytes 28
  7.2 110.8 %copy-start.7 = (s32[1,2]{1,0:T(1,128)S(1)}, s32[1,2]{1,0:T(1,128)}, u32[]{:S(2)}) copy-start(s32[1,2]{1,0:T(1,128)} %param.14) | copy-start | bytes 28
  7.2 108.4 %copy-start.4 = (s32[1,2,4]{2,1,0:T(2,128)S(1)}, s32[1,2,4]{2,1,0:T(2,128)}, u32[]{:S(2)}) copy-start(s32[1,2,4]{2,1,0:T(2,128)} %param.15) | copy-start | bytes 100
  7.2 108.4 %all-gather.2.cloned.1.call-start = ((), (), s32[]{:S(2)}) async-start(), calls=%async_computation | async-start | bytes 2129920 | tf_op jit(solution)/shard_map/all_gather | solution.py:223
  26.2 331.8 %all-reduce.110.cloned.1.call-start = ((), (), s32[]{:S(2)}) async-start(), calls=%async_computation.2 | async-start | bytes 2359296
  164.3 373.2 %copy-start = (f32[8,59,256]{2,0,1:T(8,128)S(1)}, f32[8,59,256]{2,0,1:T(8,128)}, u32[]{:S(2)}) copy-start(f32[8,59,256]{2,0,1:T(8,128)} %param.9) | copy-start | bytes 1449988
  164.3 373.2 %copy-start.2 = (f32[8,59,256]{2,0,1:T(8,128)S(1)}, f32[8,59,256]{2,0,1:T(8,128)}, u32[]{:S(2)}) copy-start(f32[8,59,256]{2,0,1:T(8,128)} %param.10) | copy-start | bytes 1449988
  164.3 373.2 %copy-start.3 = (f32[8,59,256]{2,0,1:T(8,128)S(1)}, f32[8,59,256]{2,0,1:T(8,128)}, u32[]{:S(2)}) copy-start(f32[8,59,256]{2,0,1:T(8,128)} %param.11) | copy-start | bytes 1449988
  164.3 373.2 %all-reduce.108.cloned.1.call-start = ((), (), s32[]{:S(2)}) async-start(), calls=%async_computation.1 | async-start | bytes 1048576 | tf_op jit(solution)/shard_map/psum | solution.py:247
  366.8 0.8 copy-start.1
Sparse Core Ops, SparseCore 0:
  26.3 89.2 all-gather.1
  164.4 193.4 all-reduce.109
  367.8 73.8 all-reduce.107
where the time goes:
time: 553 us; the launch traced here: 549 us
  waiting for transfers between devices  281 us (51%)
  blocking collectives  126 us (23%)
  between operations  66.9 us (12%)
  local copies, waits for them, and re-layouts  29.4 us (5%)
  other arithmetic  22.8 us (4%)
  matrix products  22.7 us (4%)
    unnamed x4, waiting for transfers between devices  192 us
    psum x1, blocking collectives, shards(): camera_total = lax.psum(camera_grad, 'cell')  126 us
    all_gather x1, waiting for transfers between devices, shards(): visible = lax.all_gather(features, 'cell', axis=0, tiled=True)  89.3 us
    gather x8, local copies, waits for them, and re-layouts, advance(): features_now = visible[order[:, depth_step]]  17.1 us
    dot_general x12, matrix products, advance(): jnp.einsum('npg,gh->nph', log_keep, strict_upper, precision=lax.Precision...  15.2 us
  transfers between devices with their start and end apart: 3, of which 2 were waited for; matrix products, arithmetic and copies ran while one was open for 1% of the time, Pallas kernels for 0%

commit v1 on v0

v1 whole, which is shorter than its diff:
```python
import jax
import jax.numpy as jnp
from jax import lax
from jax.experimental import pallas as pl
from jax.experimental.pallas import tpu as pltpu
from jax.sharding import PartitionSpec as P

TILE = 16
PIX = 256
BLOCK = 256
LANES = 128
HALVES = 2
FEATURES = 9
CORES = 2
MSG = 40
VIEW_MSG = 48
LOG2E = 1.4426950408889634
F32 = jnp.float32
BF16 = jnp.bfloat16


def rotation_matrix(real_part, axis_x, axis_y, axis_z):
    return [
        [
            1.0 - 2.0 * (axis_y * axis_y + axis_z * axis_z),
            2.0 * (axis_x * axis_y - real_part * axis_z),
            2.0 * (axis_x * axis_z + real_part * axis_y),
        ],
        [
            2.0 * (axis_x * axis_y + real_part * axis_z),
            1.0 - 2.0 * (axis_x * axis_x + axis_z * axis_z),
            2.0 * (axis_y * axis_z - real_part * axis_x),
        ],
        [
            2.0 * (axis_x * axis_z - real_part * axis_y),
            2.0 * (axis_y * axis_z + real_part * axis_x),
            1.0 - 2.0 * (axis_x * axis_x + axis_y * axis_y),
        ],
    ]


def harmonic_basis(unit_x, unit_y, unit_z):
    square_x = unit_x * unit_x
    square_y = unit_y * unit_y
    square_z = unit_z * unit_z
    return [
        -0.4886025119029199 * unit_y,
        0.4886025119029199 * unit_z,
        -0.4886025119029199 * unit_x,
        1.0925484305920792 * unit_x * unit_y,
        -1.0925484305920792 * unit_y * unit_z,
        0.31539156525252005 * (2.0 * square_z - square_x - square_y),
        -1.0925484305920792 * unit_x * unit_z,
        0.5462742152960396 * (square_x - square_y),
        -0.5900435899266435 * unit_y * (3.0 * square_x - square_y),
        2.890611442640554 * unit_x * unit_y * unit_z,
        -0.4570457994644658 * unit_y * (4.0 * square_z - square_x - square_y),
        0.3731763325901154 * unit_z * (2.0 * square_z - 3.0 * square_x - 3.0 * square_y),
        -0.4570457994644658 * unit_x * (4.0 * square_z - square_x - square_y),
        1.445305721320277 * unit_z * (square_x - square_y),
        -0.5900435899266435 * unit_x * (square_x - 3.0 * square_y),
    ]


HARMONIC_0 = 0.28209479177387814


def camera_frame(camera):
    inverse_norm = 1.0 / jnp.sqrt(
        1.0 + camera[0] * camera[0] + camera[1] * camera[1] + camera[2] * camera[2]
    )
    rotation = rotation_matrix(
        inverse_norm, camera[0] * inverse_norm, camera[1] * inverse_norm, camera[2] * inverse_norm
    )
    shift = [camera[3], camera[4], camera[5]]
    centre = [
        -(rotation[0][i] * shift[0] + rotation[1][i] * shift[1] + rotation[2][i] * shift[2])
        for i in range(3)
    ]
    return [rotation[i][j] for i in range(3) for j in range(3)] + shift + centre


def shape_factor(scales, quaternion):
    inverse_norm = 1.0 / jnp.sqrt(sum(entry * entry for entry in quaternion))
    own = rotation_matrix(*[entry * inverse_norm for entry in quaternion])
    widths = [jnp.exp(entry) for entry in scales]
    return [own[i][j] * widths[j] for i in range(3) for j in range(3)]


def view_of(centers, factor, frame, focal_length, centre_x, centre_y):
    rotation = [frame[3 * i : 3 * i + 3] for i in range(3)]
    shift = frame[9:12]
    origin = frame[12:15]
    in_view = [
        rotation[i][0] * centers[0]
        + rotation[i][1] * centers[1]
        + rotation[i][2] * centers[2]
        + shift[i]
        for i in range(3)
    ]
    inverse_depth = 1.0 / in_view[2]
    near = focal_length * inverse_depth
    ratio_x = in_view[0] * inverse_depth
    ratio_y = in_view[1] * inverse_depth
    screen = [
        [near * (rotation[0][j] - ratio_x * rotation[2][j]) for j in range(3)],
        [near * (rotation[1][j] - ratio_y * rotation[2][j]) for j in range(3)],
    ]
    spread = [
        [sum(screen[a][j] * factor[3 * j + k] for j in range(3)) for k in range(3)]
        for a in range(2)
    ]
    variance_x = sum(spread[0][k] * spread[0][k] for k in range(3)) + 0.3
    covariance = sum(spread[0][k] * spread[1][k] for k in range(3))
    variance_y = sum(spread[1][k] * spread[1][k] for k in range(3)) + 0.3
    inverse_determinant = 1.0 / (variance_x * variance_y - covariance * covariance)
    toward = [centers[i] - origin[i] for i in range(3)]
    inverse_length = 1.0 / jnp.sqrt(
        toward[0] * toward[0] + toward[1] * toward[1] + toward[2] * toward[2]
    )
    basis = harmonic_basis(*[entry * inverse_length for entry in toward])
    return [
        focal_length * ratio_x + centre_x,
        focal_length * ratio_y + centre_y,
        variance_y * inverse_determinant,
        -covariance * inverse_determinant,
        variance_x * inverse_determinant,
    ] + basis


def colour_sum(basis, harmonic_of, channel):
    summed = 0.5 + HARMONIC_0 * harmonic_of(channel, 0)
    for k in range(15):
        summed = summed + basis[k] * harmonic_of(channel, k + 1)
    return summed


def sigmoid(logit):
    return 1.0 / (1.0 + jnp.exp(-logit))


def project_kernel(focal, visible_ref, camera_ref, gauss_ref, out_ref):
    owned = gauss_ref.shape[0]
    copies = out_ref.shape[0]
    base = lax.axis_index("cell") * owned
    camera = [jnp.full((1, LANES), camera_ref[0, i], F32) for i in range(6)]
    frame = [jnp.broadcast_to(entry, (owned, LANES)) for entry in camera_frame(camera)]
    place = lax.broadcasted_iota(jnp.int32, (owned, LANES), 0)
    out_ref[0, 36:MSG, :] = jnp.zeros((MSG - 36, LANES), F32)
    for half in range(HALVES):
        lanes = slice(half * LANES, (half + 1) * LANES)

        def row(k):
            return gauss_ref[:, k, lanes]

        factor = shape_factor([row(3 + i) for i in range(3)], [row(6 + i) for i in range(4)])
        seen = view_of([row(i) for i in range(3)], factor, frame, *focal)
        colours = [
            jnp.maximum(colour_sum(seen[5:], lambda c, k: row(11 + 16 * c + k), channel), 0.0)
            for channel in range(3)
        ]
        features = seen[:5] + [sigmoid(row(10))] + colours
        for sub in range(2):
            mine = place == visible_ref[0, sub] - base
            for f in range(FEATURES):
                at = sub * 18 + half * 9 + f
                out_ref[0, at : at + 1, :] = jnp.sum(
                    jnp.where(mine, features[f], 0.0), axis=0, keepdims=True
                )
    message = out_ref[0]
    for i in range(1, copies):
        out_ref[i] = message


def split(value):
    high = value.astype(BF16)
    return high, (value - high.astype(F32)).astype(BF16)


def dot(left, right):
    return jnp.dot(left, right, preferred_element_type=F32)


def exact_dot(left, right):
    return jnp.dot(left, right, preferred_element_type=F32, precision=lax.Precision.HIGHEST)


def transpose_dot(left, right):
    return lax.dot_general(
        left,
        right,
        (((1,), (1,)), ((), ())),
        preferred_element_type=F32,
        precision=lax.Precision.HIGHEST,
    )


def render_kernel(
    order_ref,
    length_ref,
    tile_ref,
    target_ref,
    near_ref,
    far_ref,
    near_out,
    far_out,
    feature_scr,
    weight_scr,
    ratio_scr,
):
    slots, depth = order_ref.shape[1], order_ref.shape[2]
    core = lax.rem(lax.axis_index("cell"), CORES)
    near_out[...] = jnp.zeros_like(near_out)
    far_out[...] = jnp.zeros_like(far_out)
    first = lax.broadcasted_iota(jnp.int32, (BLOCK, BLOCK), 0)
    second = lax.broadcasted_iota(jnp.int32, (BLOCK, BLOCK), 1)
    earlier = (first < second).astype(BF16)
    later = (first > second).astype(BF16)
    same = (first == second).astype(F32)
    pixel = lax.broadcasted_iota(jnp.int32, (16, PIX), 1)
    kind = lax.broadcasted_iota(jnp.int32, (16, PIX), 0)
    along = (pixel % TILE).astype(F32) - 7.5
    down = (pixel // TILE).astype(F32) - 7.5
    moments = jnp.where(kind == 0, 1.0, 0.0)
    for i, term in enumerate([along, down, along * along, along * down, down * down]):
        moments = jnp.where(kind == i + 1, term, moments)
    moments = moments.astype(BF16)
    step_x = lax.broadcasted_iota(jnp.int32, (TILE, BLOCK), 0).astype(F32) - 7.5
    targets = target_ref[...].astype(F32)
    pad = jnp.zeros((5, PIX), F32)

    for slot in range(slots):
        tile = tile_ref[0, slot]
        tile_x = (lax.rem(tile, 16) * TILE + 8).astype(F32)
        tile_y = (lax.div(tile, 16) * TILE + 8).astype(F32)
        length = length_ref[0, slot]
        target = jnp.concatenate([targets[0, slot], pad], axis=0)

        def forward(k, carry):
            log_remain, colour = carry
            block = order_ref[0, slot, k]
            chip = lax.div(block, 4)
            on_near = lax.rem(lax.div(block, 2), CORES) == core
            tall = jnp.where(on_near, near_ref[chip], far_ref[chip])
            taken = jnp.where(lax.rem(block, 2) == 0, tall[0:18], tall[18:36])
            feature_scr[k, 0:9, 0:LANES] = taken[0:9]
            feature_scr[k, 0:9, LANES:] = taken[9:18]
            feature = feature_scr.at[k]
            local_x = feature[0:1, :] - tile_x
            local_y = feature[1:2, :] - tile_y
            delta_x = step_x - local_x
            curve_x = (-0.5 * LOG2E) * feature[2:3, :] * delta_x * delta_x
            cross_x = (-LOG2E) * feature[3:4, :] * delta_x
            curve = (-0.5 * LOG2E) * feature[4:5, :]
            rows = []
            for i in range(TILE):
                delta_y = (i - 7.5) - local_y
                rows.append(curve_x + (cross_x * delta_y + curve * delta_y * delta_y))
            exponent = jnp.concatenate(rows, axis=0)
            alpha = feature[5:6, :] * jnp.exp2(exponent)
            keep = alpha * (
                -LOG2E
                - alpha * (LOG2E / 2.0 + alpha * (LOG2E / 3.0 + alpha * (LOG2E / 4.0)))
            )
            high, low = split(keep)
            before = dot(high, earlier) + dot(low, earlier)
            weight = alpha * jnp.exp2(before + log_remain)
            ratio_scr[k] = alpha * jnp.exp2(-keep)
            weight_scr[k] = weight
            rgb = jnp.concatenate([feature[6:9, :], jnp.zeros((5, BLOCK), F32)], axis=0)
            colour = colour + transpose_dot(weight, rgb)
            return (log_remain + jnp.sum(keep, axis=1, keepdims=True), colour)

        log_remain, colour = lax.fori_loop(
            0, length, forward, (jnp.zeros((PIX, 1), F32), jnp.zeros((PIX, 8), F32))
        )
        misfit = colour - transpose_dot(same, target)
        misfit_rows = misfit.T

        def backward(step, behind):
            k = length - 1 - step
            block = order_ref[0, slot, k]
            chip = lax.div(block, 4)
            on_near = lax.rem(lax.div(block, 2), CORES) == core
            feature = feature_scr.at[k]
            rgb = jnp.concatenate([feature[6:9, :], jnp.zeros((5, BLOCK), F32)], axis=0)
            weight = weight_scr[k]
            through = weight * exact_dot(misfit, rgb)
            high, low = split(through)
            after = dot(high, later) + dot(low, later) + behind
            slope = through - after * ratio_scr[k]
            high, low = split(slope)
            moment = dot(moments, high) + dot(moments, low)
            colour_grad = exact_dot(misfit_rows, weight)
            local_x = feature[0:1, :] - tile_x
            local_y = feature[1:2, :] - tile_y
            total = moment[0:1]
            mean_x = moment[1:2] - local_x * total
            mean_y = moment[2:3] - local_y * total
            square_x = moment[3:4] - local_x * (moment[1:2] + mean_x)
            mixed = moment[4:5] - local_x * moment[2:3] - local_y * mean_x
            square_y = moment[5:6] - local_y * (moment[2:3] + mean_y)
            conic_x, conic_xy, conic_y = feature[2:3, :], feature[3:4, :], feature[4:5, :]
            grad = jnp.concatenate(
                [
                    conic_x * mean_x + conic_xy * mean_y,
                    conic_y * mean_y + conic_xy * mean_x,
                    -0.5 * square_x,
                    -mixed,
                    -0.5 * square_y,
                    total / feature[5:6, :],
                    colour_grad[0:3],
                ],
                axis=0,
            )
            grad = jnp.concatenate([grad[:, :LANES], grad[:, LANES:]], axis=0)
            even = (lax.rem(block, 2) == 0).astype(F32)
            grad = jnp.concatenate([grad * even, grad * (1.0 - even)], axis=0)

            @pl.when(on_near)
            def _():
                near_out[chip, 0:36, :] += grad

            @pl.when(jnp.logical_not(on_near))
            def _():
                far_out[chip, 0:36, :] += grad

            return behind + jnp.sum(through, axis=1, keepdims=True)

        lax.fori_loop(0, length, backward, jnp.zeros((PIX, 1), F32))


def collect_kernel(owned, visible_ref, camera_ref, parts_ref, out_ref):
    base = lax.axis_index("cell") * owned
    total = parts_ref[0]
    for i in range(1, parts_ref.shape[0]):
        total = total + parts_ref[i]
    out_ref[0, 0:MSG, :] = total
    for i in range(6):
        out_ref[0, 36 + i : 37 + i, :] = jnp.full((1, LANES), camera_ref[0, i], F32)
    for sub in range(2):
        chosen = (visible_ref[0, sub] - base).astype(F32)
        out_ref[0, 42 + sub : 43 + sub, :] = jnp.full((1, LANES), chosen, F32)
    out_ref[0, 44:VIEW_MSG, :] = jnp.zeros((VIEW_MSG - 44, LANES), F32)
    message = out_ref[0]
    for i in range(1, out_ref.shape[0]):
        out_ref[i] = message


def update_kernel(
    focal,
    parts_ref,
    gauss_ref,
    first_ref,
    second_ref,
    gauss_out,
    first_out,
    second_out,
    camera_out,
    rows_scr,
    factor_scr,
    sum_scr,
    grad_scr,
    frame_scr,
):
    owned, params = gauss_ref.shape[0], gauss_ref.shape[1]
    views = parts_ref.shape[0]
    own_view = lax.axis_index("view")
    place = lax.broadcasted_iota(jnp.int32, (owned, LANES), 0).astype(F32)
    whole = (owned, LANES)
    for half in range(HALVES):
        lanes = slice(half * LANES, (half + 1) * LANES)
        for k in range(params):
            rows_scr[k] = gauss_ref[:, k, lanes]
        factor, factor_pull = jax.vjp(
            shape_factor,
            [rows_scr[3 + i] for i in range(3)],
            [rows_scr[6 + i] for i in range(4)],
        )
        for i in range(9):
            factor_scr[i] = factor[i]
        sum_scr[...] = jnp.zeros_like(sum_scr)

        def one_view(view, carry):
            def message(k):
                return parts_ref[view, k : k + 1, :]

            masks = [place == message(42 + sub) for sub in range(2)]
            screen = [
                sum(
                    jnp.where(masks[sub], message(sub * 18 + half * 9 + f), 0.0)
                    for sub in range(2)
                )
                for f in range(FEATURES)
            ]
            frame = [
                jnp.broadcast_to(entry, whole)
                for entry in camera_frame([message(36 + i) for i in range(6)])
            ]
            seen, pull = jax.vjp(
                lambda centers, factor, frame: view_of(centers, factor, frame, *focal),
                [rows_scr[i] for i in range(3)],
                [factor_scr[i] for i in range(9)],
                frame,
            )
            basis = seen[5:]
            basis_grad = [jnp.zeros(whole, F32)] * 15
            for channel in range(3):
                first_row = 11 + 16 * channel
                summed = colour_sum(basis, lambda c, k: rows_scr[11 + 16 * c + k], channel)
                gate = jnp.where(summed > 0.0, 1.0, jnp.where(summed == 0.0, 0.5, 0.0))
                colour = screen[6 + channel] * gate
                sum_scr[first_row] += HARMONIC_0 * colour
                for k in range(15):
                    basis_grad[k] = basis_grad[k] + colour * rows_scr[first_row + 1 + k]
                    sum_scr[first_row + 1 + k] += colour * basis[k]
            centre_grad, factor_grad, frame_grad = pull(screen[:5] + basis_grad)
            for i in range(3):
                sum_scr[i] += centre_grad[i]
            sum_scr[10] += screen[5]
            for i in range(9):
                sum_scr[params + i] += factor_grad[i]

            @pl.when(view == own_view)
            def _():
                for i in range(15):
                    frame_scr[half, i] = frame_grad[i]
                for i in range(6):
                    frame_scr[half, 15 + i] = jnp.broadcast_to(message(36 + i), whole)

            return carry

        lax.fori_loop(0, views, one_view, 0)
        scale_grad, quaternion_grad = factor_pull([sum_scr[params + i] for i in range(9)])
        opacity = sigmoid(rows_scr[10])
        for i in range(3):
            sum_scr[3 + i] = scale_grad[i]
        for i in range(4):
            sum_scr[6 + i] = quaternion_grad[i]
        sum_scr[10] = sum_scr[10] * opacity * (1.0 - opacity)
        for k in range(params):
            grad_scr[:, k, lanes] = sum_scr[k]

    _, frame_pull = jax.vjp(camera_frame, [frame_scr[0, 15 + i, 0:1, :] for i in range(6)])
    camera_grad = frame_pull(
        [
            jnp.sum(frame_scr[0, i] + frame_scr[1, i], axis=0, keepdims=True)
            for i in range(15)
        ]
    )[0]
    lane = lax.broadcasted_iota(jnp.int32, (1, LANES), 1)
    packed = jnp.zeros((1, LANES), F32)
    for i in range(6):
        packed = packed + jnp.where(
            lane == i, jnp.sum(camera_grad[i], axis=1, keepdims=True), 0.0
        )
    packed = jnp.broadcast_to(packed, camera_out.shape[1:])
    for i in range(camera_out.shape[0]):
        camera_out[i] = packed

    for block in range(owned):
        gradient = grad_scr[block]
        moment = 0.9 * first_ref[block] + 0.1 * gradient
        second = 0.999 * second_ref[block] + 0.001 * gradient * gradient
        first_out[block] = moment
        second_out[block] = second
        gauss_out[block] = gauss_ref[block] - (0.05 / (1.0 - 0.9**10)) * moment / (
            jnp.sqrt(second * (1.0 / (1.0 - 0.999**10))) + 1e-08
        )


VMEM = pl.BlockSpec(memory_space=pltpu.VMEM)
SMEM = pl.BlockSpec(memory_space=pltpu.SMEM)
PARAMETERS = pltpu.CompilerParams(vmem_limit_bytes=40 * 1024 * 1024)


def shards(
    gaussians,
    first_moment,
    second_moment,
    cameras,
    visible_blocks,
    tile_ids,
    tile_order,
    tile_length,
    targets,
):
    owned, params = gaussians.shape[0], gaussians.shape[1]
    cells = lax.axis_size("cell")
    views = lax.axis_size("view")
    chips = cells // CORES
    tile_total = cells * tile_ids.shape[1]
    focal = (16.0 * TILE, 8.0 * TILE, tile_total * TILE / 32.0)
    same_core = [[chip * CORES + core for chip in range(chips)] for core in range(CORES)]
    swap = [(cell, cell ^ 1) for cell in range(cells)]

    with jax.named_scope("project"):
        message = pl.pallas_call(
            lambda *refs: project_kernel(focal, *refs),
            out_shape=jax.ShapeDtypeStruct((chips, MSG, LANES), F32),
            in_specs=[SMEM, SMEM, VMEM],
            out_specs=VMEM,
            compiler_params=PARAMETERS,
            name="project",
        )(visible_blocks, cameras, gaussians)
    with jax.named_scope("gather"):
        near = lax.all_to_all(message, "cell", 0, 0, axis_index_groups=same_core, tiled=True)
        far = lax.ppermute(near, "cell", swap)
    depth = tile_order.shape[2]
    with jax.named_scope("render"):
        near_grad, far_grad = pl.pallas_call(
            render_kernel,
            out_shape=[jax.ShapeDtypeStruct((chips, MSG, LANES), F32)] * 2,
            in_specs=[SMEM, SMEM, SMEM, VMEM, VMEM, VMEM],
            out_specs=[VMEM, VMEM],
            scratch_shapes=[
                pltpu.VMEM((depth, 16, BLOCK), F32),
                pltpu.VMEM((depth, PIX, BLOCK), F32),
                pltpu.VMEM((depth, PIX, BLOCK), F32),
            ],
            compiler_params=PARAMETERS,
            name="render",
        )(tile_order, tile_length, tile_ids, targets, near, far)
    with jax.named_scope("scatter"):
        pair = near_grad + lax.ppermute(far_grad, "cell", swap)
        parts = lax.all_to_all(pair, "cell", 0, 0, axis_index_groups=same_core, tiled=True)
    with jax.named_scope("collect"):
        own = pl.pallas_call(
            lambda *refs: collect_kernel(owned, *refs),
            out_shape=jax.ShapeDtypeStruct((views, VIEW_MSG, LANES), F32),
            in_specs=[SMEM, SMEM, VMEM],
            out_specs=VMEM,
            compiler_params=PARAMETERS,
            name="collect",
        )(visible_blocks, cameras, parts)
        every = lax.all_to_all(own, "view", 0, 0, tiled=True)
    with jax.named_scope("update"):
        state = jax.ShapeDtypeStruct(gaussians.shape, F32)
        new_gaussians, new_first, new_second, camera_part = pl.pallas_call(
            lambda *refs: update_kernel(focal, *refs),
            out_shape=[state, state, state, jax.ShapeDtypeStruct((cells, 1, LANES), F32)],
            in_specs=[VMEM] * 4,
            out_specs=[VMEM] * 4,
            scratch_shapes=[
                pltpu.VMEM((params, owned, LANES), F32),
                pltpu.VMEM((9, owned, LANES), F32),
                pltpu.VMEM((params + 9, owned, LANES), F32),
                pltpu.VMEM(gaussians.shape, F32),
                pltpu.VMEM((HALVES, 21, owned, LANES), F32),
            ],
            compiler_params=PARAMETERS,
            name="update",
        )(every, gaussians, first_moment, second_moment)
    with jax.named_scope("camera"):
        camera_parts = lax.all_to_all(camera_part, "cell", 0, 0, tiled=True)
        camera_total = jnp.sum(camera_parts, axis=0)[:, :6]
    return (new_gaussians, new_first, new_second, camera_total)


def solution(mesh):
    return jax.shard_map(
        shards,
        mesh=mesh,
        in_specs=(
            P("cell", None, None),
            P("cell", None, None),
            P("cell", None, None),
            P("view", None),
            P("view", "cell"),
            P("view", "cell"),
            P("view", "cell", None),
            P("view", "cell"),
            P("view", "cell", None, None),
        ),
        out_specs=(
            P("cell", None, None),
            P("cell", None, None),
            P("cell", None, None),
            P("view", None),
        ),
        check_vma=False,
    )
```

time: 553 us -> 126 us (0.23)
  waiting for transfers between devices: 281 us -> 16.9 us
  blocking collectives: 126 us -> 52.4 us
  between operations: 66.9 us -> 0.76 us
  starting transfers between devices: 0.12 us -> 29.3 us
  local copies, waits for them, and re-layouts: 29.4 us -> 5.59 us
  matrix products: 22.7 us -> 0 us
  other arithmetic: 22.8 us -> 0.68 us
  Pallas kernels: 0 us -> 19.8 us
    unnamed x4 -> x0, waiting for transfers between devices: 192 us -> none
    psum x1 -> x0, blocking collectives: 126 us -> none  [shards(): camera_total = lax.psum(camera_grad, 'cell')]
    all_gather x1 -> x0, waiting for transfers between devices: 89.3 us -> none  [shards(): visible = lax.all_gather(features, 'cell', axis=0, tiled=True)]
    all_to_all x0 -> x2, blocking collectives: none -> 52.4 us  [the longest x1 29.9 us: shards(): lax.all_to_all(message, 'cell', 0, 0, axis_index_groups=same_core, tiled=...]
    dot_general x24 -> x0, matrix products: 22.7 us -> none  [the longest x12 15.2 us: advance(): jnp.einsum('npg,gh->nph', log_keep, strict_upper, precision=lax.Precision...]
    pallas_call x0 -> x4, Pallas kernels: none -> 19.8 us  [the longest x1 13.4 us: shards(): pl.pallas_call(render_kernel, out_shape=[jax.ShapeDtypeStruct((chips, MSG...]
    gather x9 -> x0, local copies, waits for them, and re-layouts: 19.2 us -> none  [the longest x8 17.1 us: advance(): features_now = visible[order[:, depth_step]]]
    all_to_all x0 -> x2, starting transfers between devices: none -> 18 us  [the longest x1 11.4 us: shards(): camera_parts = lax.all_to_all(camera_part, 'cell', 0, 0, tiled=True)]
  transfers between devices with their start and end apart: 3 -> 4, of which waited for: 2 -> 4; matrix products, arithmetic and copies ran while one was open for 1% -> 3% of each run, Pallas kernels for 0% -> 0%
where the time goes in v1:
time: 126 us
  blocking collectives  52.4 us (42%)
  starting transfers between devices  29.3 us (23%)
  Pallas kernels  19.8 us (16%)
  waiting for transfers between devices  16.9 us (13%)
  local copies, waits for them, and re-layouts  5.59 us (4%)
    all_to_all x1, blocking collectives, shards(): lax.all_to_all(message, 'cell', 0, 0, axis_index_groups=same_core, tiled=...  29.9 us
    all_to_all x1, blocking collectives, shards(): lax.all_to_all(pair, 'cell', 0, 0, axis_index_groups=same_core, tiled=True)  22.5 us
    pallas_call x1, Pallas kernels, shards(): pl.pallas_call(render_kernel, out_shape=[jax.ShapeDtypeStruct((chips, MSG...  13.4 us
    all_to_all x1, starting transfers between devices, shards(): camera_parts = lax.all_to_all(camera_part, 'cell', 0, 0, tiled=True)  11.4 us
    all_to_all x1, waiting for transfers between devices, shards(): every = lax.all_to_all(own, 'view', 0, 0, tiled=True)  7.45 us
    ppermute x1, starting transfers between devices, shards(): far = lax.ppermute(near, 'cell', swap)  7.04 us
    all_to_all x1, starting transfers between devices, shards(): every = lax.all_to_all(own, 'view', 0, 0, tiled=True)  6.55 us
    all_to_all x1, waiting for transfers between devices, shards(): camera_parts = lax.all_to_all(camera_part, 'cell', 0, 0, tiled=True)  6.1 us
  transfers between devices with their start and end apart: 4, of which 4 were waited for; matrix products, arithmetic and copies ran while one was open for 3% of the time, Pallas kernels for 0%

profile of v1, /device:TPU:1, one launch (start us, length us, event | category | flops | bytes accessed | tf_op | source)
XLA Modules:
  0.0 125.5 jit_solution(818507005428650173)
XLA Ops:
  0.6 0.0 copy-start.1
  0.6 0.0 copy-start
  0.7 1.2 copy.13.refs_2_.refs_1_
  1.9 0.0 copy-done.1
  1.9 0.0 copy-done
  1.9 1.5 %project.1 = f32[32,40,128]{2,1,0:T(8,128)S(1)} custom-call(s32[1,2]{1,0:T(1,128)S(1)} %copy-done, f32[1,6]{1,0:T(1,128)S(1)} %copy-done.1, f32[8,59,256]{2,1,0:T(8,128)S(1)} %copy.13.refs_2_.refs_1_), custom_call_target="tpu_custom_call" | custom-call | tf_op jit(solution)/shard_map/project/project/pallas_call | solution.py:498
  3.4 0.0 copy-start.7
  3.4 29.9 %all_to_all.20.near_ref = f32[32,40,128]{2,1,0:T(8,128)S(1)} all-to-all(f32[32,40,128]{2,1,0:T(8,128)S(1)} %project.1), channel_id=1, replica_groups={{0,16,32,48,64,80,96,112,128,144,160,176,192,208,224,240,256,272,288,30..., dimensions={0} | all-to-all | bytes 1310720 | tf_op jit(solution)/shard_map/gather/all_to_all | solution.py:507
  33.3 7.0 %collective-permute-start = (f32[32,40,128]{2,1,0:T(8,128)S(1)}, f32[32,40,128]{2,1,0:T(8,128)S(1)}, u32[]{:S(2)}, u32[]{:S(2)}) collective-permute-start(f32[32,40,128]{2,1,0:T(8,128)S(1)} %all_to_all.20.near_ref), channel_id=1, source_target_pairs={{0,8},{8,0},{16,24},{24,16},{32,40},{40,32},{48,56},{56,48},{64,72... | collective-permute-start | bytes 1966088 | tf_op jit(solution)/shard_map/gather/ppermute | solution.py:508
  40.4 0.0 copy-done.7
  40.4 1.7 %collective-permute-done.far_ref = f32[32,40,128]{2,1,0:T(8,128)S(1)} collective-permute-done((f32[32,40,128]{2,1,0:T(8,128)S(1)}, f32[32,40,128]{2,1,0:T(8,128)S(1)}, u32[]{:S(2)}, u32[]{:S(2)}) %collective-permute-start) | collective-permute-done | bytes 655392 | tf_op jit(solution)/shard_map/gather/ppermute | solution.py:508
  42.1 0.0 copy-done.2
  42.1 0.0 copy-done.3
  42.1 13.4 %render.1 = (f32[32,40,128]{2,1,0:T(8,128)S(1)}, f32[32,40,128]{2,1,0:T(8,128)S(1)}) custom-call(s32[1,2,4]{2,1,0:T(2,128)S(1)} %copy-done.2, s32[1,2]{1,0:T(1,128)S(1)} %copy-done.3, s32[1,2]{1,0:T(1,128)S(1)} %copy-done.4, bf16[1,2,3,256]{3,2,1,0:T(4,128)(2,1)S(1)} %copy.14.target_ref, f32[32,40,128]{2,1,0:T(8,128)S(1)} %all_to_all.20.near_ref, ...), custom_call_target="tpu_custom_call" | custom-call | tf_op jit(solution)/shard_map/render/render/pallas_call | solution.py:511
  55.5 4.3 %collective-permute-start.1 = (f32[32,40,128]{2,1,0:T(8,128)S(1)}, f32[32,40,128]{2,1,0:T(8,128)S(1)}, u32[]{:S(2)}, u32[]{:S(2)}) collective-permute-start(f32[32,40,128]{2,1,0:T(8,128)S(1)} %get-tuple-element.11), channel_id=1, source_target_pairs={{0,8},{8,0},{16,24},{24,16},{32,40},{40,32},{48,56},{56,48},{64,72... | collective-permute-start | bytes 1966088 | tf_op jit(solution)/shard_map/scatter/ppermute | solution.py:525
  59.7 1.7 %collective-permute-done.1 = f32[32,40,128]{2,1,0:T(8,128)S(1)} collective-permute-done((f32[32,40,128]{2,1,0:T(8,128)S(1)}, f32[32,40,128]{2,1,0:T(8,128)S(1)}, u32[]{:S(2)}, u32[]{:S(2)}) %collective-permute-start.1) | collective-permute-done | bytes 655392 | tf_op jit(solution)/shard_map/scatter/ppermute | solution.py:525
  61.5 0.1 add.3
  61.5 22.5 %all_to_all.21.refs_2_ = f32[32,40,128]{2,1,0:T(8,128)S(1)} all-to-all(f32[32,40,128]{2,1,0:T(8,128)S(1)} %add.3), channel_id=1, replica_groups={{0,16,32,48,64,80,96,112,128,144,160,176,192,208,224,240,256,272,288,30..., dimensions={0} | all-to-all | bytes 1310720 | tf_op jit(solution)/shard_map/scatter/all_to_all | solution.py:526
  84.1 1.3 %collect.1 = f32[8,48,128]{2,1,0:T(8,128)} custom-call(s32[1,2]{1,0:T(1,128)S(1)} %copy-done, f32[1,6]{1,0:T(1,128)S(1)} %copy-done.1, f32[32,40,128]{2,1,0:T(8,128)S(1)} %all_to_all.21.refs_2_), custom_call_target="tpu_custom_call" | custom-call | tf_op jit(solution)/shard_map/collect/collect/pallas_call | solution.py:528
  85.3 6.5 %all-to-all-start.2 = ((f32[8,48,128]{2,1,0:T(8,128)}), f32[8,48,128]{2,1,0:T(8,128)S(1)}, u32[]{:S(2)}, u32[]{:S(2)}) async-start(f32[8,48,128]{2,1,0:T(8,128)} %collect.1), calls=%async_computation.2 | async-start | bytes 393216 | tf_op jit(solution)/shard_map/collect/all_to_all | solution.py:536
  91.9 0.0 copy-start.6
  91.9 0.2 copy.16.refs_2_
  92.1 0.8 copy-done.6
  92.9 0.2 copy.17.refs_3_
  93.1 7.5 %all-to-all-done.2.refs_0_ = f32[8,48,128]{2,1,0:T(8,128)S(1)} async-done(((f32[8,48,128]{2,1,0:T(8,128)}), f32[8,48,128]{2,1,0:T(8,128)S(1)}, u32[]{:S(2)}, u32[]{:S(2)}) %all-to-all-start.2) | async-done | bytes 196640 | tf_op jit(solution)/shard_map/collect/all_to_all | solution.py:536
  100.5 3.6 %update.1 = (f32[8,59,256]{2,1,0:T(8,128)S(1)}, f32[8,59,256]{2,1,0:T(8,128)S(1)}, f32[8,59,256]{2,1,0:T(8,128)S(1)}, f32[64,1,128]{2,1,0:T(1,128)}) custom-call(f32[8,48,128]{2,1,0:T(8,128)S(1)} %all-to-all-done.2.refs_0_, f32[8,59,256]{2,1,0:T(8,128)S(1)} %copy.13.refs_2_.refs_1_, f32[8,59,256]{2,1,0:T(8,128)S(1)} %copy.16.refs_2_, ...), custom_call_target="tpu_custom_call" | custom-call | tf_op jit(solution)/shard_map/update/update/pallas_call | solution.py:539
  104.2 11.4 %all-to-all-start.3 = ((f32[64,1,128]{2,1,0:T(1,128)}), f32[64,1,128]{2,1,0:T(1,128)S(1)}, u32[]{:S(2)}, u32[]{:S(2)}) async-start(f32[64,1,128]{2,1,0:T(1,128)} %get-tuple-element.15), calls=%async_computation.3 | async-start | bytes 65536 | tf_op jit(solution)/shard_map/camera/all_to_all | solution.py:555
  115.6 1.1 copy.18
  116.7 1.1 copy.19
  117.7 1.1 copy.20
  118.8 6.1 %all-to-all-done.3 = f32[64,1,128]{2,1,0:T(1,128)S(1)} async-done(((f32[64,1,128]{2,1,0:T(1,128)}), f32[64,1,128]{2,1,0:T(1,128)S(1)}, u32[]{:S(2)}, u32[]{:S(2)}) %all-to-all-start.3) | async-done | bytes 32800 | tf_op jit(solution)/shard_map/camera/all_to_all | solution.py:555
  124.9 0.6 reduce_sum.11
  (7 shorter events, 0.0 us)
Async XLA Ops:
  0.6 1.2 copy-start.1
  0.6 1.2 copy-start
  3.4 37.0 %copy-start.7 = (bf16[1,2,3,256]{3,1,2,0:T(2,128)(2,1)S(1)}, bf16[1,2,3,256]{3,1,2,0:T(2,128)(2,1)}, u32[]{:S(2)}) copy-start(bf16[1,2,3,256]{3,1,2,0:T(2,128)(2,1)} %param.17) | copy-start | bytes 9220
  33.3 8.8 %copy-start.2 = (s32[1,2,4]{2,1,0:T(2,128)S(1)}, s32[1,2,4]{2,1,0:T(2,128)}, u32[]{:S(2)}) copy-start(s32[1,2,4]{2,1,0:T(2,128)} %order_ref.1) | copy-start | bytes 100
  33.3 8.8 %copy-start.3 = (s32[1,2]{1,0:T(1,128)S(1)}, s32[1,2]{1,0:T(1,128)}, u32[]{:S(2)}) copy-start(s32[1,2]{1,0:T(1,128)} %length_ref.1) | copy-start | bytes 28
  33.3 8.8 %copy-start.4 = (s32[1,2]{1,0:T(1,128)S(1)}, s32[1,2]{1,0:T(1,128)}, u32[]{:S(2)}) copy-start(s32[1,2]{1,0:T(1,128)} %tile_ref.1) | copy-start | bytes 28
  33.3 8.8 %collective-permute-start = (f32[32,40,128]{2,1,0:T(8,128)S(1)}, f32[32,40,128]{2,1,0:T(8,128)S(1)}, u32[]{:S(2)}, u32[]{:S(2)}) collective-permute-start(f32[32,40,128]{2,1,0:T(8,128)S(1)} %all_to_all.20.near_ref), channel_id=1, source_target_pairs={{0,8},{8,0},{16,24},{24,16},{32,40},{40,32},{48,56},{56,48},{64,72... | collective-permute-start | bytes 1966088 | tf_op jit(solution)/shard_map/gather/ppermute | solution.py:508
  55.5 6.0 %collective-permute-start.1 = (f32[32,40,128]{2,1,0:T(8,128)S(1)}, f32[32,40,128]{2,1,0:T(8,128)S(1)}, u32[]{:S(2)}, u32[]{:S(2)}) collective-permute-start(f32[32,40,128]{2,1,0:T(8,128)S(1)} %get-tuple-element.11), channel_id=1, source_target_pairs={{0,8},{8,0},{16,24},{24,16},{32,40},{40,32},{48,56},{56,48},{64,72... | collective-permute-start | bytes 1966088 | tf_op jit(solution)/shard_map/scatter/ppermute | solution.py:525
  84.1 7.8 %copy-start.5 = (f32[8,59,256]{2,0,1:T(8,128)S(1)}, f32[8,59,256]{2,0,1:T(8,128)}, u32[]{:S(2)}) copy-start(f32[8,59,256]{2,0,1:T(8,128)} %param.10) | copy-start | bytes 1449988
  85.3 15.2 %all-to-all-start.2 = ((f32[8,48,128]{2,1,0:T(8,128)}), f32[8,48,128]{2,1,0:T(8,128)S(1)}, u32[]{:S(2)}, u32[]{:S(2)}) async-start(f32[8,48,128]{2,1,0:T(8,128)} %collect.1), calls=%async_computation.2 | async-start | bytes 393216 | tf_op jit(solution)/shard_map/collect/all_to_all | solution.py:536
  91.9 1.0 copy-start.6
  104.2 20.7 %all-to-all-start.3 = ((f32[64,1,128]{2,1,0:T(1,128)}), f32[64,1,128]{2,1,0:T(1,128)S(1)}, u32[]{:S(2)}, u32[]{:S(2)}) async-start(f32[64,1,128]{2,1,0:T(1,128)} %get-tuple-element.15), calls=%async_computation.3 | async-start | bytes 65536 | tf_op jit(solution)/shard_map/camera/all_to_all | solution.py:555

commit v2 on v1

v2 whole, which is shorter than its diff:
```python
import jax
import jax.numpy as jnp
from jax import lax
from jax.experimental import pallas as pl
from jax.experimental.pallas import tpu as pltpu
from jax.sharding import PartitionSpec as P

TILE = 16
PIX = 256
BLOCK = 256
LANES = 128
HALVES = 2
FEATURES = 9
CORES = 2
ROWS = 4
VIEW_MSG = 11
LOG2E = 1.4426950408889634
F32 = jnp.float32
BF16 = jnp.bfloat16


def rotation_matrix(real_part, axis_x, axis_y, axis_z):
    return [
        [
            1.0 - 2.0 * (axis_y * axis_y + axis_z * axis_z),
            2.0 * (axis_x * axis_y - real_part * axis_z),
            2.0 * (axis_x * axis_z + real_part * axis_y),
        ],
        [
            2.0 * (axis_x * axis_y + real_part * axis_z),
            1.0 - 2.0 * (axis_x * axis_x + axis_z * axis_z),
            2.0 * (axis_y * axis_z - real_part * axis_x),
        ],
        [
            2.0 * (axis_x * axis_z - real_part * axis_y),
            2.0 * (axis_y * axis_z + real_part * axis_x),
            1.0 - 2.0 * (axis_x * axis_x + axis_y * axis_y),
        ],
    ]


def harmonic_basis(unit_x, unit_y, unit_z):
    square_x = unit_x * unit_x
    square_y = unit_y * unit_y
    square_z = unit_z * unit_z
    return [
        -0.4886025119029199 * unit_y,
        0.4886025119029199 * unit_z,
        -0.4886025119029199 * unit_x,
        1.0925484305920792 * unit_x * unit_y,
        -1.0925484305920792 * unit_y * unit_z,
        0.31539156525252005 * (2.0 * square_z - square_x - square_y),
        -1.0925484305920792 * unit_x * unit_z,
        0.5462742152960396 * (square_x - square_y),
        -0.5900435899266435 * unit_y * (3.0 * square_x - square_y),
        2.890611442640554 * unit_x * unit_y * unit_z,
        -0.4570457994644658 * unit_y * (4.0 * square_z - square_x - square_y),
        0.3731763325901154 * unit_z * (2.0 * square_z - 3.0 * square_x - 3.0 * square_y),
        -0.4570457994644658 * unit_x * (4.0 * square_z - square_x - square_y),
        1.445305721320277 * unit_z * (square_x - square_y),
        -0.5900435899266435 * unit_x * (square_x - 3.0 * square_y),
    ]


HARMONIC_0 = 0.28209479177387814


def camera_frame(camera):
    inverse_norm = 1.0 / jnp.sqrt(
        1.0 + camera[0] * camera[0] + camera[1] * camera[1] + camera[2] * camera[2]
    )
    rotation = rotation_matrix(
        inverse_norm, camera[0] * inverse_norm, camera[1] * inverse_norm, camera[2] * inverse_norm
    )
    shift = [camera[3], camera[4], camera[5]]
    centre = [
        -(rotation[0][i] * shift[0] + rotation[1][i] * shift[1] + rotation[2][i] * shift[2])
        for i in range(3)
    ]
    return [rotation[i][j] for i in range(3) for j in range(3)] + shift + centre


def shape_factor(scales, quaternion):
    inverse_norm = 1.0 / jnp.sqrt(sum(entry * entry for entry in quaternion))
    own = rotation_matrix(*[entry * inverse_norm for entry in quaternion])
    widths = [jnp.exp(entry) for entry in scales]
    return [own[i][j] * widths[j] for i in range(3) for j in range(3)]


def view_of(centers, factor, frame, focal_length, centre_x, centre_y):
    rotation = [frame[3 * i : 3 * i + 3] for i in range(3)]
    shift = frame[9:12]
    origin = frame[12:15]
    in_view = [
        rotation[i][0] * centers[0]
        + rotation[i][1] * centers[1]
        + rotation[i][2] * centers[2]
        + shift[i]
        for i in range(3)
    ]
    inverse_depth = 1.0 / in_view[2]
    near = focal_length * inverse_depth
    ratio_x = in_view[0] * inverse_depth
    ratio_y = in_view[1] * inverse_depth
    screen = [
        [near * (rotation[0][j] - ratio_x * rotation[2][j]) for j in range(3)],
        [near * (rotation[1][j] - ratio_y * rotation[2][j]) for j in range(3)],
    ]
    spread = [
        [sum(screen[a][j] * factor[3 * j + k] for j in range(3)) for k in range(3)]
        for a in range(2)
    ]
    variance_x = sum(spread[0][k] * spread[0][k] for k in range(3)) + 0.3
    covariance = sum(spread[0][k] * spread[1][k] for k in range(3))
    variance_y = sum(spread[1][k] * spread[1][k] for k in range(3)) + 0.3
    inverse_determinant = 1.0 / (variance_x * variance_y - covariance * covariance)
    toward = [centers[i] - origin[i] for i in range(3)]
    inverse_length = 1.0 / jnp.sqrt(
        toward[0] * toward[0] + toward[1] * toward[1] + toward[2] * toward[2]
    )
    basis = harmonic_basis(*[entry * inverse_length for entry in toward])
    return [
        focal_length * ratio_x + centre_x,
        focal_length * ratio_y + centre_y,
        variance_y * inverse_determinant,
        -covariance * inverse_determinant,
        variance_x * inverse_determinant,
    ] + basis


def colour_sum(basis, harmonic_of, channel):
    summed = 0.5 + HARMONIC_0 * harmonic_of(channel, 0)
    for k in range(15):
        summed = summed + basis[k] * harmonic_of(channel, k + 1)
    return summed


def sigmoid(logit):
    return 1.0 / (1.0 + jnp.exp(-logit))


def features_of(row, camera, focal):
    shape = row(0).shape
    frame = [jnp.broadcast_to(entry, shape) for entry in camera_frame(camera)]
    factor = shape_factor([row(3 + i) for i in range(3)], [row(6 + i) for i in range(4)])
    seen = view_of([row(i) for i in range(3)], factor, frame, *focal)
    colours = [
        jnp.maximum(colour_sum(seen[5:], lambda c, k: row(11 + 16 * c + k), channel), 0.0)
        for channel in range(3)
    ]
    return seen[:5] + [sigmoid(row(10))] + colours


def halves_of(gauss_ref):
    return lambda k: jnp.concatenate(
        [gauss_ref[k, :, half * LANES : (half + 1) * LANES] for half in range(HALVES)], axis=0
    )


def pick(visible_ref, owned):
    base = lax.axis_index("cell") * owned
    place = lax.broadcasted_iota(jnp.int32, (owned, LANES), 0)
    masks = [place == visible_ref[0, sub] - base for sub in range(2)]
    return lambda value: [
        jnp.sum(
            jnp.where(mask, value[half * owned : (half + 1) * owned], 0.0), axis=0, keepdims=True
        )
        for mask in masks
        for half in range(HALVES)
    ]


def camera_rows(camera_ref):
    return [jnp.full((1, LANES), camera_ref[0, i], F32) for i in range(6)]


def project_kernel(focal, visible_ref, camera_ref, gauss_ref, out_ref):
    features = features_of(halves_of(gauss_ref), camera_rows(camera_ref), focal)
    picked = pick(visible_ref, gauss_ref.shape[1])
    for f in range(FEATURES):
        out_ref[0, f] = jnp.concatenate(picked(features[f]), axis=0)
    message = out_ref[0]
    for i in range(1, out_ref.shape[0]):
        out_ref[i] = message


def slope_kernel(focal, visible_ref, camera_ref, gauss_ref, out_ref):
    camera = camera_rows(camera_ref)
    whole = halves_of(gauss_ref)
    picked = pick(visible_ref, gauss_ref.shape[1])
    held = [jnp.concatenate(picked(whole(k)), axis=0) for k in range(gauss_ref.shape[0])]
    for i in range(6):
        tangents = [jnp.full((1, LANES), 1.0 if j == i else 0.0, F32) for j in range(6)]
        _, slopes = jax.jvp(
            lambda *entries: features_of(held.__getitem__, entries, focal), camera, tangents
        )
        for f in range(FEATURES):
            out_ref[i, f] = slopes[f]


def split(value):
    high = value.astype(BF16)
    return high, (value - high.astype(F32)).astype(BF16)


def dot(left, right):
    return jnp.dot(left, right, preferred_element_type=F32)


def both_dots(pair, right):
    return dot(pair[0], right) + dot(pair[1], right)


def transpose_dot(left, right):
    return lax.dot_general(
        left, right, (((1,), (1,)), ((), ())), preferred_element_type=F32
    )


def stacked(value, rows):
    high, low = split(value)
    return jnp.concatenate(
        [high.astype(F32), low.astype(F32), jnp.zeros((rows - 6, value.shape[1]), F32)], axis=0
    ).astype(BF16)


def render_kernel(
    order_ref,
    length_ref,
    tile_ref,
    target_ref,
    near_ref,
    far_ref,
    near_out,
    far_out,
    feature_scr,
    rgb_scr,
    weight_scr,
    high_scr,
    low_scr,
    ratio_scr,
):
    slots = order_ref.shape[1]
    core = lax.rem(lax.axis_index("cell"), CORES)
    near_out[...] = jnp.zeros_like(near_out)
    far_out[...] = jnp.zeros_like(far_out)
    first = lax.broadcasted_iota(jnp.int32, (BLOCK, BLOCK), 0)
    second = lax.broadcasted_iota(jnp.int32, (BLOCK, BLOCK), 1)
    earlier = (first < second).astype(BF16)
    later = (first > second).astype(BF16)
    ones = jnp.ones((BLOCK, LANES), BF16)
    step_x = lax.broadcasted_iota(jnp.int32, (TILE, BLOCK), 0).astype(F32) - 7.5
    part = lax.broadcasted_iota(jnp.int32, (ROWS, LANES), 0)
    targets = target_ref[...].astype(F32)

    def spread_over(value):
        return jnp.concatenate([value, value], axis=1)

    for slot in range(slots):
        tile = tile_ref[0, slot]
        tile_x = (lax.rem(tile, 16) * TILE + 8).astype(F32)
        tile_y = (lax.div(tile, 16) * TILE + 8).astype(F32)
        length = length_ref[0, slot]

        def forward(k, carry):
            log_remain, colour = carry
            block = order_ref[0, slot, k]
            chip = lax.div(block, 4)
            on_near = lax.rem(lax.div(block, 2), CORES) == core
            even = lax.rem(block, 2) == 0
            for f in range(FEATURES):
                entry = jnp.where(on_near, near_ref[chip, f], far_ref[chip, f])
                entry = jnp.where(even, entry[0:2], entry[2:4])
                feature_scr[k, f : f + 1, 0:LANES] = entry[0:1]
                feature_scr[k, f : f + 1, LANES:] = entry[1:2]
            feature = feature_scr.at[k]
            rgb_scr[k] = stacked(feature[6:9, :], 16)
            delta_x = step_x - (feature[0:1, :] - tile_x)
            local_y = feature[1:2, :] - tile_y
            curve_x = (-0.5 * LOG2E) * feature[2:3, :] * delta_x * delta_x
            cross_x = (-LOG2E) * feature[3:4, :] * delta_x
            curve = (-0.5 * LOG2E) * feature[4:5, :]
            rows = []
            for i in range(TILE):
                delta_y = (i - 7.5) - local_y
                rows.append(curve_x + (cross_x * delta_y + curve * delta_y * delta_y))
            exponent = jnp.concatenate(rows, axis=0)
            alpha = feature[5:6, :] * jnp.exp2(exponent)
            keep = alpha * (
                -LOG2E
                - alpha * (LOG2E / 2.0 + alpha * (LOG2E / 3.0 + alpha * (LOG2E / 4.0)))
            )
            pair = split(keep)
            before = both_dots(pair, earlier) + spread_over(log_remain)
            weight = alpha * jnp.exp2(before)
            ratio_scr[k] = alpha * jnp.exp2(-keep)
            weight_scr[k] = weight
            high, low = split(weight)
            high_scr[k] = high
            low_scr[k] = low
            colour = colour + transpose_dot(high, rgb_scr[k]) + transpose_dot(low, rgb_scr[k])
            return (log_remain + both_dots(pair, ones), colour)

        _, colour = lax.fori_loop(
            0, length, forward, (jnp.zeros((PIX, LANES), F32), jnp.zeros((PIX, 16), F32))
        )
        turned = colour.T
        misfit = turned[0:3] + turned[3:6] - targets[0, slot]
        misfit_rows = stacked(misfit, 16)
        misfit_high, misfit_low = split(misfit)
        misfit_high = misfit_high.astype(F32)
        misfit_low = misfit_low.astype(F32)
        blank = jnp.zeros((10, PIX), F32)
        misfit_pair = tuple(
            jnp.concatenate([term, term, blank], axis=0).T.astype(BF16)
            for term in (misfit_high, misfit_low)
        )

        def backward(step, behind):
            k = length - 1 - step
            block = order_ref[0, slot, k]
            chip = lax.div(block, 4)
            on_near = lax.rem(lax.div(block, 2), CORES) == core
            side = lax.rem(block, 2) * 2
            feature = feature_scr.at[k]
            through = weight_scr[k] * both_dots(misfit_pair, rgb_scr[k])
            pair = split(through)
            after = both_dots(pair, later) + spread_over(behind)
            slope = through - after * ratio_scr[k]
            flat = jnp.zeros((TILE, BLOCK), F32)
            tilt = jnp.zeros((TILE, BLOCK), F32)
            bend = jnp.zeros((TILE, BLOCK), F32)
            for i in range(TILE // 2):
                top = slope[i * TILE : (i + 1) * TILE]
                bottom = slope[(TILE - 1 - i) * TILE : (TILE - i) * TILE]
                away = 7.5 - i
                flat = flat + (top + bottom)
                tilt = tilt + away * (bottom - top)
                bend = bend + (away * away) * (top + bottom)
            colour_grad = dot(misfit_rows, high_scr[k]) + dot(misfit_rows, low_scr[k])
            delta_x = step_x - (feature[0:1, :] - tile_x)
            local_y = feature[1:2, :] - tile_y
            mean = tilt - local_y * flat
            bend = bend - local_y * (tilt + mean)

            def across(value):
                return jnp.sum(value, axis=0, keepdims=True)

            total, mean_x, mean_y = across(flat), across(delta_x * flat), across(mean)
            square_x = across(delta_x * delta_x * flat)
            mixed = across(delta_x * mean)
            square_y = across(bend)
            conic_x, conic_xy, conic_y = feature[2:3, :], feature[3:4, :], feature[4:5, :]
            grads = [
                conic_x * mean_x + conic_xy * mean_y,
                conic_y * mean_y + conic_xy * mean_x,
                -0.5 * square_x,
                -mixed,
                -0.5 * square_y,
                total / feature[5:6, :],
            ] + [colour_grad[i : i + 1] + colour_grad[i + 3 : i + 4] for i in range(3)]
            placed = [
                jnp.where(
                    part == side,
                    grad[:, :LANES],
                    jnp.where(part == side + 1, grad[:, LANES:], 0.0),
                )
                for grad in grads
            ]

            @pl.when(on_near)
            def _():
                for f in range(FEATURES):
                    near_out[chip, f] += placed[f]

            @pl.when(jnp.logical_not(on_near))
            def _():
                for f in range(FEATURES):
                    far_out[chip, f] += placed[f]

            return behind + both_dots(pair, ones)

        lax.fori_loop(0, length, backward, jnp.zeros((PIX, LANES), F32))


def collect_kernel(owned, visible_ref, camera_ref, parts_ref, slope_ref, out_ref, camera_out):
    base = lax.axis_index("cell") * owned
    total = parts_ref[0]
    for i in range(1, parts_ref.shape[0]):
        total = total + parts_ref[i]
    out_ref[0, 0:FEATURES] = total
    base_rows = [jnp.full((1, LANES), camera_ref[0, i], F32) for i in range(6)] + [
        jnp.full((1, LANES), (visible_ref[0, sub] - base).astype(F32), F32) for sub in range(2)
    ]
    for i in range(2):
        out_ref[0, FEATURES + i] = jnp.concatenate(base_rows[4 * i : 4 * i + 4], axis=0)
    message = out_ref[0]
    for i in range(1, out_ref.shape[0]):
        out_ref[i] = message
    lane = lax.broadcasted_iota(jnp.int32, (1, LANES), 1)
    packed = jnp.zeros((1, LANES), F32)
    for i in range(6):
        across = jnp.sum(
            jnp.sum(total * slope_ref[i], axis=0), axis=0, keepdims=True
        )
        packed = packed + jnp.where(lane == i, jnp.sum(across, axis=1, keepdims=True), 0.0)
    for i in range(camera_out.shape[0]):
        camera_out[i] = packed


def update_kernel(
    focal,
    parts_ref,
    gauss_ref,
    first_ref,
    second_ref,
    gauss_out,
    first_out,
    second_out,
    factor_scr,
    sum_scr,
):
    params, owned = gauss_ref.shape[0], gauss_ref.shape[1]
    views = parts_ref.shape[0]
    place = lax.broadcasted_iota(jnp.int32, (owned, LANES), 0).astype(F32)
    whole = (owned, LANES)
    for half in range(HALVES):
        lanes = slice(half * LANES, (half + 1) * LANES)

        def row(k, lanes=lanes):
            return gauss_ref[k, :, lanes]

        factor, factor_pull = jax.vjp(
            shape_factor,
            [row(3 + i) for i in range(3)],
            [row(6 + i) for i in range(4)],
        )
        for i in range(9):
            factor_scr[i] = factor[i]
        sum_scr[...] = jnp.zeros_like(sum_scr)

        def one_view(view, carry):
            def message(f, r):
                return parts_ref[view, f, r : r + 1, :]

            masks = [place == message(FEATURES + 1, 2 + sub) for sub in range(2)]
            screen = [
                sum(
                    jnp.where(masks[sub], message(f, sub * 2 + half), 0.0)
                    for sub in range(2)
                )
                for f in range(FEATURES)
            ]
            frame = [
                jnp.broadcast_to(entry, whole)
                for entry in camera_frame([message(FEATURES + i // 4, i % 4) for i in range(6)])
            ]
            seen, pull = jax.vjp(
                lambda centers, factor: view_of(centers, factor, frame, *focal),
                [row(i) for i in range(3)],
                [factor_scr[i] for i in range(9)],
            )
            basis = seen[5:]
            basis_grad = [jnp.zeros(whole, F32)] * 15
            for channel in range(3):
                first_row = 11 + 16 * channel
                summed = colour_sum(basis, lambda c, k: row(11 + 16 * c + k), channel)
                gate = jnp.where(summed > 0.0, 1.0, jnp.where(summed == 0.0, 0.5, 0.0))
                colour = screen[6 + channel] * gate
                sum_scr[first_row] += HARMONIC_0 * colour
                for k in range(15):
                    basis_grad[k] = basis_grad[k] + colour * row(first_row + 1 + k)
                    sum_scr[first_row + 1 + k] += colour * basis[k]
            centre_grad, factor_grad = pull(screen[:5] + basis_grad)
            for i in range(3):
                sum_scr[i] += centre_grad[i]
            sum_scr[10] += screen[5]
            for i in range(9):
                sum_scr[params + i] += factor_grad[i]
            return carry

        lax.fori_loop(0, views, one_view, 0)
        scale_grad, quaternion_grad = factor_pull([sum_scr[params + i] for i in range(9)])
        opacity = sigmoid(row(10))
        for i in range(3):
            sum_scr[3 + i] = scale_grad[i]
        for i in range(4):
            sum_scr[6 + i] = quaternion_grad[i]
        sum_scr[10] = sum_scr[10] * opacity * (1.0 - opacity)
        for k in range(params):
            gradient = sum_scr[k]
            moment = 0.9 * first_ref[k, :, lanes] + 0.1 * gradient
            second = 0.999 * second_ref[k, :, lanes] + 0.001 * gradient * gradient
            first_out[k, :, lanes] = moment
            second_out[k, :, lanes] = second
            gauss_out[k, :, lanes] = row(k) - (0.05 / (1.0 - 0.9**10)) * moment / (
                jnp.sqrt(second * (1.0 / (1.0 - 0.999**10))) + 1e-08
            )


VMEM = pl.BlockSpec(memory_space=pltpu.VMEM)
SMEM = pl.BlockSpec(memory_space=pltpu.SMEM)
PARAMETERS = pltpu.CompilerParams(vmem_limit_bytes=40 * 1024 * 1024)


def shards(
    gaussians,
    first_moment,
    second_moment,
    cameras,
    visible_blocks,
    tile_ids,
    tile_order,
    tile_length,
    targets,
):
    owned, params = gaussians.shape[0], gaussians.shape[1]
    gaussians, first_moment, second_moment = (
        array.transpose(1, 0, 2) for array in (gaussians, first_moment, second_moment)
    )
    cells = lax.axis_size("cell")
    views = lax.axis_size("view")
    chips = cells // CORES
    tile_total = cells * tile_ids.shape[1]
    focal = (16.0 * TILE, 8.0 * TILE, tile_total * TILE / 32.0)
    same_core = [[chip * CORES + core for chip in range(chips)] for core in range(CORES)]
    swap = [(cell, cell ^ 1) for cell in range(cells)]

    with jax.named_scope("project"):
        message = pl.pallas_call(
            lambda *refs: project_kernel(focal, *refs),
            out_shape=jax.ShapeDtypeStruct((chips, FEATURES, ROWS, LANES), F32),
            in_specs=[SMEM, SMEM, VMEM],
            out_specs=VMEM,
            compiler_params=PARAMETERS,
            name="project",
        )(visible_blocks, cameras, gaussians)
        slopes = pl.pallas_call(
            lambda *refs: slope_kernel(focal, *refs),
            out_shape=jax.ShapeDtypeStruct((6, FEATURES, ROWS, LANES), F32),
            in_specs=[SMEM, SMEM, VMEM],
            out_specs=VMEM,
            compiler_params=PARAMETERS,
            cost_estimate=pl.CostEstimate(
                flops=4_000_000, bytes_accessed=200_000, transcendentals=10_000
            ),
            name="slope",
        )(visible_blocks, cameras, gaussians)
    with jax.named_scope("gather"):
        near = lax.all_to_all(message, "cell", 0, 0, axis_index_groups=same_core, tiled=True)
        far = lax.ppermute(near, "cell", swap)
    depth = tile_order.shape[2]
    with jax.named_scope("render"):
        near_grad, far_grad = pl.pallas_call(
            render_kernel,
            out_shape=[jax.ShapeDtypeStruct((chips, FEATURES, ROWS, LANES), F32)] * 2,
            in_specs=[SMEM, SMEM, SMEM, VMEM, VMEM, VMEM],
            out_specs=[VMEM, VMEM],
            scratch_shapes=[
                pltpu.VMEM((depth, 16, BLOCK), F32),
                pltpu.VMEM((depth, 16, BLOCK), BF16),
                pltpu.VMEM((depth, PIX, BLOCK), F32),
                pltpu.VMEM((depth, PIX, BLOCK), BF16),
                pltpu.VMEM((depth, PIX, BLOCK), BF16),
                pltpu.VMEM((depth, PIX, BLOCK), F32),
            ],
            compiler_params=PARAMETERS,
            name="render",
        )(tile_order, tile_length, tile_ids, targets, near, far)
    with jax.named_scope("scatter"):
        pair = near_grad + lax.ppermute(far_grad, "cell", swap)
        parts = lax.all_to_all(pair, "cell", 0, 0, axis_index_groups=same_core, tiled=True)
    with jax.named_scope("collect"):
        own, camera_part = pl.pallas_call(
            lambda *refs: collect_kernel(owned, *refs),
            out_shape=[
                jax.ShapeDtypeStruct((views, VIEW_MSG, ROWS, LANES), F32),
                jax.ShapeDtypeStruct((1, 1, LANES), F32),
            ],
            in_specs=[SMEM, SMEM, VMEM, VMEM],
            out_specs=[VMEM, VMEM],
            compiler_params=PARAMETERS,
            name="collect",
        )(visible_blocks, cameras, parts, slopes)
        every = lax.all_to_all(own, "view", 0, 0, tiled=True)
    with jax.named_scope("camera"):
        camera_pair = camera_part + lax.ppermute(camera_part, "cell", swap)
        every, camera_pair = lax.optimization_barrier((every, camera_pair))
        camera_parts = lax.all_to_all(
            jnp.broadcast_to(camera_pair, (chips, 1, LANES)),
            "cell",
            0,
            0,
            axis_index_groups=same_core,
            tiled=True,
        )
    with jax.named_scope("update"):
        state = jax.ShapeDtypeStruct(gaussians.shape, F32)
        new_gaussians, new_first, new_second = pl.pallas_call(
            lambda *refs: update_kernel(focal, *refs),
            out_shape=[state, state, state],
            in_specs=[VMEM] * 4,
            out_specs=[VMEM] * 3,
            scratch_shapes=[
                pltpu.VMEM((9, owned, LANES), F32),
                pltpu.VMEM((params + 9, owned, LANES), F32),
            ],
            compiler_params=PARAMETERS,
            name="update",
        )(every, gaussians, first_moment, second_moment)
    with jax.named_scope("camera"):
        camera_total = jnp.sum(camera_parts, axis=0)[:, :6]
    return (
        new_gaussians.transpose(1, 0, 2),
        new_first.transpose(1, 0, 2),
        new_second.transpose(1, 0, 2),
        camera_total,
    )


def solution(mesh):
    return jax.shard_map(
        shards,
        mesh=mesh,
        in_specs=(
            P("cell", None, None),
            P("cell", None, None),
            P("cell", None, None),
            P("view", None),
            P("view", "cell"),
            P("view", "cell"),
            P("view", "cell", None),
            P("view", "cell"),
            P("view", "cell", None, None),
        ),
        out_specs=(
            P("cell", None, None),
            P("cell", None, None),
            P("cell", None, None),
            P("view", None),
        ),
        check_vma=False,
    )
```

time: 126 us -> 114 us (0.905); the launches traced: 126 us -> 112 us
  blocking collectives: 52.4 us -> 28.8 us
  starting transfers between devices: 29.3 us -> 42.1 us
  Pallas kernels: 19.8 us -> 11 us
  waiting for transfers between devices: 16.9 us -> 25.5 us
  local copies, waits for them, and re-layouts: 5.59 us -> 2.33 us
    all_to_all x1 -> x0, blocking collectives: 22.5 us -> none  [shards(): lax.all_to_all(pair, 'cell', 0, 0, axis_index_groups=same_core, tiled=True)]
    all_to_all x1 -> x2, waiting for transfers between devices: 6.1 us -> 19.4 us  [the longest x1 14.6 us: shards(): lax.all_to_all(pair, 'cell', 0, 0, axis_index_groups=same_core, tiled=True)]
    pallas_call x2 -> x3, Pallas kernels: 14.6 us -> 6.46 us  [the longest x1 3.96 us: shards(): pl.pallas_call(render_kernel, out_shape=[jax.ShapeDtypeStruct((chips, FEA...]
    all_to_all x1 -> x2, starting transfers between devices: 11.4 us -> 17.4 us  [the longest x1 9.29 us: shards(): lax.all_to_all(pair, 'cell', 0, 0, axis_index_groups=same_core, tiled=True)]
    ppermute x0 -> x1, starting transfers between devices: none -> 5.59 us  [shards(): camera_pair = camera_part + lax.ppermute(camera_part, 'cell', swap)]
    all_to_all x1, waiting for transfers between devices: 7.45 us -> 2.16 us  [shards(): every = lax.all_to_all(own, 'view', 0, 0, tiled=True)]
    unnamed x23 -> x21, local copies, waits for them, and re-layouts: 5.59 us -> 1.72 us
    ppermute x1, starting transfers between devices: 4.27 us -> 6.52 us  [shards(): pair = near_grad + lax.ppermute(far_grad, 'cell', swap)]
  transfers between devices with their start and end apart: 4 -> 6, of which waited for: 4 -> 6; matrix products, arithmetic and copies ran while one was open for 3% -> 0% of each run, Pallas kernels for 0% -> 4%
where the time goes in v2:
time: 114 us; the launch traced here: 112 us
  starting transfers between devices  42.1 us (37%)
  blocking collectives  28.8 us (25%)
  waiting for transfers between devices  25.5 us (22%)
  Pallas kernels  11 us (10%)
  local copies, waits for them, and re-layouts  2.33 us (2%)
  other arithmetic  1.51 us (1%)
    all_to_all x1, blocking collectives, shards(): lax.all_to_all(message, 'cell', 0, 0, axis_index_groups=same_core, tiled=...  28.8 us
    all_to_all x1, waiting for transfers between devices, shards(): lax.all_to_all(pair, 'cell', 0, 0, axis_index_groups=same_core, tiled=True)  14.6 us
    all_to_all x1, starting transfers between devices, shards(): lax.all_to_all(pair, 'cell', 0, 0, axis_index_groups=same_core, tiled=True)  9.29 us
    all_to_all x1, starting transfers between devices, shards(): lax.all_to_all(jnp.broadcast_to(camera_pair, (chips, 1, LANES)), 'cell',...  8.08 us
    ppermute x1, starting transfers between devices, shards(): pair = near_grad + lax.ppermute(far_grad, 'cell', swap)  6.52 us
    all_to_all x1, starting transfers between devices, shards(): every = lax.all_to_all(own, 'view', 0, 0, tiled=True)  6.41 us
    ppermute x1, starting transfers between devices, shards(): far = lax.ppermute(near, 'cell', swap)  6.16 us
    ppermute x1, starting transfers between devices, shards(): camera_pair = camera_part + lax.ppermute(camera_part, 'cell', swap)  5.59 us
  transfers between devices with their start and end apart: 6, of which 6 were waited for; matrix products, arithmetic and copies ran while one was open for 0% of the time, Pallas kernels for 4%

profile of v2, /device:TPU:1, one launch (start us, length us, event | category | flops | bytes accessed | tf_op | source)
XLA Modules:
  0.0 112.0 jit_solution(9294782888098357202)
XLA Ops:
  0.6 0.0 copy-start.5
  0.6 0.0 copy-start.4
  0.7 0.6 copy-done.5
  1.3 0.0 copy-done.4
  1.3 1.0 copy-done
  2.3 0.8 project.1
  3.1 0.0 copy-start.9
  3.1 28.8 %all_to_all.20.near_ref = f32[32,9,4,128]{3,2,1,0:T(4,128)S(1)} all-to-all(f32[32,9,4,128]{3,2,1,0:T(4,128)S(1)} %project.1), channel_id=1, replica_groups={{0,16,32,48,64,80,96,112,128,144,160,176,192,208,224,240,256,272,288,30..., dimensions={0} | all-to-all | bytes 1179648 | tf_op jit(solution)/shard_map/gather/all_to_all | solution.py:550
  31.9 6.2 %collective-permute-start = (f32[32,9,4,128]{3,2,1,0:T(4,128)S(1)}, f32[32,9,4,128]{3,2,1,0:T(4,128)S(1)}, u32[]{:S(2)}, u32[]{:S(2)}) collective-permute-start(f32[32,9,4,128]{3,2,1,0:T(4,128)S(1)} %all_to_all.20.near_ref), channel_id=1, source_target_pairs={{0,8},{8,0},{16,24},{24,16},{32,40},{40,32},{48,56},{56,48},{64,72... | collective-permute-start | bytes 1769480 | tf_op jit(solution)/shard_map/gather/ppermute | solution.py:551
  38.1 0.0 copy-done.9
  38.1 1.6 %collective-permute-done.far_ref = f32[32,9,4,128]{3,2,1,0:T(4,128)S(1)} collective-permute-done((f32[32,9,4,128]{3,2,1,0:T(4,128)S(1)}, f32[32,9,4,128]{3,2,1,0:T(4,128)S(1)}, u32[]{:S(2)}, u32[]{:S(2)}) %collective-permute-start) | collective-permute-done | bytes 589856 | tf_op jit(solution)/shard_map/gather/ppermute | solution.py:551
  39.7 0.0 copy-done.7
  39.7 4.0 %render.1 = (f32[32,9,4,128]{3,2,1,0:T(4,128)S(1)}, f32[32,9,4,128]{3,2,1,0:T(4,128)S(1)}) custom-call(s32[1,2,4]{2,1,0:T(2,128)S(1)} %copy-done.6, s32[1,2]{1,0:T(1,128)S(1)} %copy-done.7, s32[1,2]{1,0:T(1,128)S(1)} %copy-done.8, bf16[1,2,3,256]{3,2,1,0:T(4,128)(2,1)S(1)} %copy.15.target_ref, f32[32,9,4,128]{3,2,1,0:T(4,128)S(1)} %all_to_all.20.near_ref, ...), custom_call_target="tpu_custom_call" | custom-call | tf_op jit(solution)/shard_map/render/render/pallas_call | solution.py:554
  43.7 6.5 %collective-permute-start.1 = (f32[32,9,4,128]{3,2,1,0:T(4,128)S(1)}, f32[32,9,4,128]{3,2,1,0:T(4,128)S(1)}, u32[]{:S(2)}, u32[]{:S(2)}) collective-permute-start(f32[32,9,4,128]{3,2,1,0:T(4,128)S(1)} %get-tuple-element.14), channel_id=1, source_target_pairs={{0,8},{8,0},{16,24},{24,16},{32,40},{40,32},{48,56},{56,48},{64,72... | collective-permute-start | bytes 1769480 | tf_op jit(solution)/shard_map/scatter/ppermute | solution.py:571
  50.2 1.6 %collective-permute-done.1 = f32[32,9,4,128]{3,2,1,0:T(4,128)S(1)} collective-permute-done((f32[32,9,4,128]{3,2,1,0:T(4,128)S(1)}, f32[32,9,4,128]{3,2,1,0:T(4,128)S(1)}, u32[]{:S(2)}, u32[]{:S(2)}) %collective-permute-start.1) | collective-permute-done | bytes 589856 | tf_op jit(solution)/shard_map/scatter/ppermute | solution.py:571
  51.8 1.0 add.6
  52.8 9.3 %all-to-all-start.1 = ((f32[32,9,4,128]{3,2,1,0:T(4,128)}), f32[32,9,4,128]{3,2,1,0:T(4,128)S(1)}, u32[]{:S(2)}, u32[]{:S(2)}) async-start(f32[32,9,4,128]{3,2,1,0:T(4,128)} %add.6), calls=%async_computation.1 | async-start | bytes 1179648 | tf_op jit(solution)/shard_map/scatter/all_to_all | solution.py:572
  62.1 0.0 copy-done.1
  62.1 1.2 %slope.1.refs_3_ = f32[6,9,4,128]{3,2,1,0:T(4,128)S(1)} custom-call(s32[1,2]{1,0:T(1,128)S(1)} %copy-done.4, f32[1,6]{1,0:T(1,128)S(1)} %copy-done.5, f32[59,8,256]{2,1,0:T(8,128)S(1)} %bitcast.11), custom_call_target="tpu_custom_call" | custom-call | flops 4000000 | bytes 200000 | tf_op jit(solution)/shard_map/project/slope/pallas_call | solution.py:538
  63.3 0.0 copy-start.2
  63.3 0.0 copy-start.3
  63.3 14.6 %all-to-all-done.1.refs_2_ = f32[32,9,4,128]{3,2,1,0:T(4,128)S(1)} async-done(((f32[32,9,4,128]{3,2,1,0:T(4,128)}), f32[32,9,4,128]{3,2,1,0:T(4,128)S(1)}, u32[]{:S(2)}, u32[]{:S(2)}) %all-to-all-start.1) | async-done | bytes 589856 | tf_op jit(solution)/shard_map/scatter/all_to_all | solution.py:572
  77.9 1.3 %collect.1 = (f32[8,11,4,128]{3,2,1,0:T(4,128)}, f32[1,1,128]{2,1,0:T(1,128)S(1)}) custom-call(s32[1,2]{1,0:T(1,128)S(1)} %copy-done.4, f32[1,6]{1,0:T(1,128)S(1)} %copy-done.5, f32[32,9,4,128]{3,2,1,0:T(4,128)S(1)} %all-to-all-done.1.refs_2_, f32[6,9,4,128]{3,2,1,0:T(4,128)S(1)} %slope.1.refs_3_), custom_call_target="tpu_custom_call" | custom-call | tf_op jit(solution)/shard_map/collect/collect/pallas_call | solution.py:574
  79.2 6.4 %all-to-all-start.2 = ((f32[8,11,4,128]{3,2,1,0:T(4,128)}), f32[8,11,4,128]{3,2,1,0:T(4,128)S(1)}, u32[]{:S(2)}, u32[]{:S(2)}) async-start(f32[8,11,4,128]{3,2,1,0:T(4,128)} %get-tuple-element.15), calls=%async_computation.2 | async-start | bytes 360448 | tf_op jit(solution)/shard_map/collect/all_to_all | solution.py:585
  85.6 5.6 %collective-permute-start.2 = (f32[1,1,128]{2,1,0:T(1,128)S(1)}, f32[1,1,128]{2,1,0:T(1,128)S(1)}, u32[]{:S(2)}, u32[]{:S(2)}) collective-permute-start(f32[1,1,128]{2,1,0:T(1,128)S(1)} %get-tuple-element.16), channel_id=1, source_target_pairs={{0,8},{8,0},{16,24},{24,16},{32,40},{40,32},{48,56},{56,48},{64,72... | collective-permute-start | bytes 1544 | tf_op jit(solution)/shard_map/camera/ppermute | solution.py:587
  91.2 0.8 collective-permute-done.2
  92.0 2.2 %all-to-all-done.2.refs_0_ = f32[8,11,4,128]{3,2,1,0:T(4,128)S(1)} async-done(((f32[8,11,4,128]{3,2,1,0:T(4,128)}), f32[8,11,4,128]{3,2,1,0:T(4,128)S(1)}, u32[]{:S(2)}, u32[]{:S(2)}) %all-to-all-start.2) | async-done | bytes 180256 | tf_op jit(solution)/shard_map/collect/all_to_all | solution.py:585
  94.2 0.6 broadcast_in_dim.8
  94.8 8.1 %all-to-all-start.3 = ((f32[32,1,128]{2,1,0:T(1,128)}), f32[32,1,128]{2,1,0:T(1,128)S(1)}, u32[]{:S(2)}, u32[]{:S(2)}) async-start(f32[32,1,128]{2,1,0:T(1,128)} %broadcast_in_dim.8), calls=%async_computation.3 | async-start | bytes 32768 | tf_op jit(solution)/shard_map/camera/all_to_all | solution.py:589
  102.9 3.8 %update.1 = (f32[59,8,256]{2,1,0:T(8,128)}, f32[59,8,256]{2,1,0:T(8,128)}, f32[59,8,256]{2,1,0:T(8,128)}) custom-call(f32[8,11,4,128]{3,2,1,0:T(4,128)S(1)} %all-to-all-done.2.refs_0_, f32[59,8,256]{2,1,0:T(8,128)S(1)} %bitcast.12, f32[59,8,256]{2,1,0:T(8,128)S(1)} %bitcast.13, f32[59,8,256]{2,1,0:T(8,128)S(1)} %bitcast.14), custom_call_target="tpu_custom_call" | custom-call | tf_op jit(solution)/shard_map/update/update/pallas_call | solution.py:599
  106.7 4.8 %all-to-all-done.3 = f32[32,1,128]{2,1,0:T(1,128)S(1)} async-done(((f32[32,1,128]{2,1,0:T(1,128)}), f32[32,1,128]{2,1,0:T(1,128)S(1)}, u32[]{:S(2)}, u32[]{:S(2)}) %all-to-all-start.3) | async-done | bytes 16416 | tf_op jit(solution)/shard_map/camera/all_to_all | solution.py:589
  111.5 0.5 reduce_sum.11
  (11 shorter events, 0.0 us)
Async XLA Ops:
  0.6 0.7 copy-start.5
  0.6 0.7 copy-start.4
  1.3 1.0 copy-start
  3.1 35.0 %copy-start.9 = (bf16[1,2,3,256]{3,1,2,0:T(2,128)(2,1)S(1)}, bf16[1,2,3,256]{3,1,2,0:T(2,128)(2,1)}, u32[]{:S(2)}) copy-start(bf16[1,2,3,256]{3,1,2,0:T(2,128)(2,1)} %param.17) | copy-start | bytes 9220
  31.9 7.8 %copy-start.6 = (s32[1,2,4]{2,1,0:T(2,128)S(1)}, s32[1,2,4]{2,1,0:T(2,128)}, u32[]{:S(2)}) copy-start(s32[1,2,4]{2,1,0:T(2,128)} %order_ref.1) | copy-start | bytes 100
  31.9 7.8 %copy-start.7 = (s32[1,2]{1,0:T(1,128)S(1)}, s32[1,2]{1,0:T(1,128)}, u32[]{:S(2)}) copy-start(s32[1,2]{1,0:T(1,128)} %length_ref.1) | copy-start | bytes 28
  31.9 7.8 %copy-start.8 = (s32[1,2]{1,0:T(1,128)S(1)}, s32[1,2]{1,0:T(1,128)}, u32[]{:S(2)}) copy-start(s32[1,2]{1,0:T(1,128)} %tile_ref.1) | copy-start | bytes 28
  31.9 7.8 %collective-permute-start = (f32[32,9,4,128]{3,2,1,0:T(4,128)S(1)}, f32[32,9,4,128]{3,2,1,0:T(4,128)S(1)}, u32[]{:S(2)}, u32[]{:S(2)}) collective-permute-start(f32[32,9,4,128]{3,2,1,0:T(4,128)S(1)} %all_to_all.20.near_ref), channel_id=1, source_target_pairs={{0,8},{8,0},{16,24},{24,16},{32,40},{40,32},{48,56},{56,48},{64,72... | collective-permute-start | bytes 1769480 | tf_op jit(solution)/shard_map/gather/ppermute | solution.py:551
  43.7 8.1 %collective-permute-start.1 = (f32[32,9,4,128]{3,2,1,0:T(4,128)S(1)}, f32[32,9,4,128]{3,2,1,0:T(4,128)S(1)}, u32[]{:S(2)}, u32[]{:S(2)}) collective-permute-start(f32[32,9,4,128]{3,2,1,0:T(4,128)S(1)} %get-tuple-element.14), channel_id=1, source_target_pairs={{0,8},{8,0},{16,24},{24,16},{32,40},{40,32},{48,56},{56,48},{64,72... | collective-permute-start | bytes 1769480 | tf_op jit(solution)/shard_map/scatter/ppermute | solution.py:571
  52.8 9.3 %copy-start.1 = (f32[8,59,256]{2,0,1:T(8,128)S(1)}, f32[8,59,256]{2,0,1:T(8,128)}, u32[]{:S(2)}) copy-start(f32[8,59,256]{2,0,1:T(8,128)} %param.9) | copy-start | bytes 1449988
  52.8 25.1 %all-to-all-start.1 = ((f32[32,9,4,128]{3,2,1,0:T(4,128)}), f32[32,9,4,128]{3,2,1,0:T(4,128)S(1)}, u32[]{:S(2)}, u32[]{:S(2)}) async-start(f32[32,9,4,128]{3,2,1,0:T(4,128)} %add.6), calls=%async_computation.1 | async-start | bytes 1179648 | tf_op jit(solution)/shard_map/scatter/all_to_all | solution.py:572
  63.3 39.6 %copy-start.2 = (f32[8,59,256]{2,0,1:T(8,128)S(1)}, f32[8,59,256]{2,0,1:T(8,128)}, u32[]{:S(2)}) copy-start(f32[8,59,256]{2,0,1:T(8,128)} %param.10) | copy-start | bytes 1449988
  63.3 39.6 %copy-start.3 = (f32[8,59,256]{2,0,1:T(8,128)S(1)}, f32[8,59,256]{2,0,1:T(8,128)}, u32[]{:S(2)}) copy-start(f32[8,59,256]{2,0,1:T(8,128)} %param.11) | copy-start | bytes 1449988
  79.2 15.0 %all-to-all-start.2 = ((f32[8,11,4,128]{3,2,1,0:T(4,128)}), f32[8,11,4,128]{3,2,1,0:T(4,128)S(1)}, u32[]{:S(2)}, u32[]{:S(2)}) async-start(f32[8,11,4,128]{3,2,1,0:T(4,128)} %get-tuple-element.15), calls=%async_computation.2 | async-start | bytes 360448 | tf_op jit(solution)/shard_map/collect/all_to_all | solution.py:585
  85.6 6.4 %collective-permute-start.2 = (f32[1,1,128]{2,1,0:T(1,128)S(1)}, f32[1,1,128]{2,1,0:T(1,128)S(1)}, u32[]{:S(2)}, u32[]{:S(2)}) collective-permute-start(f32[1,1,128]{2,1,0:T(1,128)S(1)} %get-tuple-element.16), channel_id=1, source_target_pairs={{0,8},{8,0},{16,24},{24,16},{32,40},{40,32},{48,56},{56,48},{64,72... | collective-permute-start | bytes 1544 | tf_op jit(solution)/shard_map/camera/ppermute | solution.py:587
  94.8 16.7 %all-to-all-start.3 = ((f32[32,1,128]{2,1,0:T(1,128)}), f32[32,1,128]{2,1,0:T(1,128)S(1)}, u32[]{:S(2)}, u32[]{:S(2)}) async-start(f32[32,1,128]{2,1,0:T(1,128)} %broadcast_in_dim.8), calls=%async_computation.3 | async-start | bytes 32768 | tf_op jit(solution)/shard_map/camera/all_to_all | solution.py:589

commit v3 on v2

--- a/solution.py
+++ b/solution.py
@@ -1,3 +1,5 @@
+import functools
+
 import jax
 import jax.numpy as jnp
 from jax import lax
@@ -248,85 +250,100 @@
     second = lax.broadcasted_iota(jnp.int32, (BLOCK, BLOCK), 1)
     earlier = (first < second).astype(BF16)
     later = (first > second).astype(BF16)
-    ones = jnp.ones((BLOCK, LANES), BF16)
     step_x = lax.broadcasted_iota(jnp.int32, (TILE, BLOCK), 0).astype(F32) - 7.5
-    part = lax.broadcasted_iota(jnp.int32, (ROWS, LANES), 0)
+    part = lax.broadcasted_iota(jnp.int32, (8, LANES), 0)
     targets = target_ref[...].astype(F32)
 
-    def spread_over(value):
-        return jnp.concatenate([value, value], axis=1)
-
+    places = []
     for slot in range(slots):
         tile = tile_ref[0, slot]
-        tile_x = (lax.rem(tile, 16) * TILE + 8).astype(F32)
-        tile_y = (lax.div(tile, 16) * TILE + 8).astype(F32)
-        length = length_ref[0, slot]
-
-        def forward(k, carry):
-            log_remain, colour = carry
-            block = order_ref[0, slot, k]
-            chip = lax.div(block, 4)
-            on_near = lax.rem(lax.div(block, 2), CORES) == core
-            even = lax.rem(block, 2) == 0
+        places.append(
+            (
+                (lax.rem(tile, 16) * TILE + 8).astype(F32),
+                (lax.div(tile, 16) * TILE + 8).astype(F32),
+            )
+        )
+    longest = functools.reduce(jnp.maximum, [length_ref[0, slot] for slot in range(slots)])
+
+    def owner(slot, k):
+        block = order_ref[0, slot, k]
+        on_near = lax.rem(lax.div(block, 2), CORES) == core
+        return lax.div(block, 4), on_near, lax.rem(block, 2)
+
+    def forward(k, carry):
+        remains, colours = carry
+        alphas, keeps = [], []
+        for slot in range(slots):
+            chip, on_near, side = owner(slot, k)
             for f in range(FEATURES):
                 entry = jnp.where(on_near, near_ref[chip, f], far_ref[chip, f])
-                entry = jnp.where(even, entry[0:2], entry[2:4])
-                feature_scr[k, f : f + 1, 0:LANES] = entry[0:1]
-                feature_scr[k, f : f + 1, LANES:] = entry[1:2]
-            feature = feature_scr.at[k]
-            rgb_scr[k] = stacked(feature[6:9, :], 16)
-            delta_x = step_x - (feature[0:1, :] - tile_x)
-            local_y = feature[1:2, :] - tile_y
+                entry = jnp.where(side == 0, entry[0:2], entry[2:4])
+                feature_scr[slot, k, f : f + 1, 0:LANES] = entry[0:1]
+                feature_scr[slot, k, f : f + 1, LANES:] = entry[1:2]
+            feature = feature_scr.at[slot, k]
+            rgb_scr[slot, k] = stacked(feature[6:9, :], 16)
+            delta_x = step_x - (feature[0:1, :] - places[slot][0])
+            local_y = feature[1:2, :] - places[slot][1]
             curve_x = (-0.5 * LOG2E) * feature[2:3, :] * delta_x * delta_x
             cross_x = (-LOG2E) * feature[3:4, :] * delta_x
             curve = (-0.5 * LOG2E) * feature[4:5, :]
+            opacity = jnp.where(k < length_ref[0, slot], feature[5:6, :], 0.0)
             rows = []
             for i in range(TILE):
                 delta_y = (i - 7.5) - local_y
                 rows.append(curve_x + (cross_x * delta_y + curve * delta_y * delta_y))
-            exponent = jnp.concatenate(rows, axis=0)
-            alpha = feature[5:6, :] * jnp.exp2(exponent)
+            alpha = opacity * jnp.exp2(jnp.concatenate(rows, axis=0))
             keep = alpha * (
                 -LOG2E
                 - alpha * (LOG2E / 2.0 + alpha * (LOG2E / 3.0 + alpha * (LOG2E / 4.0)))
             )
-            pair = split(keep)
-            before = both_dots(pair, earlier) + spread_over(log_remain)
-            weight = alpha * jnp.exp2(before)
-            ratio_scr[k] = alpha * jnp.exp2(-keep)
-            weight_scr[k] = weight
+            ratio_scr[slot, k] = alpha * jnp.exp2(-keep)
+            alphas.append(alpha)
+            keeps.append(keep)
+        inner = [both_dots(split(keep), earlier) for keep in keeps]
+        new_remains, new_colours = [], []
+        for slot in range(slots):
+            before = inner[slot] + remains[slot]
+            weight = alphas[slot] * jnp.exp2(before)
+            weight_scr[slot, k] = weight
             high, low = split(weight)
-            high_scr[k] = high
-            low_scr[k] = low
-            colour = colour + transpose_dot(high, rgb_scr[k]) + transpose_dot(low, rgb_scr[k])
-            return (log_remain + both_dots(pair, ones), colour)
-
-        _, colour = lax.fori_loop(
-            0, length, forward, (jnp.zeros((PIX, LANES), F32), jnp.zeros((PIX, 16), F32))
-        )
-        turned = colour.T
-        misfit = turned[0:3] + turned[3:6] - targets[0, slot]
-        misfit_rows = stacked(misfit, 16)
-        misfit_high, misfit_low = split(misfit)
-        misfit_high = misfit_high.astype(F32)
-        misfit_low = misfit_low.astype(F32)
-        blank = jnp.zeros((10, PIX), F32)
-        misfit_pair = tuple(
-            jnp.concatenate([term, term, blank], axis=0).T.astype(BF16)
-            for term in (misfit_high, misfit_low)
-        )
-
-        def backward(step, behind):
-            k = length - 1 - step
-            block = order_ref[0, slot, k]
-            chip = lax.div(block, 4)
-            on_near = lax.rem(lax.div(block, 2), CORES) == core
-            side = lax.rem(block, 2) * 2
-            feature = feature_scr.at[k]
-            through = weight_scr[k] * both_dots(misfit_pair, rgb_scr[k])
-            pair = split(through)
-            after = both_dots(pair, later) + spread_over(behind)
-            slope = through - after * ratio_scr[k]
+            high_scr[slot, k] = high
+            low_scr[slot, k] = low
+            rgb = rgb_scr[slot, k]
+            new_remains.append(before[:, BLOCK - 1 :] + keeps[slot][:, BLOCK - 1 :])
+            new_colours.append(
+                colours[slot] + transpose_dot(rgb, high) + transpose_dot(rgb, low)
+            )
+        return tuple(new_remains), tuple(new_colours)
+
+    zero = (jnp.zeros((PIX, 1), F32),) * slots
+    _, colours = lax.fori_loop(
+        0, longest, forward, (zero, (jnp.zeros((16, PIX), F32),) * slots)
+    )
+    misfit_rows, misfit_cols = [], []
+    for slot in range(slots):
+        misfit = colours[slot][0:3] + colours[slot][3:6] - targets[0, slot]
+        misfit_rows.append(stacked(misfit, 16))
+        turned = jnp.concatenate([misfit, jnp.zeros((5, PIX), F32)], axis=0).T
+        misfit_cols.append([turned[:, c : c + 1] for c in range(3)])
+
+    def backward(step, behind):
+        k = longest - 1 - step
+        throughs = []
+        for slot in range(slots):
+            feature = feature_scr.at[slot, k]
+            throughs.append(
+                weight_scr[slot, k]
+                * sum(misfit_cols[slot][c] * feature[6 + c : 7 + c, :] for c in range(3))
+            )
+        inner = [both_dots(split(through), later) for through in throughs]
+        new_behind = []
+        for slot in range(slots):
+            feature = feature_scr.at[slot, k]
+            chip, on_near, side = owner(slot, k)
+            after = inner[slot] + behind[slot]
+            slope = throughs[slot] - after * ratio_scr[slot, k]
+            new_behind.append(after[:, 0:1] + throughs[slot][:, 0:1])
             flat = jnp.zeros((TILE, BLOCK), F32)
             tilt = jnp.zeros((TILE, BLOCK), F32)
             bend = jnp.zeros((TILE, BLOCK), F32)
@@ -337,9 +354,11 @@
                 flat = flat + (top + bottom)
                 tilt = tilt + away * (bottom - top)
                 bend = bend + (away * away) * (top + bottom)
-            colour_grad = dot(misfit_rows, high_scr[k]) + dot(misfit_rows, low_scr[k])
-            delta_x = step_x - (feature[0:1, :] - tile_x)
-            local_y = feature[1:2, :] - tile_y
+            colour_grad = dot(misfit_rows[slot], high_scr[slot, k]) + dot(
+                misfit_rows[slot], low_scr[slot, k]
+            )
+            delta_x = step_x - (feature[0:1, :] - places[slot][0])
+            local_y = feature[1:2, :] - places[slot][1]
             mean = tilt - local_y * flat
             bend = bend - local_y * (tilt + mean)
 
@@ -359,36 +378,54 @@
                 -0.5 * square_y,
                 total / feature[5:6, :],
             ] + [colour_grad[i : i + 1] + colour_grad[i + 3 : i + 4] for i in range(3)]
-            placed = [
-                jnp.where(
-                    part == side,
-                    grad[:, :LANES],
-                    jnp.where(part == side + 1, grad[:, LANES:], 0.0),
+            spots, placed = [], []
+            for f in range(FEATURES):
+                spot = chip * FEATURES + f
+                at = lax.rem(spot, 2) * ROWS + side * 2
+                spots.append(lax.div(spot, 2))
+                placed.append(
+                    jnp.where(
+                        part == at,
+                        grads[f][:, :LANES],
+                        jnp.where(part == at + 1, grads[f][:, LANES:], 0.0),
+                    )
                 )
-                for grad in grads
-            ]
 
             @pl.when(on_near)
             def _():
                 for f in range(FEATURES):
-                    near_out[chip, f] += placed[f]
+                    near_out[spots[f]] += placed[f]
 
             @pl.when(jnp.logical_not(on_near))
             def _():
                 for f in range(FEATURES):
-                    far_out[chip, f] += placed[f]
-
-            return behind + both_dots(pair, ones)
-
-        lax.fori_loop(0, length, backward, jnp.zeros((PIX, LANES), F32))
+                    far_out[spots[f]] += placed[f]
+
+        return tuple(new_behind)
+
+    lax.fori_loop(0, longest, backward, zero)
+
+
+def render_scratch(slots, depth):
+    return [
+        pltpu.VMEM((slots, depth, 16, BLOCK), F32),
+        pltpu.VMEM((slots, depth, 16, BLOCK), BF16),
+        pltpu.VMEM((slots, depth, PIX, BLOCK), F32),
+        pltpu.VMEM((slots, depth, PIX, BLOCK), BF16),
+        pltpu.VMEM((slots, depth, PIX, BLOCK), BF16),
+        pltpu.VMEM((slots, depth, PIX, BLOCK), F32),
+    ]
 
 
 def collect_kernel(owned, visible_ref, camera_ref, parts_ref, slope_ref, out_ref, camera_out):
     base = lax.axis_index("cell") * owned
-    total = parts_ref[0]
-    for i in range(1, parts_ref.shape[0]):
-        total = total + parts_ref[i]
-    out_ref[0, 0:FEATURES] = total
+    paired = parts_ref[0:FEATURES]
+    for i in range(1, parts_ref.shape[0] // FEATURES):
+        paired = paired + parts_ref[i * FEATURES : (i + 1) * FEATURES]
+    pieces = [paired[i // 2, (i % 2) * ROWS : (i % 2 + 1) * ROWS] for i in range(2 * FEATURES)]
+    total = [pieces[f] + pieces[FEATURES + f] for f in range(FEATURES)]
+    for f in range(FEATURES):
+        out_ref[0, f] = total[f]
     base_rows = [jnp.full((1, LANES), camera_ref[0, i], F32) for i in range(6)] + [
         jnp.full((1, LANES), (visible_ref[0, sub] - base).astype(F32), F32) for sub in range(2)
     ]
@@ -401,7 +438,7 @@
     packed = jnp.zeros((1, LANES), F32)
     for i in range(6):
         across = jnp.sum(
-            jnp.sum(total * slope_ref[i], axis=0), axis=0, keepdims=True
+            sum(total[f] * slope_ref[i, f] for f in range(FEATURES)), axis=0, keepdims=True
         )
         packed = packed + jnp.where(lane == i, jnp.sum(across, axis=1, keepdims=True), 0.0)
     for i in range(camera_out.shape[0]):
@@ -549,27 +586,20 @@
     with jax.named_scope("gather"):
         near = lax.all_to_all(message, "cell", 0, 0, axis_index_groups=same_core, tiled=True)
         far = lax.ppermute(near, "cell", swap)
-    depth = tile_order.shape[2]
     with jax.named_scope("render"):
         near_grad, far_grad = pl.pallas_call(
             render_kernel,
-            out_shape=[jax.ShapeDtypeStruct((chips, FEATURES, ROWS, LANES), F32)] * 2,
+            out_shape=[jax.ShapeDtypeStruct((chips * FEATURES * ROWS // 8, 8, LANES), F32)] * 2,
             in_specs=[SMEM, SMEM, SMEM, VMEM, VMEM, VMEM],
             out_specs=[VMEM, VMEM],
-            scratch_shapes=[
-                pltpu.VMEM((depth, 16, BLOCK), F32),
-                pltpu.VMEM((depth, 16, BLOCK), BF16),
-                pltpu.VMEM((depth, PIX, BLOCK), F32),
-                pltpu.VMEM((depth, PIX, BLOCK), BF16),
-                pltpu.VMEM((depth, PIX, BLOCK), BF16),
-                pltpu.VMEM((depth, PIX, BLOCK), F32),
-            ],
+            scratch_shapes=render_scratch(*tile_order.shape[1:]),
             compiler_params=PARAMETERS,
             name="render",
         )(tile_order, tile_length, tile_ids, targets, near, far)
     with jax.named_scope("scatter"):
         pair = near_grad + lax.ppermute(far_grad, "cell", swap)
-        parts = lax.all_to_all(pair, "cell", 0, 0, axis_index_groups=same_core, tiled=True)
+        parts = lax.all_to_all(
+            pair.reshape(near.shape), "cell", 0, 0, axis_index_groups=same_core, tiled=True)
     with jax.named_scope("collect"):
         own, camera_part = pl.pallas_call(
             lambda *refs: collect_kernel(owned, *refs),
@@ -581,7 +611,7 @@
             out_specs=[VMEM, VMEM],
             compiler_params=PARAMETERS,
             name="collect",
-        )(visible_blocks, cameras, parts, slopes)
+        )(visible_blocks, cameras, parts.reshape(pair.shape), slopes)
         every = lax.all_to_all(own, "view", 0, 0, tiled=True)
     with jax.named_scope("camera"):
         camera_pair = camera_part + lax.ppermute(camera_part, "cell", swap)

time: 114 us -> 109 us (0.956)
  starting transfers between devices: 42.1 us -> 33.5 us
  Pallas kernels: 11 us -> 14.4 us
    ppermute x1, starting transfers between devices: 6.52 us -> 1.92 us  [shards(): pair = near_grad + lax.ppermute(far_grad, 'cell', swap)]
    all_to_all x1, starting transfers between devices: 9.29 us -> 5.2 us  [shards(): lax.all_to_all(pair.reshape(near.shape), 'cell', 0, 0, axis_index_groups=...]
    pallas_call x1, Pallas kernels: 3.96 us -> 7.33 us  [shards(): pl.pallas_call(render_kernel, out_shape=[jax.ShapeDtypeStruct((chips * FE...]
  transfers between devices with their start and end apart: 6 -> 6, of which waited for: 6 -> 6; matrix products, arithmetic and copies ran while one was open for 0% -> 0% of each run, Pallas kernels for 4% -> 5%
where the time goes in v3:
time: 109 us; the launch traced here: 107 us
  starting transfers between devices  33.5 us (31%)
  blocking collectives  28.8 us (26%)
  waiting for transfers between devices  25.7 us (24%)
  Pallas kernels  14.4 us (13%)
  local copies, waits for them, and re-layouts  2.32 us (2%)
  other arithmetic  1.41 us (1%)
    all_to_all x1, blocking collectives, shards(): lax.all_to_all(message, 'cell', 0, 0, axis_index_groups=same_core, tiled=...  28.8 us
    all_to_all x1, waiting for transfers between devices, shards(): lax.all_to_all(pair.reshape(near.shape), 'cell', 0, 0, axis_index_groups=...  14.3 us
    all_to_all x1, starting transfers between devices, shards(): lax.all_to_all(jnp.broadcast_to(camera_pair, (chips, 1, LANES)), 'cell',...  8.08 us
    pallas_call x1, Pallas kernels, shards(): pl.pallas_call(render_kernel, out_shape=[jax.ShapeDtypeStruct((chips * FE...  7.33 us
    all_to_all x1, starting transfers between devices, shards(): every = lax.all_to_all(own, 'view', 0, 0, tiled=True)  6.54 us
    ppermute x1, starting transfers between devices, shards(): far = lax.ppermute(near, 'cell', swap)  6.16 us
    ppermute x1, starting transfers between devices, shards(): camera_pair = camera_part + lax.ppermute(camera_part, 'cell', swap)  5.59 us
    all_to_all x1, starting transfers between devices, shards(): lax.all_to_all(pair.reshape(near.shape), 'cell', 0, 0, axis_index_groups=...  5.2 us
  transfers between devices with their start and end apart: 6, of which 6 were waited for; matrix products, arithmetic and copies ran while one was open for 0% of the time, Pallas kernels for 5%

profile of v3, /device:TPU:1, one launch (start us, length us, event | category | flops | bytes accessed | tf_op | source)
XLA Modules:
  0.0 106.8 jit_solution(15451727131619347187)
XLA Ops:
  0.6 0.0 copy-start.5
  0.6 0.0 copy-start.4
  0.7 0.6 copy-done.5
  1.3 0.0 copy-done.4
  1.3 1.0 copy-done
  2.3 0.8 project.1
  3.1 0.0 copy-start.9
  3.1 28.8 %all_to_all.20.near_ref = f32[32,9,4,128]{3,2,1,0:T(4,128)S(1)} all-to-all(f32[32,9,4,128]{3,2,1,0:T(4,128)S(1)} %project.1), channel_id=1, replica_groups={{0,16,32,48,64,80,96,112,128,144,160,176,192,208,224,240,256,272,288,30..., dimensions={0} | all-to-all | bytes 1179648 | tf_op jit(solution)/shard_map/gather/all_to_all | solution.py:587
  31.9 6.2 %collective-permute-start = (f32[32,9,4,128]{3,2,1,0:T(4,128)S(1)}, f32[32,9,4,128]{3,2,1,0:T(4,128)S(1)}, u32[]{:S(2)}, u32[]{:S(2)}) collective-permute-start(f32[32,9,4,128]{3,2,1,0:T(4,128)S(1)} %all_to_all.20.near_ref), channel_id=1, source_target_pairs={{0,8},{8,0},{16,24},{24,16},{32,40},{40,32},{48,56},{56,48},{64,72... | collective-permute-start | bytes 1769480 | tf_op jit(solution)/shard_map/gather/ppermute | solution.py:588
  38.1 0.0 copy-done.9
  38.1 1.6 %collective-permute-done.far_ref = f32[32,9,4,128]{3,2,1,0:T(4,128)S(1)} collective-permute-done((f32[32,9,4,128]{3,2,1,0:T(4,128)S(1)}, f32[32,9,4,128]{3,2,1,0:T(4,128)S(1)}, u32[]{:S(2)}, u32[]{:S(2)}) %collective-permute-start) | collective-permute-done | bytes 589856 | tf_op jit(solution)/shard_map/gather/ppermute | solution.py:588
  39.7 0.0 copy-done.6
  39.7 0.0 copy-done.7
  39.7 0.0 copy-done.8
  39.7 7.3 %render.1 = (f32[144,8,128]{2,1,0:T(8,128)S(1)}, f32[144,8,128]{2,1,0:T(8,128)S(1)}) custom-call(s32[1,2,4]{2,1,0:T(2,128)S(1)} %copy-done.6, s32[1,2]{1,0:T(1,128)S(1)} %copy-done.7, s32[1,2]{1,0:T(1,128)S(1)} %copy-done.8, bf16[1,2,3,256]{3,2,1,0:T(4,128)(2,1)S(1)} %copy.15.target_ref, f32[32,9,4,128]{3,2,1,0:T(4,128)S(1)} %all_to_all.20.near_ref, ...), custom_call_target="tpu_custom_call" | custom-call | tf_op jit(solution)/shard_map/render/render/pallas_call | solution.py:590
  47.0 1.9 %collective-permute-start.1 = (f32[144,8,128]{2,1,0:T(8,128)S(1)}, f32[144,8,128]{2,1,0:T(8,128)S(1)}, u32[]{:S(2)}, u32[]{:S(2)}) collective-permute-start(f32[144,8,128]{2,1,0:T(8,128)S(1)} %get-tuple-element.14), channel_id=1, source_target_pairs={{0,8},{8,0},{16,24},{24,16},{32,40},{40,32},{48,56},{56,48},{64,72... | collective-permute-start | bytes 1769480 | tf_op jit(solution)/shard_map/scatter/ppermute | solution.py:600
  49.0 2.0 %collective-permute-done.1 = f32[144,8,128]{2,1,0:T(8,128)S(1)} collective-permute-done((f32[144,8,128]{2,1,0:T(8,128)S(1)}, f32[144,8,128]{2,1,0:T(8,128)S(1)}, u32[]{:S(2)}, u32[]{:S(2)}) %collective-permute-start.1) | collective-permute-done | bytes 589856 | tf_op jit(solution)/shard_map/scatter/ppermute | solution.py:600
  50.9 0.9 add.6
  51.8 5.2 %all-to-all-start.1 = ((f32[32,9,4,128]{3,2,1,0:T(4,128)}), f32[32,9,4,128]{3,2,1,0:T(4,128)S(1)}, u32[]{:S(2)}, u32[]{:S(2)}) async-start(f32[32,9,4,128]{3,2,1,0:T(4,128)} %bitcast.1), calls=%async_computation.1 | async-start | bytes 1179648 | tf_op jit(solution)/shard_map/scatter/all_to_all | solution.py:601
  57.0 0.0 copy-done.1
  57.1 1.2 %slope.1.refs_3_ = f32[6,9,4,128]{3,2,1,0:T(4,128)S(1)} custom-call(s32[1,2]{1,0:T(1,128)S(1)} %copy-done.4, f32[1,6]{1,0:T(1,128)S(1)} %copy-done.5, f32[59,8,256]{2,1,0:T(8,128)S(1)} %bitcast.13), custom_call_target="tpu_custom_call" | custom-call | flops 4000000 | bytes 200000 | tf_op jit(solution)/shard_map/project/slope/pallas_call | solution.py:575
  58.2 14.3 %all-to-all-done.1 = f32[32,9,4,128]{3,2,1,0:T(4,128)S(1)} async-done(((f32[32,9,4,128]{3,2,1,0:T(4,128)}), f32[32,9,4,128]{3,2,1,0:T(4,128)S(1)}, u32[]{:S(2)}, u32[]{:S(2)}) %all-to-all-start.1) | async-done | bytes 589856 | tf_op jit(solution)/shard_map/scatter/all_to_all | solution.py:601
  72.6 1.3 %collect.1 = (f32[8,11,4,128]{3,2,1,0:T(4,128)}, f32[1,1,128]{2,1,0:T(1,128)S(1)}) custom-call(s32[1,2]{1,0:T(1,128)S(1)} %copy-done.4, f32[1,6]{1,0:T(1,128)S(1)} %copy-done.5, f32[144,8,128]{2,1,0:T(8,128)S(1)} %bitcast.15, f32[6,9,4,128]{3,2,1,0:T(4,128)S(1)} %slope.1.refs_3_), custom_call_target="tpu_custom_call" | custom-call | tf_op jit(solution)/shard_map/collect/collect/pallas_call | solution.py:604
  73.9 6.5 %all-to-all-start.2 = ((f32[8,11,4,128]{3,2,1,0:T(4,128)}), f32[8,11,4,128]{3,2,1,0:T(4,128)S(1)}, u32[]{:S(2)}, u32[]{:S(2)}) async-start(f32[8,11,4,128]{3,2,1,0:T(4,128)} %get-tuple-element.15), calls=%async_computation.2 | async-start | bytes 360448 | tf_op jit(solution)/shard_map/collect/all_to_all | solution.py:615
  80.4 5.6 %collective-permute-start.2 = (f32[1,1,128]{2,1,0:T(1,128)S(1)}, f32[1,1,128]{2,1,0:T(1,128)S(1)}, u32[]{:S(2)}, u32[]{:S(2)}) collective-permute-start(f32[1,1,128]{2,1,0:T(1,128)S(1)} %get-tuple-element.16), channel_id=1, source_target_pairs={{0,8},{8,0},{16,24},{24,16},{32,40},{40,32},{48,56},{56,48},{64,72... | collective-permute-start | bytes 1544 | tf_op jit(solution)/shard_map/camera/ppermute | solution.py:617
  86.0 0.8 collective-permute-done.2
  86.8 2.2 %all-to-all-done.2.refs_0_ = f32[8,11,4,128]{3,2,1,0:T(4,128)S(1)} async-done(((f32[8,11,4,128]{3,2,1,0:T(4,128)}), f32[8,11,4,128]{3,2,1,0:T(4,128)S(1)}, u32[]{:S(2)}, u32[]{:S(2)}) %all-to-all-start.2) | async-done | bytes 180256 | tf_op jit(solution)/shard_map/collect/all_to_all | solution.py:615
  89.0 0.6 broadcast_in_dim.8
  89.6 8.1 %all-to-all-start.3 = ((f32[32,1,128]{2,1,0:T(1,128)}), f32[32,1,128]{2,1,0:T(1,128)S(1)}, u32[]{:S(2)}, u32[]{:S(2)}) async-start(f32[32,1,128]{2,1,0:T(1,128)} %broadcast_in_dim.8), calls=%async_computation.3 | async-start | bytes 32768 | tf_op jit(solution)/shard_map/camera/all_to_all | solution.py:619
  97.7 3.8 %update.1 = (f32[59,8,256]{2,1,0:T(8,128)}, f32[59,8,256]{2,1,0:T(8,128)}, f32[59,8,256]{2,1,0:T(8,128)}) custom-call(f32[8,11,4,128]{3,2,1,0:T(4,128)S(1)} %all-to-all-done.2.refs_0_, f32[59,8,256]{2,1,0:T(8,128)S(1)} %bitcast.14, f32[59,8,256]{2,1,0:T(8,128)S(1)} %bitcast.16, f32[59,8,256]{2,1,0:T(8,128)S(1)} %bitcast.17), custom_call_target="tpu_custom_call" | custom-call | tf_op jit(solution)/shard_map/update/update/pallas_call | solution.py:629
  101.5 4.8 %all-to-all-done.3 = f32[32,1,128]{2,1,0:T(1,128)S(1)} async-done(((f32[32,1,128]{2,1,0:T(1,128)}), f32[32,1,128]{2,1,0:T(1,128)S(1)}, u32[]{:S(2)}, u32[]{:S(2)}) %all-to-all-start.3) | async-done | bytes 16416 | tf_op jit(solution)/shard_map/camera/all_to_all | solution.py:619
  106.3 0.5 reduce_sum.11
  (11 shorter events, 0.0 us)
Async XLA Ops:
  0.6 0.7 copy-start.5
  0.6 0.7 copy-start.4
  1.3 1.0 copy-start
  3.1 35.0 %copy-start.9 = (bf16[1,2,3,256]{3,1,2,0:T(2,128)(2,1)S(1)}, bf16[1,2,3,256]{3,1,2,0:T(2,128)(2,1)}, u32[]{:S(2)}) copy-start(bf16[1,2,3,256]{3,1,2,0:T(2,128)(2,1)} %param.17) | copy-start | bytes 9220
  31.9 7.8 %copy-start.6 = (s32[1,2,4]{2,1,0:T(2,128)S(1)}, s32[1,2,4]{2,1,0:T(2,128)}, u32[]{:S(2)}) copy-start(s32[1,2,4]{2,1,0:T(2,128)} %order_ref.1) | copy-start | bytes 100
  31.9 7.8 %copy-start.7 = (s32[1,2]{1,0:T(1,128)S(1)}, s32[1,2]{1,0:T(1,128)}, u32[]{:S(2)}) copy-start(s32[1,2]{1,0:T(1,128)} %length_ref.1) | copy-start | bytes 28
  31.9 7.8 %copy-start.8 = (s32[1,2]{1,0:T(1,128)S(1)}, s32[1,2]{1,0:T(1,128)}, u32[]{:S(2)}) copy-start(s32[1,2]{1,0:T(1,128)} %tile_ref.1) | copy-start | bytes 28
  31.9 7.8 %collective-permute-start = (f32[32,9,4,128]{3,2,1,0:T(4,128)S(1)}, f32[32,9,4,128]{3,2,1,0:T(4,128)S(1)}, u32[]{:S(2)}, u32[]{:S(2)}) collective-permute-start(f32[32,9,4,128]{3,2,1,0:T(4,128)S(1)} %all_to_all.20.near_ref), channel_id=1, source_target_pairs={{0,8},{8,0},{16,24},{24,16},{32,40},{40,32},{48,56},{56,48},{64,72... | collective-permute-start | bytes 1769480 | tf_op jit(solution)/shard_map/gather/ppermute | solution.py:588
  47.0 3.9 %collective-permute-start.1 = (f32[144,8,128]{2,1,0:T(8,128)S(1)}, f32[144,8,128]{2,1,0:T(8,128)S(1)}, u32[]{:S(2)}, u32[]{:S(2)}) collective-permute-start(f32[144,8,128]{2,1,0:T(8,128)S(1)} %get-tuple-element.14), channel_id=1, source_target_pairs={{0,8},{8,0},{16,24},{24,16},{32,40},{40,32},{48,56},{56,48},{64,72... | collective-permute-start | bytes 1769480 | tf_op jit(solution)/shard_map/scatter/ppermute | solution.py:600
  51.8 5.2 %copy-start.1 = (f32[8,59,256]{2,0,1:T(8,128)S(1)}, f32[8,59,256]{2,0,1:T(8,128)}, u32[]{:S(2)}) copy-start(f32[8,59,256]{2,0,1:T(8,128)} %param.9) | copy-start | bytes 1449988
  51.8 20.8 %all-to-all-start.1 = ((f32[32,9,4,128]{3,2,1,0:T(4,128)}), f32[32,9,4,128]{3,2,1,0:T(4,128)S(1)}, u32[]{:S(2)}, u32[]{:S(2)}) async-start(f32[32,9,4,128]{3,2,1,0:T(4,128)} %bitcast.1), calls=%async_computation.1 | async-start | bytes 1179648 | tf_op jit(solution)/shard_map/scatter/all_to_all | solution.py:601
  72.6 25.1 %copy-start.2 = (f32[8,59,256]{2,0,1:T(8,128)S(1)}, f32[8,59,256]{2,0,1:T(8,128)}, u32[]{:S(2)}) copy-start(f32[8,59,256]{2,0,1:T(8,128)} %param.10) | copy-start | bytes 1449988
  72.6 25.1 %copy-start.3 = (f32[8,59,256]{2,0,1:T(8,128)S(1)}, f32[8,59,256]{2,0,1:T(8,128)}, u32[]{:S(2)}) copy-start(f32[8,59,256]{2,0,1:T(8,128)} %param.11) | copy-start | bytes 1449988
  73.9 15.1 %all-to-all-start.2 = ((f32[8,11,4,128]{3,2,1,0:T(4,128)}), f32[8,11,4,128]{3,2,1,0:T(4,128)S(1)}, u32[]{:S(2)}, u32[]{:S(2)}) async-start(f32[8,11,4,128]{3,2,1,0:T(4,128)} %get-tuple-element.15), calls=%async_computation.2 | async-start | bytes 360448 | tf_op jit(solution)/shard_map/collect/all_to_all | solution.py:615
  80.4 6.4 %collective-permute-start.2 = (f32[1,1,128]{2,1,0:T(1,128)S(1)}, f32[1,1,128]{2,1,0:T(1,128)S(1)}, u32[]{:S(2)}, u32[]{:S(2)}) collective-permute-start(f32[1,1,128]{2,1,0:T(1,128)S(1)} %get-tuple-element.16), channel_id=1, source_target_pairs={{0,8},{8,0},{16,24},{24,16},{32,40},{40,32},{48,56},{56,48},{64,72... | collective-permute-start | bytes 1544 | tf_op jit(solution)/shard_map/camera/ppermute | solution.py:617
  89.6 16.7 %all-to-all-start.3 = ((f32[32,1,128]{2,1,0:T(1,128)}), f32[32,1,128]{2,1,0:T(1,128)S(1)}, u32[]{:S(2)}, u32[]{:S(2)}) async-start(f32[32,1,128]{2,1,0:T(1,128)} %broadcast_in_dim.8), calls=%async_computation.3 | async-start | bytes 32768 | tf_op jit(solution)/shard_map/camera/all_to_all | solution.py:619

commit v4 on v3

--- a/solution.py
+++ b/solution.py
@@ -15,7 +15,7 @@
 FEATURES = 9
 CORES = 2
 ROWS = 4
-VIEW_MSG = 11
+VIEW_MSG = 10
 LOG2E = 1.4426950408889634
 F32 = jnp.float32
 BF16 = jnp.bfloat16
@@ -176,9 +176,50 @@
     return [jnp.full((1, LANES), camera_ref[0, i], F32) for i in range(6)]
 
 
-def project_kernel(focal, visible_ref, camera_ref, gauss_ref, out_ref):
+def project_kernel(
+    focal,
+    visible_any,
+    camera_any,
+    gauss_any,
+    out_ref,
+    extra_ref,
+    visible_ref,
+    camera_ref,
+    gauss_ref,
+    small_done,
+    large_done,
+):
+    small = [
+        pltpu.make_async_copy(visible_any, visible_ref, small_done.at[0]),
+        pltpu.make_async_copy(camera_any, camera_ref, small_done.at[1]),
+    ]
+    cuts = [0, 11, 27, 43, 59]
+    large = [
+        pltpu.make_async_copy(
+            gauss_any.at[low:high], gauss_ref.at[low:high], large_done.at[i]
+        )
+        for i, (low, high) in enumerate(zip(cuts[:-1], cuts[1:]))
+    ]
+    for copy in small + large:
+        copy.start()
+    for copy in small:
+        copy.wait()
+    owned = gauss_ref.shape[1]
+    base = lax.axis_index("cell") * owned
+    values = [camera_ref[0, i] for i in range(6)] + [
+        (visible_ref[0, sub] - base).astype(F32) for sub in range(2)
+    ]
+    row = lax.broadcasted_iota(jnp.int32, (ROWS, LANES), 0)
+    lane = lax.broadcasted_iota(jnp.int32, (ROWS, LANES), 1)
+    place = row + jnp.where(lane < LANES // 2, 0, ROWS)
+    extra = jnp.zeros((ROWS, LANES), F32)
+    for i, value in enumerate(values):
+        extra = jnp.where(place == i, value, extra)
+    extra_ref[...] = extra
+    for copy in large:
+        copy.wait()
     features = features_of(halves_of(gauss_ref), camera_rows(camera_ref), focal)
-    picked = pick(visible_ref, gauss_ref.shape[1])
+    picked = pick(visible_ref, owned)
     for f in range(FEATURES):
         out_ref[0, f] = jnp.concatenate(picked(features[f]), axis=0)
     message = out_ref[0]
@@ -233,8 +274,10 @@
     target_ref,
     near_ref,
     far_ref,
+    extra_ref,
     near_out,
     far_out,
+    extra_out,
     feature_scr,
     rgb_scr,
     weight_scr,
@@ -242,8 +285,9 @@
     low_scr,
     ratio_scr,
 ):
-    slots = order_ref.shape[1]
+    slots, depth = order_ref.shape[1], order_ref.shape[2]
     core = lax.rem(lax.axis_index("cell"), CORES)
+    extra_out[...] = extra_ref[...]
     near_out[...] = jnp.zeros_like(near_out)
     far_out[...] = jnp.zeros_like(far_out)
     first = lax.broadcasted_iota(jnp.int32, (BLOCK, BLOCK), 0)
@@ -263,8 +307,6 @@
                 (lax.div(tile, 16) * TILE + 8).astype(F32),
             )
         )
-    longest = functools.reduce(jnp.maximum, [length_ref[0, slot] for slot in range(slots)])
-
     def owner(slot, k):
         block = order_ref[0, slot, k]
         on_near = lax.rem(lax.div(block, 2), CORES) == core
@@ -317,9 +359,10 @@
         return tuple(new_remains), tuple(new_colours)
 
     zero = (jnp.zeros((PIX, 1), F32),) * slots
-    _, colours = lax.fori_loop(
-        0, longest, forward, (zero, (jnp.zeros((16, PIX), F32),) * slots)
-    )
+    carry = (zero, (jnp.zeros((16, PIX), F32),) * slots)
+    for k in range(depth):
+        carry = forward(k, carry)
+    colours = carry[1]
     misfit_rows, misfit_cols = [], []
     for slot in range(slots):
         misfit = colours[slot][0:3] + colours[slot][3:6] - targets[0, slot]
@@ -328,7 +371,7 @@
         misfit_cols.append([turned[:, c : c + 1] for c in range(3)])
 
     def backward(step, behind):
-        k = longest - 1 - step
+        k = depth - 1 - step
         throughs = []
         for slot in range(slots):
             feature = feature_scr.at[slot, k]
@@ -391,19 +434,15 @@
                     )
                 )
 
-            @pl.when(on_near)
-            def _():
-                for f in range(FEATURES):
-                    near_out[spots[f]] += placed[f]
-
-            @pl.when(jnp.logical_not(on_near))
-            def _():
-                for f in range(FEATURES):
-                    far_out[spots[f]] += placed[f]
+            for f in range(FEATURES):
+                near_out[spots[f]] += jnp.where(on_near, placed[f], 0.0)
+                far_out[spots[f]] += jnp.where(on_near, 0.0, placed[f])
 
         return tuple(new_behind)
 
-    lax.fori_loop(0, longest, backward, zero)
+    carry = zero
+    for k in range(depth):
+        carry = backward(k, carry)
 
 
 def render_scratch(slots, depth):
@@ -417,32 +456,29 @@
     ]
 
 
-def collect_kernel(owned, visible_ref, camera_ref, parts_ref, slope_ref, out_ref, camera_out):
-    base = lax.axis_index("cell") * owned
+def collect_kernel(parts_ref, extra_ref, out_ref):
     paired = parts_ref[0:FEATURES]
     for i in range(1, parts_ref.shape[0] // FEATURES):
         paired = paired + parts_ref[i * FEATURES : (i + 1) * FEATURES]
     pieces = [paired[i // 2, (i % 2) * ROWS : (i % 2 + 1) * ROWS] for i in range(2 * FEATURES)]
-    total = [pieces[f] + pieces[FEATURES + f] for f in range(FEATURES)]
     for f in range(FEATURES):
-        out_ref[0, f] = total[f]
-    base_rows = [jnp.full((1, LANES), camera_ref[0, i], F32) for i in range(6)] + [
-        jnp.full((1, LANES), (visible_ref[0, sub] - base).astype(F32), F32) for sub in range(2)
-    ]
-    for i in range(2):
-        out_ref[0, FEATURES + i] = jnp.concatenate(base_rows[4 * i : 4 * i + 4], axis=0)
+        out_ref[0, f] = pieces[f] + pieces[FEATURES + f]
+    out_ref[0, FEATURES] = extra_ref[...]
     message = out_ref[0]
     for i in range(1, out_ref.shape[0]):
         out_ref[i] = message
+
+
+def pose_kernel(own_ref, slope_ref, out_ref):
     lane = lax.broadcasted_iota(jnp.int32, (1, LANES), 1)
     packed = jnp.zeros((1, LANES), F32)
     for i in range(6):
         across = jnp.sum(
-            sum(total[f] * slope_ref[i, f] for f in range(FEATURES)), axis=0, keepdims=True
+            sum(own_ref[0, f] * slope_ref[i, f] for f in range(FEATURES)), axis=0, keepdims=True
         )
         packed = packed + jnp.where(lane == i, jnp.sum(across, axis=1, keepdims=True), 0.0)
-    for i in range(camera_out.shape[0]):
-        camera_out[i] = packed
+    for i in range(out_ref.shape[0]):
+        out_ref[i] = packed
 
 
 def update_kernel(
@@ -480,7 +516,11 @@
             def message(f, r):
                 return parts_ref[view, f, r : r + 1, :]
 
-            masks = [place == message(FEATURES + 1, 2 + sub) for sub in range(2)]
+            def extra(i):
+                at = i // ROWS * (LANES // 2)
+                return jnp.broadcast_to(message(FEATURES, i % ROWS)[:, at : at + 1], (1, LANES))
+
+            masks = [place == extra(6 + sub) for sub in range(2)]
             screen = [
                 sum(
                     jnp.where(masks[sub], message(f, sub * 2 + half), 0.0)
@@ -490,7 +530,7 @@
             ]
             frame = [
                 jnp.broadcast_to(entry, whole)
-                for entry in camera_frame([message(FEATURES + i // 4, i % 4) for i in range(6)])
+                for entry in camera_frame([extra(i) for i in range(6)])
             ]
             seen, pull = jax.vjp(
                 lambda centers, factor: view_of(centers, factor, frame, *focal),
@@ -564,12 +604,22 @@
     swap = [(cell, cell ^ 1) for cell in range(cells)]
 
     with jax.named_scope("project"):
-        message = pl.pallas_call(
+        message, extra = pl.pallas_call(
             lambda *refs: project_kernel(focal, *refs),
-            out_shape=jax.ShapeDtypeStruct((chips, FEATURES, ROWS, LANES), F32),
-            in_specs=[SMEM, SMEM, VMEM],
-            out_specs=VMEM,
-            compiler_params=PARAMETERS,
+            out_shape=[
+                jax.ShapeDtypeStruct((chips, FEATURES, ROWS, LANES), F32),
+                jax.ShapeDtypeStruct((ROWS, LANES), F32),
+            ],
+            in_specs=[pl.BlockSpec(memory_space=pl.ANY)] * 3,
+            out_specs=[VMEM, VMEM],
+            scratch_shapes=[
+                pltpu.SMEM(visible_blocks.shape, jnp.int32),
+                pltpu.SMEM(cameras.shape, F32),
+                pltpu.VMEM(gaussians.shape, F32),
+                pltpu.SemaphoreType.DMA((2,)),
+                pltpu.SemaphoreType.DMA((4,)),
+            ],
+            compiler_params=pltpu.CompilerParams(vmem_limit_bytes=60 * 1024 * 1024),
             name="project",
         )(visible_blocks, cameras, gaussians)
         slopes = pl.pallas_call(
@@ -587,42 +637,47 @@
         near = lax.all_to_all(message, "cell", 0, 0, axis_index_groups=same_core, tiled=True)
         far = lax.ppermute(near, "cell", swap)
     with jax.named_scope("render"):
-        near_grad, far_grad = pl.pallas_call(
+        pairs = jax.ShapeDtypeStruct((chips * FEATURES * ROWS // 8, 8, LANES), F32)
+        near_grad, far_grad, extra = pl.pallas_call(
             render_kernel,
-            out_shape=[jax.ShapeDtypeStruct((chips * FEATURES * ROWS // 8, 8, LANES), F32)] * 2,
-            in_specs=[SMEM, SMEM, SMEM, VMEM, VMEM, VMEM],
-            out_specs=[VMEM, VMEM],
+            out_shape=[pairs, pairs, jax.ShapeDtypeStruct(extra.shape, F32)],
+            in_specs=[SMEM, SMEM, SMEM, VMEM, VMEM, VMEM, VMEM],
+            out_specs=[VMEM, VMEM, VMEM],
             scratch_shapes=render_scratch(*tile_order.shape[1:]),
             compiler_params=PARAMETERS,
             name="render",
-        )(tile_order, tile_length, tile_ids, targets, near, far)
+        )(tile_order, tile_length, tile_ids, targets, near, far, extra)
     with jax.named_scope("scatter"):
         pair = near_grad + lax.ppermute(far_grad, "cell", swap)
         parts = lax.all_to_all(
             pair.reshape(near.shape), "cell", 0, 0, axis_index_groups=same_core, tiled=True)
     with jax.named_scope("collect"):
-        own, camera_part = pl.pallas_call(
-            lambda *refs: collect_kernel(owned, *refs),
-            out_shape=[
-                jax.ShapeDtypeStruct((views, VIEW_MSG, ROWS, LANES), F32),
-                jax.ShapeDtypeStruct((1, 1, LANES), F32),
-            ],
-            in_specs=[SMEM, SMEM, VMEM, VMEM],
-            out_specs=[VMEM, VMEM],
+        own = pl.pallas_call(
+            collect_kernel,
+            out_shape=jax.ShapeDtypeStruct((views, VIEW_MSG, ROWS, LANES), F32),
+            in_specs=[VMEM, VMEM],
+            out_specs=VMEM,
             compiler_params=PARAMETERS,
             name="collect",
-        )(visible_blocks, cameras, parts.reshape(pair.shape), slopes)
+        )(parts.reshape(pair.shape), extra)
         every = lax.all_to_all(own, "view", 0, 0, tiled=True)
     with jax.named_scope("camera"):
+        camera_part = pl.pallas_call(
+            pose_kernel,
+            out_shape=jax.ShapeDtypeStruct((1, 1, LANES), F32),
+            in_specs=[VMEM, VMEM],
+            out_specs=VMEM,
+            compiler_params=PARAMETERS,
+            cost_estimate=pl.CostEstimate(
+                flops=100_000, bytes_accessed=250_000, transcendentals=0
+            ),
+            name="pose",
+        )(own, slopes)
         camera_pair = camera_part + lax.ppermute(camera_part, "cell", swap)
-        every, camera_pair = lax.optimization_barrier((every, camera_pair))
+        camera_copies = jnp.broadcast_to(camera_pair, (chips, 1, LANES))
+        every, camera_copies = lax.optimization_barrier((every, camera_copies))
         camera_parts = lax.all_to_all(
-            jnp.broadcast_to(camera_pair, (chips, 1, LANES)),
-            "cell",
-            0,
-            0,
-            axis_index_groups=same_core,
-            tiled=True,
+            camera_copies, "cell", 0, 0, axis_index_groups=same_core, tiled=True
         )
     with jax.named_scope("update"):
         state = jax.ShapeDtypeStruct(gaussians.shape, F32)

time: 109 us -> 105 us (0.963)
  blocking collectives: 28.8 us -> 49.5 us
  waiting for transfers between devices: 25.7 us -> 7.47 us
  starting transfers between devices: 33.5 us -> 28.5 us
  local copies, waits for them, and re-layouts: 2.32 us -> 0.67 us
    all_to_all x0 -> x1, blocking collectives: none -> 20.5 us  [shards(): lax.all_to_all(pair.reshape(near.shape), 'cell', 0, 0, axis_index_groups=...]
    all_to_all x2 -> x1, waiting for transfers between devices: 19.2 us -> 3.52 us  [shards(): lax.all_to_all(camera_copies, 'cell', 0, 0, axis_index_groups=same_core,...]
    all_to_all x2 -> x1, starting transfers between devices: 13.3 us -> 7.71 us  [shards(): lax.all_to_all(camera_copies, 'cell', 0, 0, axis_index_groups=same_core,...]
    all_to_all x1, waiting for transfers between devices: 2.16 us -> 0.01 us  [shards(): every = lax.all_to_all(own, 'view', 0, 0, tiled=True)]
    unnamed x21, local copies, waits for them, and re-layouts: 1.72 us -> 0.06 us
    pallas_call x1, Pallas kernels: 3.78 us -> 5.09 us  [shards(): pl.pallas_call(lambda *refs: update_kernel(focal, *refs), out_shape=[stat...]
    pallas_call x3 -> x4, Pallas kernels: 9.39 us -> 9.13 us  [the longest x1 5.21 us: shards(): pl.pallas_call(render_kernel, out_shape=[pairs, pairs, jax.ShapeDtypeStru...]
  transfers between devices with their start and end apart: 6 -> 5, of which waited for: 6 -> 4; matrix products, arithmetic and copies ran while one was open for 0% -> 0% of each run, Pallas kernels for 5% -> 7%
where the time goes in v4:
time: 105 us; the launch traced here: 103 us
  blocking collectives  49.5 us (47%)
  starting transfers between devices  28.5 us (27%)
  Pallas kernels  15.4 us (15%)
  waiting for transfers between devices  7.47 us (7%)
    all_to_all x1, blocking collectives, shards(): lax.all_to_all(message, 'cell', 0, 0, axis_index_groups=same_core, tiled=...  29 us
    all_to_all x1, blocking collectives, shards(): lax.all_to_all(pair.reshape(near.shape), 'cell', 0, 0, axis_index_groups=...  20.5 us
    all_to_all x1, starting transfers between devices, shards(): lax.all_to_all(camera_copies, 'cell', 0, 0, axis_index_groups=same_core,...  7.71 us
    all_to_all x1, starting transfers between devices, shards(): every = lax.all_to_all(own, 'view', 0, 0, tiled=True)  6.93 us
    ppermute x1, starting transfers between devices, shards(): far = lax.ppermute(near, 'cell', swap)  6.03 us
    ppermute x1, starting transfers between devices, shards(): camera_pair = camera_part + lax.ppermute(camera_part, 'cell', swap)  5.59 us
    pallas_call x1, Pallas kernels, shards(): pl.pallas_call(render_kernel, out_shape=[pairs, pairs, jax.ShapeDtypeStru...  5.21 us
    pallas_call x1, Pallas kernels, shards(): pl.pallas_call(lambda *refs: update_kernel(focal, *refs), out_shape=[stat...  5.09 us
  transfers between devices with their start and end apart: 5, of which 4 were waited for; matrix products, arithmetic and copies ran while one was open for 0% of the time, Pallas kernels for 7%

profile of v4, /device:TPU:1, one launch (start us, length us, event | category | flops | bytes accessed | tf_op | source)
XLA Modules:
  0.0 103.0 jit_solution(11443350616840589991)
XLA Ops:
  0.6 2.2 %project.1 = (f32[32,9,4,128]{3,2,1,0:T(4,128)}, f32[4,128]{1,0:T(4,128)}) custom-call(s32[1,2]{1,0:T(1,128)} %refs_0_.3, f32[1,6]{1,0:T(1,128)} %refs_1_.3, f32[59,8,256]{2,1,0:T(8,128)} %bitcast.13), custom_call_target="tpu_custom_call" | custom-call | tf_op jit(solution)/shard_map/project/project/pallas_call | solution.py:607
  2.8 0.0 copy-start.9
  2.8 29.0 %all_to_all.20.near_ref = f32[32,9,4,128]{3,2,1,0:T(4,128)S(1)} all-to-all(f32[32,9,4,128]{3,2,1,0:T(4,128)} %get-tuple-element.14), channel_id=1, replica_groups={{0,16,32,48,64,80,96,112,128,144,160,176,192,208,224,240,256,272,288,30..., dimensions={0} | all-to-all | bytes 1179648 | tf_op jit(solution)/shard_map/gather/all_to_all | solution.py:637
  31.8 6.0 %collective-permute-start = (f32[32,9,4,128]{3,2,1,0:T(4,128)S(1)}, f32[32,9,4,128]{3,2,1,0:T(4,128)S(1)}, u32[]{:S(2)}, u32[]{:S(2)}) collective-permute-start(f32[32,9,4,128]{3,2,1,0:T(4,128)S(1)} %all_to_all.20.near_ref), channel_id=1, source_target_pairs={{0,8},{8,0},{16,24},{24,16},{32,40},{40,32},{48,56},{56,48},{64,72... | collective-permute-start | bytes 1769480 | tf_op jit(solution)/shard_map/gather/ppermute | solution.py:638
  37.9 0.0 copy-done.9
  37.9 0.0 copy-start.3
  37.9 0.0 copy-start.8
  37.9 0.0 copy-start.6
  37.9 0.0 copy-start.7
  37.9 1.5 %collective-permute-done.far_ref = f32[32,9,4,128]{3,2,1,0:T(4,128)S(1)} collective-permute-done((f32[32,9,4,128]{3,2,1,0:T(4,128)S(1)}, f32[32,9,4,128]{3,2,1,0:T(4,128)S(1)}, u32[]{:S(2)}, u32[]{:S(2)}) %collective-permute-start) | collective-permute-done | bytes 589856 | tf_op jit(solution)/shard_map/gather/ppermute | solution.py:638
  39.5 0.0 copy-done.3
  39.5 0.0 copy-done.8
  39.5 0.0 copy-done.6
  39.5 0.0 copy-done.7
  39.5 5.2 %render.1 = (f32[144,8,128]{2,1,0:T(8,128)S(1)}, f32[144,8,128]{2,1,0:T(8,128)S(1)}, f32[4,128]{1,0:T(4,128)S(1)}) custom-call(s32[1,2,4]{2,1,0:T(2,128)S(1)} %copy-done.6, s32[1,2]{1,0:T(1,128)S(1)} %copy-done.7, s32[1,2]{1,0:T(1,128)S(1)} %copy-done.8, bf16[1,2,3,256]{3,2,1,0:T(4,128)(2,1)S(1)} %copy.15.target_ref, ...), custom_call_target="tpu_custom_call" | custom-call | tf_op jit(solution)/shard_map/render/render/pallas_call | solution.py:641
  44.7 2.3 %collective-permute-start.1 = (f32[144,8,128]{2,1,0:T(8,128)S(1)}, f32[144,8,128]{2,1,0:T(8,128)S(1)}, u32[]{:S(2)}, u32[]{:S(2)}) collective-permute-start(f32[144,8,128]{2,1,0:T(8,128)S(1)} %get-tuple-element.17), channel_id=1, source_target_pairs={{0,8},{8,0},{16,24},{24,16},{32,40},{40,32},{48,56},{56,48},{64,72... | collective-permute-start | bytes 1769480 | tf_op jit(solution)/shard_map/scatter/ppermute | solution.py:651
  47.0 1.6 %collective-permute-done.1 = f32[144,8,128]{2,1,0:T(8,128)S(1)} collective-permute-done((f32[144,8,128]{2,1,0:T(8,128)S(1)}, f32[144,8,128]{2,1,0:T(8,128)S(1)}, u32[]{:S(2)}, u32[]{:S(2)}) %collective-permute-start.1) | collective-permute-done | bytes 589856 | tf_op jit(solution)/shard_map/scatter/ppermute | solution.py:651
  48.6 0.1 add.6
  48.7 20.5 %all_to_all.21 = f32[32,9,4,128]{3,2,1,0:T(4,128)S(1)} all-to-all(f32[32,9,4,128]{3,2,1,0:T(4,128)S(1)} %bitcast.19), channel_id=1, replica_groups={{0,16,32,48,64,80,96,112,128,144,160,176,192,208,224,240,256,272,288,30..., dimensions={0} | all-to-all | bytes 1179648 | tf_op jit(solution)/shard_map/scatter/all_to_all | solution.py:652
  69.2 0.7 collect.1.own_ref
  69.9 6.9 %all-to-all-start.2 = ((f32[8,10,4,128]{3,2,1,0:T(4,128)}), f32[8,10,4,128]{3,2,1,0:T(4,128)S(1)}, u32[]{:S(2)}, u32[]{:S(2)}) async-start(f32[8,10,4,128]{3,2,1,0:T(4,128)} %collect.1.own_ref), calls=%async_computation.2 | async-start | bytes 327680 | tf_op jit(solution)/shard_map/collect/all_to_all | solution.py:663
  76.9 0.0 copy-start.1
  76.9 1.2 %slope.1.slope_ref = f32[6,9,4,128]{3,2,1,0:T(4,128)S(1)} custom-call(s32[1,2]{1,0:T(1,128)S(1)} %copy-done.4, f32[1,6]{1,0:T(1,128)S(1)} %copy-done.5, f32[59,8,256]{2,1,0:T(8,128)S(1)} %bitcast.14), custom_call_target="tpu_custom_call" | custom-call | flops 4000000 | bytes 200000 | tf_op jit(solution)/shard_map/project/slope/pallas_call | solution.py:625
  78.1 1.0 pose.1
  79.1 5.6 %collective-permute-start.2 = (f32[1,1,128]{2,1,0:T(1,128)S(1)}, f32[1,1,128]{2,1,0:T(1,128)S(1)}, u32[]{:S(2)}, u32[]{:S(2)}) collective-permute-start(f32[1,1,128]{2,1,0:T(1,128)S(1)} %pose.1), channel_id=1, source_target_pairs={{0,8},{8,0},{16,24},{24,16},{32,40},{40,32},{48,56},{56,48},{64,72... | collective-permute-start | bytes 1544 | tf_op jit(solution)/shard_map/camera/ppermute | solution.py:676
  84.7 0.8 collective-permute-done.2
  85.5 0.0 all-to-all-done.2.refs_0_
  85.5 0.6 broadcast_in_dim.8
  86.1 7.7 %all-to-all-start.3 = ((f32[32,1,128]{2,1,0:T(1,128)}), f32[32,1,128]{2,1,0:T(1,128)S(1)}, u32[]{:S(2)}, u32[]{:S(2)}) async-start(f32[32,1,128]{2,1,0:T(1,128)} %broadcast_in_dim.8), calls=%async_computation.3 | async-start | bytes 32768 | tf_op jit(solution)/shard_map/camera/all_to_all | solution.py:679
  93.8 5.1 %update.1 = (f32[59,8,256]{2,1,0:T(8,128)}, f32[59,8,256]{2,1,0:T(8,128)}, f32[59,8,256]{2,1,0:T(8,128)}) custom-call(f32[8,10,4,128]{3,2,1,0:T(4,128)S(1)} %all-to-all-done.2.refs_0_, f32[59,8,256]{2,1,0:T(8,128)S(1)} %bitcast.15, f32[59,8,256]{2,1,0:T(8,128)S(1)} %bitcast.17, f32[59,8,256]{2,1,0:T(8,128)S(1)} %bitcast.18), custom_call_target="tpu_custom_call" | custom-call | tf_op jit(solution)/shard_map/update/update/pallas_call | solution.py:684
  98.9 3.5 %all-to-all-done.3 = f32[32,1,128]{2,1,0:T(1,128)S(1)} async-done(((f32[32,1,128]{2,1,0:T(1,128)}), f32[32,1,128]{2,1,0:T(1,128)S(1)}, u32[]{:S(2)}, u32[]{:S(2)}) %all-to-all-start.3) | async-done | bytes 16416 | tf_op jit(solution)/shard_map/camera/all_to_all | solution.py:679
  102.5 0.5 reduce_sum.11
  (11 shorter events, 0.0 us)
Async XLA Ops:
  2.8 35.1 %copy-start.9 = (bf16[1,2,3,256]{3,1,2,0:T(2,128)(2,1)S(1)}, bf16[1,2,3,256]{3,1,2,0:T(2,128)(2,1)}, u32[]{:S(2)}) copy-start(bf16[1,2,3,256]{3,1,2,0:T(2,128)(2,1)} %param.17) | copy-start | bytes 9220
  31.8 7.6 %collective-permute-start = (f32[32,9,4,128]{3,2,1,0:T(4,128)S(1)}, f32[32,9,4,128]{3,2,1,0:T(4,128)S(1)}, u32[]{:S(2)}, u32[]{:S(2)}) collective-permute-start(f32[32,9,4,128]{3,2,1,0:T(4,128)S(1)} %all_to_all.20.near_ref), channel_id=1, source_target_pairs={{0,8},{8,0},{16,24},{24,16},{32,40},{40,32},{48,56},{56,48},{64,72... | collective-permute-start | bytes 1769480 | tf_op jit(solution)/shard_map/gather/ppermute | solution.py:638
  37.9 1.6 %copy-start.3 = (f32[4,128]{1,0:T(4,128)S(1)}, f32[4,128]{1,0:T(4,128)}, u32[]{:S(2)}) copy-start(f32[4,128]{1,0:T(4,128)} %get-tuple-element.15.extra_ref) | copy-start | bytes 6148
  37.9 1.6 %copy-start.8 = (s32[1,2]{1,0:T(1,128)S(1)}, s32[1,2]{1,0:T(1,128)}, u32[]{:S(2)}) copy-start(s32[1,2]{1,0:T(1,128)} %tile_ref.1) | copy-start | bytes 28
  37.9 1.6 %copy-start.6 = (s32[1,2,4]{2,1,0:T(2,128)S(1)}, s32[1,2,4]{2,1,0:T(2,128)}, u32[]{:S(2)}) copy-start(s32[1,2,4]{2,1,0:T(2,128)} %order_ref.1) | copy-start | bytes 100
  37.9 1.6 %copy-start.7 = (s32[1,2]{1,0:T(1,128)S(1)}, s32[1,2]{1,0:T(1,128)}, u32[]{:S(2)}) copy-start(s32[1,2]{1,0:T(1,128)} %length_ref.1) | copy-start | bytes 28
  44.7 3.9 %collective-permute-start.1 = (f32[144,8,128]{2,1,0:T(8,128)S(1)}, f32[144,8,128]{2,1,0:T(8,128)S(1)}, u32[]{:S(2)}, u32[]{:S(2)}) collective-permute-start(f32[144,8,128]{2,1,0:T(8,128)S(1)} %get-tuple-element.17), channel_id=1, source_target_pairs={{0,8},{8,0},{16,24},{24,16},{32,40},{40,32},{48,56},{56,48},{64,72... | collective-permute-start | bytes 1769480 | tf_op jit(solution)/shard_map/scatter/ppermute | solution.py:651
  69.2 7.7 %copy-start = (f32[8,59,256]{2,0,1:T(8,128)S(1)}, f32[8,59,256]{2,0,1:T(8,128)}, u32[]{:S(2)}) copy-start(f32[8,59,256]{2,0,1:T(8,128)} %param.9) | copy-start | bytes 1449988
  69.2 7.7 %copy-start.4 = (s32[1,2]{1,0:T(1,128)S(1)}, s32[1,2]{1,0:T(1,128)}, u32[]{:S(2)}) copy-start(s32[1,2]{1,0:T(1,128)} %refs_0_.3) | copy-start | bytes 28
  69.2 7.7 %copy-start.5 = (f32[1,6]{1,0:T(1,128)S(1)}, f32[1,6]{1,0:T(1,128)}, u32[]{:S(2)}) copy-start(f32[1,6]{1,0:T(1,128)} %refs_1_.3) | copy-start | bytes 76
  69.9 23.9 %copy-start.2 = (f32[8,59,256]{2,0,1:T(8,128)S(1)}, f32[8,59,256]{2,0,1:T(8,128)}, u32[]{:S(2)}) copy-start(f32[8,59,256]{2,0,1:T(8,128)} %param.11) | copy-start | bytes 1449988
  69.9 15.6 %all-to-all-start.2 = ((f32[8,10,4,128]{3,2,1,0:T(4,128)}), f32[8,10,4,128]{3,2,1,0:T(4,128)S(1)}, u32[]{:S(2)}, u32[]{:S(2)}) async-start(f32[8,10,4,128]{3,2,1,0:T(4,128)} %collect.1.own_ref), calls=%async_computation.2 | async-start | bytes 327680 | tf_op jit(solution)/shard_map/collect/all_to_all | solution.py:663
  76.9 17.0 %copy-start.1 = (f32[8,59,256]{2,0,1:T(8,128)S(1)}, f32[8,59,256]{2,0,1:T(8,128)}, u32[]{:S(2)}) copy-start(f32[8,59,256]{2,0,1:T(8,128)} %param.10) | copy-start | bytes 1449988
  79.1 6.4 %collective-permute-start.2 = (f32[1,1,128]{2,1,0:T(1,128)S(1)}, f32[1,1,128]{2,1,0:T(1,128)S(1)}, u32[]{:S(2)}, u32[]{:S(2)}) collective-permute-start(f32[1,1,128]{2,1,0:T(1,128)S(1)} %pose.1), channel_id=1, source_target_pairs={{0,8},{8,0},{16,24},{24,16},{32,40},{40,32},{48,56},{56,48},{64,72... | collective-permute-start | bytes 1544 | tf_op jit(solution)/shard_map/camera/ppermute | solution.py:676
  86.1 16.4 %all-to-all-start.3 = ((f32[32,1,128]{2,1,0:T(1,128)}), f32[32,1,128]{2,1,0:T(1,128)S(1)}, u32[]{:S(2)}, u32[]{:S(2)}) async-start(f32[32,1,128]{2,1,0:T(1,128)} %broadcast_in_dim.8), calls=%async_computation.3 | async-start | bytes 32768 | tf_op jit(solution)/shard_map/camera/all_to_all | solution.py:679

commit v5 on v4

--- a/solution.py
+++ b/solution.py
@@ -664,7 +664,7 @@
     with jax.named_scope("camera"):
         camera_part = pl.pallas_call(
             pose_kernel,
-            out_shape=jax.ShapeDtypeStruct((1, 1, LANES), F32),
+            out_shape=jax.ShapeDtypeStruct((chips, 1, LANES), F32),
             in_specs=[VMEM, VMEM],
             out_specs=VMEM,
             compiler_params=PARAMETERS,
@@ -673,8 +673,7 @@
             ),
             name="pose",
         )(own, slopes)
-        camera_pair = camera_part + lax.ppermute(camera_part, "cell", swap)
-        camera_copies = jnp.broadcast_to(camera_pair, (chips, 1, LANES))
+        camera_copies = camera_part + lax.ppermute(camera_part, "cell", swap)
         every, camera_copies = lax.optimization_barrier((every, camera_copies))
         camera_parts = lax.all_to_all(
             camera_copies, "cell", 0, 0, axis_index_groups=same_core, tiled=True

time: 105 us -> 104 us (level)
  transfers between devices with their start and end apart: 5 -> 5, of which waited for: 4 -> 4; matrix products, arithmetic and copies ran while one was open for 0% -> 1% of each run, Pallas kernels for 7% -> 7%
where the time goes in v5:
time: 104 us; the launch traced here: 102 us
  blocking collectives  49.5 us (48%)
  starting transfers between devices  27.9 us (27%)
  Pallas kernels  15.4 us (15%)
  waiting for transfers between devices  7.49 us (7%)
  other arithmetic  1.24 us (1%)
    all_to_all x1, blocking collectives, shards(): lax.all_to_all(message, 'cell', 0, 0, axis_index_groups=same_core, tiled=...  29 us
    all_to_all x1, blocking collectives, shards(): lax.all_to_all(pair.reshape(near.shape), 'cell', 0, 0, axis_index_groups=...  20.5 us
    all_to_all x1, starting transfers between devices, shards(): lax.all_to_all(camera_copies, 'cell', 0, 0, axis_index_groups=same_core,...  7.04 us
    all_to_all x1, starting transfers between devices, shards(): every = lax.all_to_all(own, 'view', 0, 0, tiled=True)  6.96 us
    ppermute x1, starting transfers between devices, shards(): far = lax.ppermute(near, 'cell', swap)  6.03 us
    ppermute x1, starting transfers between devices, shards(): camera_copies = camera_part + lax.ppermute(camera_part, 'cell', swap)  5.6 us
    pallas_call x1, Pallas kernels, shards(): pl.pallas_call(render_kernel, out_shape=[pairs, pairs, jax.ShapeDtypeStru...  5.2 us
    pallas_call x1, Pallas kernels, shards(): pl.pallas_call(lambda *refs: update_kernel(focal, *refs), out_shape=[stat...  5.09 us
  transfers between devices with their start and end apart: 5, of which 4 were waited for; matrix products, arithmetic and copies ran while one was open for 1% of the time, Pallas kernels for 7%

profile of v5, /device:TPU:1, one launch (start us, length us, event | category | flops | bytes accessed | tf_op | source)
XLA Modules:
  0.0 102.4 jit_solution(15319156880457254914)
XLA Ops:
  0.6 2.2 %project.1 = (f32[32,9,4,128]{3,2,1,0:T(4,128)}, f32[4,128]{1,0:T(4,128)}) custom-call(s32[1,2]{1,0:T(1,128)} %refs_0_.3, f32[1,6]{1,0:T(1,128)} %refs_1_.3, f32[59,8,256]{2,1,0:T(8,128)} %bitcast.10), custom_call_target="tpu_custom_call" | custom-call | tf_op jit(solution)/shard_map/project/project/pallas_call | solution.py:607
  2.8 0.0 copy-start.9
  2.8 29.0 %all_to_all.20.near_ref = f32[32,9,4,128]{3,2,1,0:T(4,128)S(1)} all-to-all(f32[32,9,4,128]{3,2,1,0:T(4,128)} %get-tuple-element.14), channel_id=1, replica_groups={{0,16,32,48,64,80,96,112,128,144,160,176,192,208,224,240,256,272,288,30..., dimensions={0} | all-to-all | bytes 1179648 | tf_op jit(solution)/shard_map/gather/all_to_all | solution.py:637
  31.8 6.0 %collective-permute-start = (f32[32,9,4,128]{3,2,1,0:T(4,128)S(1)}, f32[32,9,4,128]{3,2,1,0:T(4,128)S(1)}, u32[]{:S(2)}, u32[]{:S(2)}) collective-permute-start(f32[32,9,4,128]{3,2,1,0:T(4,128)S(1)} %all_to_all.20.near_ref), channel_id=1, source_target_pairs={{0,8},{8,0},{16,24},{24,16},{32,40},{40,32},{48,56},{56,48},{64,72... | collective-permute-start | bytes 1769480 | tf_op jit(solution)/shard_map/gather/ppermute | solution.py:638
  37.9 0.0 copy-done.9
  37.9 0.0 copy-start.3
  37.9 0.0 copy-start.8
  37.9 0.0 copy-start.6
  37.9 0.0 copy-start.7
  37.9 1.5 %collective-permute-done.far_ref = f32[32,9,4,128]{3,2,1,0:T(4,128)S(1)} collective-permute-done((f32[32,9,4,128]{3,2,1,0:T(4,128)S(1)}, f32[32,9,4,128]{3,2,1,0:T(4,128)S(1)}, u32[]{:S(2)}, u32[]{:S(2)}) %collective-permute-start) | collective-permute-done | bytes 589856 | tf_op jit(solution)/shard_map/gather/ppermute | solution.py:638
  39.5 0.0 copy-done.3
  39.5 0.0 copy-done.8
  39.5 0.0 copy-done.6
  39.5 5.2 %render.1 = (f32[144,8,128]{2,1,0:T(8,128)S(1)}, f32[144,8,128]{2,1,0:T(8,128)S(1)}, f32[4,128]{1,0:T(4,128)S(1)}) custom-call(s32[1,2,4]{2,1,0:T(2,128)S(1)} %copy-done.6, s32[1,2]{1,0:T(1,128)S(1)} %copy-done.7, s32[1,2]{1,0:T(1,128)S(1)} %copy-done.8, bf16[1,2,3,256]{3,2,1,0:T(4,128)(2,1)S(1)} %copy.13.target_ref, ...), custom_call_target="tpu_custom_call" | custom-call | tf_op jit(solution)/shard_map/render/render/pallas_call | solution.py:641
  44.7 2.3 %collective-permute-start.1 = (f32[144,8,128]{2,1,0:T(8,128)S(1)}, f32[144,8,128]{2,1,0:T(8,128)S(1)}, u32[]{:S(2)}, u32[]{:S(2)}) collective-permute-start(f32[144,8,128]{2,1,0:T(8,128)S(1)} %get-tuple-element.17), channel_id=1, source_target_pairs={{0,8},{8,0},{16,24},{24,16},{32,40},{40,32},{48,56},{56,48},{64,72... | collective-permute-start | bytes 1769480 | tf_op jit(solution)/shard_map/scatter/ppermute | solution.py:651
  47.0 1.6 %collective-permute-done.1 = f32[144,8,128]{2,1,0:T(8,128)S(1)} collective-permute-done((f32[144,8,128]{2,1,0:T(8,128)S(1)}, f32[144,8,128]{2,1,0:T(8,128)S(1)}, u32[]{:S(2)}, u32[]{:S(2)}) %collective-permute-start.1) | collective-permute-done | bytes 589856 | tf_op jit(solution)/shard_map/scatter/ppermute | solution.py:651
  48.6 0.1 add.6
  48.7 20.5 %all_to_all.21 = f32[32,9,4,128]{3,2,1,0:T(4,128)S(1)} all-to-all(f32[32,9,4,128]{3,2,1,0:T(4,128)S(1)} %bitcast.16), channel_id=1, replica_groups={{0,16,32,48,64,80,96,112,128,144,160,176,192,208,224,240,256,272,288,30..., dimensions={0} | all-to-all | bytes 1179648 | tf_op jit(solution)/shard_map/scatter/all_to_all | solution.py:652
  69.2 0.7 collect.1.own_ref
  69.9 7.0 %all-to-all-start.2 = ((f32[8,10,4,128]{3,2,1,0:T(4,128)}), f32[8,10,4,128]{3,2,1,0:T(4,128)S(1)}, u32[]{:S(2)}, u32[]{:S(2)}) async-start(f32[8,10,4,128]{3,2,1,0:T(4,128)} %collect.1.own_ref), calls=%async_computation.2 | async-start | bytes 327680 | tf_op jit(solution)/shard_map/collect/all_to_all | solution.py:663
  76.9 0.0 copy-start.1
  76.9 0.0 copy-start.2
  76.9 1.2 %slope.1.slope_ref = f32[6,9,4,128]{3,2,1,0:T(4,128)S(1)} custom-call(s32[1,2]{1,0:T(1,128)S(1)} %copy-done.4, f32[1,6]{1,0:T(1,128)S(1)} %copy-done.5, f32[59,8,256]{2,1,0:T(8,128)S(1)} %bitcast.11), custom_call_target="tpu_custom_call" | custom-call | flops 4000000 | bytes 200000 | tf_op jit(solution)/shard_map/project/slope/pallas_call | solution.py:625
  78.1 1.0 %pose.1 = f32[32,1,128]{2,1,0:T(1,128)S(1)} custom-call(f32[8,10,4,128]{3,2,1,0:T(4,128)} %collect.1.own_ref, f32[6,9,4,128]{3,2,1,0:T(4,128)S(1)} %slope.1.slope_ref), custom_call_target="tpu_custom_call" | custom-call | flops 100000 | bytes 250000 | tf_op jit(solution)/shard_map/camera/pose/pallas_call | solution.py:665
  79.1 5.6 %collective-permute-start.2 = (f32[32,1,128]{2,1,0:T(1,128)S(1)}, f32[32,1,128]{2,1,0:T(1,128)S(1)}, u32[]{:S(2)}, u32[]{:S(2)}) collective-permute-start(f32[32,1,128]{2,1,0:T(1,128)S(1)} %pose.1), channel_id=1, source_target_pairs={{0,8},{8,0},{16,24},{24,16},{32,40},{40,32},{48,56},{56,48},{64,72... | collective-permute-start | bytes 49160 | tf_op jit(solution)/shard_map/camera/ppermute | solution.py:676
  84.7 0.8 collective-permute-done.2
  85.5 0.6 add.7
  86.2 0.0 all-to-all-done.2.refs_0_
  86.2 7.0 %all-to-all-start.3 = ((f32[32,1,128]{2,1,0:T(1,128)}), f32[32,1,128]{2,1,0:T(1,128)S(1)}, u32[]{:S(2)}, u32[]{:S(2)}) async-start(f32[32,1,128]{2,1,0:T(1,128)} %add.7), calls=%async_computation.3 | async-start | bytes 32768 | tf_op jit(solution)/shard_map/camera/all_to_all | solution.py:678
  93.2 5.1 %update.1 = (f32[59,8,256]{2,1,0:T(8,128)}, f32[59,8,256]{2,1,0:T(8,128)}, f32[59,8,256]{2,1,0:T(8,128)}) custom-call(f32[8,10,4,128]{3,2,1,0:T(4,128)S(1)} %all-to-all-done.2.refs_0_, f32[59,8,256]{2,1,0:T(8,128)S(1)} %bitcast.12, f32[59,8,256]{2,1,0:T(8,128)S(1)} %bitcast.14, f32[59,8,256]{2,1,0:T(8,128)S(1)} %bitcast.15), custom_call_target="tpu_custom_call" | custom-call | tf_op jit(solution)/shard_map/update/update/pallas_call | solution.py:683
  98.3 3.5 %all-to-all-done.3 = f32[32,1,128]{2,1,0:T(1,128)S(1)} async-done(((f32[32,1,128]{2,1,0:T(1,128)}), f32[32,1,128]{2,1,0:T(1,128)S(1)}, u32[]{:S(2)}, u32[]{:S(2)}) %all-to-all-start.3) | async-done | bytes 16416 | tf_op jit(solution)/shard_map/camera/all_to_all | solution.py:678
  101.9 0.6 reduce_sum.11
  (10 shorter events, 0.0 us)
Async XLA Ops:
  2.8 35.1 %copy-start.9 = (bf16[1,2,3,256]{3,1,2,0:T(2,128)(2,1)S(1)}, bf16[1,2,3,256]{3,1,2,0:T(2,128)(2,1)}, u32[]{:S(2)}) copy-start(bf16[1,2,3,256]{3,1,2,0:T(2,128)(2,1)} %param.17) | copy-start | bytes 9220
  31.8 7.6 %collective-permute-start = (f32[32,9,4,128]{3,2,1,0:T(4,128)S(1)}, f32[32,9,4,128]{3,2,1,0:T(4,128)S(1)}, u32[]{:S(2)}, u32[]{:S(2)}) collective-permute-start(f32[32,9,4,128]{3,2,1,0:T(4,128)S(1)} %all_to_all.20.near_ref), channel_id=1, source_target_pairs={{0,8},{8,0},{16,24},{24,16},{32,40},{40,32},{48,56},{56,48},{64,72... | collective-permute-start | bytes 1769480 | tf_op jit(solution)/shard_map/gather/ppermute | solution.py:638
  37.9 1.6 %copy-start.3 = (f32[4,128]{1,0:T(4,128)S(1)}, f32[4,128]{1,0:T(4,128)}, u32[]{:S(2)}) copy-start(f32[4,128]{1,0:T(4,128)} %get-tuple-element.15.extra_ref) | copy-start | bytes 6148
  37.9 1.6 %copy-start.8 = (s32[1,2]{1,0:T(1,128)S(1)}, s32[1,2]{1,0:T(1,128)}, u32[]{:S(2)}) copy-start(s32[1,2]{1,0:T(1,128)} %tile_ref.1) | copy-start | bytes 28
  37.9 1.6 %copy-start.6 = (s32[1,2,4]{2,1,0:T(2,128)S(1)}, s32[1,2,4]{2,1,0:T(2,128)}, u32[]{:S(2)}) copy-start(s32[1,2,4]{2,1,0:T(2,128)} %order_ref.1) | copy-start | bytes 100
  37.9 1.6 %copy-start.7 = (s32[1,2]{1,0:T(1,128)S(1)}, s32[1,2]{1,0:T(1,128)}, u32[]{:S(2)}) copy-start(s32[1,2]{1,0:T(1,128)} %length_ref.1) | copy-start | bytes 28
  44.7 3.9 %collective-permute-start.1 = (f32[144,8,128]{2,1,0:T(8,128)S(1)}, f32[144,8,128]{2,1,0:T(8,128)S(1)}, u32[]{:S(2)}, u32[]{:S(2)}) collective-permute-start(f32[144,8,128]{2,1,0:T(8,128)S(1)} %get-tuple-element.17), channel_id=1, source_target_pairs={{0,8},{8,0},{16,24},{24,16},{32,40},{40,32},{48,56},{56,48},{64,72... | collective-permute-start | bytes 1769480 | tf_op jit(solution)/shard_map/scatter/ppermute | solution.py:651
  69.2 7.7 %copy-start = (f32[8,59,256]{2,0,1:T(8,128)S(1)}, f32[8,59,256]{2,0,1:T(8,128)}, u32[]{:S(2)}) copy-start(f32[8,59,256]{2,0,1:T(8,128)} %param.9) | copy-start | bytes 1449988
  69.9 7.0 %copy-start.4 = (s32[1,2]{1,0:T(1,128)S(1)}, s32[1,2]{1,0:T(1,128)}, u32[]{:S(2)}) copy-start(s32[1,2]{1,0:T(1,128)} %refs_0_.3) | copy-start | bytes 28
  69.9 7.0 %copy-start.5 = (f32[1,6]{1,0:T(1,128)S(1)}, f32[1,6]{1,0:T(1,128)}, u32[]{:S(2)}) copy-start(f32[1,6]{1,0:T(1,128)} %refs_1_.3) | copy-start | bytes 76
  69.9 16.3 %all-to-all-start.2 = ((f32[8,10,4,128]{3,2,1,0:T(4,128)}), f32[8,10,4,128]{3,2,1,0:T(4,128)S(1)}, u32[]{:S(2)}, u32[]{:S(2)}) async-start(f32[8,10,4,128]{3,2,1,0:T(4,128)} %collect.1.own_ref), calls=%async_computation.2 | async-start | bytes 327680 | tf_op jit(solution)/shard_map/collect/all_to_all | solution.py:663
  76.9 16.4 %copy-start.1 = (f32[8,59,256]{2,0,1:T(8,128)S(1)}, f32[8,59,256]{2,0,1:T(8,128)}, u32[]{:S(2)}) copy-start(f32[8,59,256]{2,0,1:T(8,128)} %param.10) | copy-start | bytes 1449988
  76.9 16.4 %copy-start.2 = (f32[8,59,256]{2,0,1:T(8,128)S(1)}, f32[8,59,256]{2,0,1:T(8,128)}, u32[]{:S(2)}) copy-start(f32[8,59,256]{2,0,1:T(8,128)} %param.11) | copy-start | bytes 1449988
  79.1 6.4 %collective-permute-start.2 = (f32[32,1,128]{2,1,0:T(1,128)S(1)}, f32[32,1,128]{2,1,0:T(1,128)S(1)}, u32[]{:S(2)}, u32[]{:S(2)}) collective-permute-start(f32[32,1,128]{2,1,0:T(1,128)S(1)} %pose.1), channel_id=1, source_target_pairs={{0,8},{8,0},{16,24},{24,16},{32,40},{40,32},{48,56},{56,48},{64,72... | collective-permute-start | bytes 49160 | tf_op jit(solution)/shard_map/camera/ppermute | solution.py:676
  86.2 15.7 %all-to-all-start.3 = ((f32[32,1,128]{2,1,0:T(1,128)}), f32[32,1,128]{2,1,0:T(1,128)S(1)}, u32[]{:S(2)}, u32[]{:S(2)}) async-start(f32[32,1,128]{2,1,0:T(1,128)} %add.7), calls=%async_computation.3 | async-start | bytes 32768 | tf_op jit(solution)/shard_map/camera/all_to_all | solution.py:678

commit v6 on v5

--- a/solution.py
+++ b/solution.py
@@ -607,7 +607,7 @@
         message, extra = pl.pallas_call(
             lambda *refs: project_kernel(focal, *refs),
             out_shape=[
-                jax.ShapeDtypeStruct((chips, FEATURES, ROWS, LANES), F32),
+                jax.ShapeDtypeStruct((8, FEATURES, ROWS, LANES), F32),
                 jax.ShapeDtypeStruct((ROWS, LANES), F32),
             ],
             in_specs=[pl.BlockSpec(memory_space=pl.ANY)] * 3,
@@ -634,7 +634,24 @@
             name="slope",
         )(visible_blocks, cameras, gaussians)
     with jax.named_scope("gather"):
-        near = lax.all_to_all(message, "cell", 0, 0, axis_index_groups=same_core, tiled=True)
+        deep, wide = 8, chips // 8
+        z_groups = [
+            [(x * deep + z) * CORES + core for z in range(deep)]
+            for x in range(wide)
+            for core in range(CORES)
+        ]
+        x_groups = [
+            [(x * deep + z) * CORES + core for x in range(wide)]
+            for z in range(deep)
+            for core in range(CORES)
+        ]
+        column = lax.all_to_all(
+            message, "cell", 0, 0, axis_index_groups=z_groups, tiled=True
+        )
+        columns = lax.optimization_barrier(jnp.broadcast_to(column, (wide, *column.shape)))
+        near = lax.all_to_all(
+            columns, "cell", 0, 0, axis_index_groups=x_groups, tiled=True
+        ).reshape(chips, FEATURES, ROWS, LANES)
         far = lax.ppermute(near, "cell", swap)
     with jax.named_scope("render"):
         pairs = jax.ShapeDtypeStruct((chips * FEATURES * ROWS // 8, 8, LANES), F32)

time: 104 us -> 103 us (level)
    all_to_all x1, blocking collectives: 20.5 us -> 18.8 us  [shards(): lax.all_to_all(pair.reshape(near.shape), 'cell', 0, 0, axis_index_groups=...]
    all_to_all x1 -> x2, blocking collectives: 29 us -> 29.9 us  [the longest x1 18.8 us: shards(): lax.all_to_all(message, 'cell', 0, 0, axis_index_groups=z_groups, tiled=T...]
where the time goes in v6:
time: 103 us; the launch traced here: 101 us
  blocking collectives  48.7 us (47%)
  starting transfers between devices  27.7 us (27%)
  Pallas kernels  15.2 us (15%)
  waiting for transfers between devices  7.49 us (7%)
  other arithmetic  1.24 us (1%)
    all_to_all x1, blocking collectives, shards(): lax.all_to_all(pair.reshape(near.shape), 'cell', 0, 0, axis_index_groups=...  18.8 us
    all_to_all x1, blocking collectives, shards(): lax.all_to_all(message, 'cell', 0, 0, axis_index_groups=z_groups, tiled=T...  18.8 us
    all_to_all x1, blocking collectives, shards(): lax.all_to_all(columns, 'cell', 0, 0, axis_index_groups=x_groups, tiled=T...  11.1 us
    all_to_all x1, starting transfers between devices, shards(): lax.all_to_all(camera_copies, 'cell', 0, 0, axis_index_groups=same_core,...  7.04 us
    all_to_all x1, starting transfers between devices, shards(): every = lax.all_to_all(own, 'view', 0, 0, tiled=True)  6.96 us
    ppermute x1, starting transfers between devices, shards(): far = lax.ppermute(near, 'cell', swap)  5.76 us
    ppermute x1, starting transfers between devices, shards(): camera_copies = camera_part + lax.ppermute(camera_part, 'cell', swap)  5.6 us
    pallas_call x1, Pallas kernels, shards(): pl.pallas_call(render_kernel, out_shape=[pairs, pairs, jax.ShapeDtypeStru...  5.2 us
  transfers between devices with their start and end apart: 5, of which 4 were waited for; matrix products, arithmetic and copies ran while one was open for 1% of the time, Pallas kernels for 7%

profile of v6, /device:TPU:1, one launch (start us, length us, event | category | flops | bytes accessed | tf_op | source)
XLA Modules:
  0.0 101.2 jit_solution(4876595302317904202)
XLA Ops:
  0.6 2.0 %project.1 = (f32[8,9,4,128]{3,2,1,0:T(4,128)}, f32[4,128]{1,0:T(4,128)}) custom-call(s32[1,2]{1,0:T(1,128)} %refs_0_.3, f32[1,6]{1,0:T(1,128)} %refs_1_.3, f32[59,8,256]{2,1,0:T(8,128)} %bitcast.11), custom_call_target="tpu_custom_call" | custom-call | tf_op jit(solution)/shard_map/project/project/pallas_call | solution.py:607
  2.6 18.8 %all_to_all.25 = f32[8,9,4,128]{3,2,1,0:T(4,128)S(1)} all-to-all(f32[8,9,4,128]{3,2,1,0:T(4,128)} %get-tuple-element.14), channel_id=1, replica_groups={{0,16,32,48,64,80,96,112},{8,24,40,56,72,88,104,120},{128,144,160,176,1..., dimensions={0} | all-to-all | bytes 294912 | tf_op jit(solution)/shard_map/gather/all_to_all | solution.py:648
  21.4 0.1 broadcast_in_dim.3
  21.5 0.0 copy-start.9
  21.5 11.1 %all_to_all.26 = f32[4,8,9,4,128]{4,3,2,1,0:T(4,128)S(1)} all-to-all(f32[4,8,9,4,128]{4,3,2,1,0:T(4,128)S(1)} %broadcast_in_dim.3), channel_id=1, replica_groups={{0,128,256,384},{8,136,264,392},{16,144,272,400},{24,152,280,408},{32,1..., dimensions={0} | all-to-all | bytes 1179648 | tf_op jit(solution)/shard_map/gather/all_to_all | solution.py:652
  32.6 5.8 %collective-permute-start = (f32[32,9,4,128]{3,2,1,0:T(4,128)S(1)}, f32[32,9,4,128]{3,2,1,0:T(4,128)S(1)}, u32[]{:S(2)}, u32[]{:S(2)}) collective-permute-start(f32[32,9,4,128]{3,2,1,0:T(4,128)S(1)} %bitcast.14), channel_id=1, source_target_pairs={{0,8},{8,0},{16,24},{24,16},{32,40},{40,32},{48,56},{56,48},{64,72... | collective-permute-start | bytes 1769480 | tf_op jit(solution)/shard_map/gather/ppermute | solution.py:655
  38.4 0.0 copy-start.3
  38.4 0.0 copy-start.8
  38.4 0.0 copy-start.6
  38.4 0.0 copy-start.7
  38.5 1.5 %collective-permute-done.far_ref = f32[32,9,4,128]{3,2,1,0:T(4,128)S(1)} collective-permute-done((f32[32,9,4,128]{3,2,1,0:T(4,128)S(1)}, f32[32,9,4,128]{3,2,1,0:T(4,128)S(1)}, u32[]{:S(2)}, u32[]{:S(2)}) %collective-permute-start) | collective-permute-done | bytes 589856 | tf_op jit(solution)/shard_map/gather/ppermute | solution.py:655
  40.0 0.0 copy-done.3
  40.0 5.2 %render.1 = (f32[144,8,128]{2,1,0:T(8,128)S(1)}, f32[144,8,128]{2,1,0:T(8,128)S(1)}, f32[4,128]{1,0:T(4,128)S(1)}) custom-call(s32[1,2,4]{2,1,0:T(2,128)S(1)} %copy-done.6, s32[1,2]{1,0:T(1,128)S(1)} %copy-done.7, s32[1,2]{1,0:T(1,128)S(1)} %copy-done.8, bf16[1,2,3,256]{3,2,1,0:T(4,128)(2,1)S(1)} %copy.13.target_ref, f32[32,9,4,128]{3,2,1,0:T(4,128)S(1)} %bitcast.15, ...), custom_call_target="tpu_custom_call" | custom-call | tf_op jit(solution)/shard_map/render/render/pallas_call | solution.py:658
  45.2 2.3 %collective-permute-start.1 = (f32[144,8,128]{2,1,0:T(8,128)S(1)}, f32[144,8,128]{2,1,0:T(8,128)S(1)}, u32[]{:S(2)}, u32[]{:S(2)}) collective-permute-start(f32[144,8,128]{2,1,0:T(8,128)S(1)} %get-tuple-element.17), channel_id=1, source_target_pairs={{0,8},{8,0},{16,24},{24,16},{32,40},{40,32},{48,56},{56,48},{64,72... | collective-permute-start | bytes 1769480 | tf_op jit(solution)/shard_map/scatter/ppermute | solution.py:668
  47.5 1.6 %collective-permute-done.1 = f32[144,8,128]{2,1,0:T(8,128)S(1)} collective-permute-done((f32[144,8,128]{2,1,0:T(8,128)S(1)}, f32[144,8,128]{2,1,0:T(8,128)S(1)}, u32[]{:S(2)}, u32[]{:S(2)}) %collective-permute-start.1) | collective-permute-done | bytes 589856 | tf_op jit(solution)/shard_map/scatter/ppermute | solution.py:668
  49.1 0.1 add.6
  49.2 18.8 %all_to_all.27 = f32[32,9,4,128]{3,2,1,0:T(4,128)S(1)} all-to-all(f32[32,9,4,128]{3,2,1,0:T(4,128)S(1)} %bitcast.19), channel_id=1, replica_groups={{0,16,32,48,64,80,96,112,128,144,160,176,192,208,224,240,256,272,288,30..., dimensions={0} | all-to-all | bytes 1179648 | tf_op jit(solution)/shard_map/scatter/all_to_all | solution.py:669
  68.0 0.7 collect.1.own_ref
  68.7 7.0 %all-to-all-start.3 = ((f32[8,10,4,128]{3,2,1,0:T(4,128)}), f32[8,10,4,128]{3,2,1,0:T(4,128)S(1)}, u32[]{:S(2)}, u32[]{:S(2)}) async-start(f32[8,10,4,128]{3,2,1,0:T(4,128)} %collect.1.own_ref), calls=%async_computation.3 | async-start | bytes 327680 | tf_op jit(solution)/shard_map/collect/all_to_all | solution.py:680
  75.7 0.0 copy-start.1
  75.7 0.0 copy-start.2
  75.7 1.2 %slope.1.slope_ref = f32[6,9,4,128]{3,2,1,0:T(4,128)S(1)} custom-call(s32[1,2]{1,0:T(1,128)S(1)} %copy-done.4, f32[1,6]{1,0:T(1,128)S(1)} %copy-done.5, f32[59,8,256]{2,1,0:T(8,128)S(1)} %bitcast.12), custom_call_target="tpu_custom_call" | custom-call | flops 4000000 | bytes 200000 | tf_op jit(solution)/shard_map/project/slope/pallas_call | solution.py:625
  76.9 1.0 %pose.1 = f32[32,1,128]{2,1,0:T(1,128)S(1)} custom-call(f32[8,10,4,128]{3,2,1,0:T(4,128)} %collect.1.own_ref, f32[6,9,4,128]{3,2,1,0:T(4,128)S(1)} %slope.1.slope_ref), custom_call_target="tpu_custom_call" | custom-call | flops 100000 | bytes 250000 | tf_op jit(solution)/shard_map/camera/pose/pallas_call | solution.py:682
  78.0 5.6 %collective-permute-start.2 = (f32[32,1,128]{2,1,0:T(1,128)S(1)}, f32[32,1,128]{2,1,0:T(1,128)S(1)}, u32[]{:S(2)}, u32[]{:S(2)}) collective-permute-start(f32[32,1,128]{2,1,0:T(1,128)S(1)} %pose.1), channel_id=1, source_target_pairs={{0,8},{8,0},{16,24},{24,16},{32,40},{40,32},{48,56},{56,48},{64,72... | collective-permute-start | bytes 49160 | tf_op jit(solution)/shard_map/camera/ppermute | solution.py:693
  83.6 0.8 collective-permute-done.2
  84.4 0.6 add.7
  85.0 0.0 all-to-all-done.3.refs_0_
  85.0 7.0 %all-to-all-start.4 = ((f32[32,1,128]{2,1,0:T(1,128)}), f32[32,1,128]{2,1,0:T(1,128)S(1)}, u32[]{:S(2)}, u32[]{:S(2)}) async-start(f32[32,1,128]{2,1,0:T(1,128)} %add.7), calls=%async_computation.4 | async-start | bytes 32768 | tf_op jit(solution)/shard_map/camera/all_to_all | solution.py:695
  92.1 0.0 copy-done.1
  92.1 5.1 %update.1 = (f32[59,8,256]{2,1,0:T(8,128)}, f32[59,8,256]{2,1,0:T(8,128)}, f32[59,8,256]{2,1,0:T(8,128)}) custom-call(f32[8,10,4,128]{3,2,1,0:T(4,128)S(1)} %all-to-all-done.3.refs_0_, f32[59,8,256]{2,1,0:T(8,128)S(1)} %bitcast.13, f32[59,8,256]{2,1,0:T(8,128)S(1)} %bitcast.17, f32[59,8,256]{2,1,0:T(8,128)S(1)} %bitcast.18), custom_call_target="tpu_custom_call" | custom-call | tf_op jit(solution)/shard_map/update/update/pallas_call | solution.py:700
  97.2 3.5 %all-to-all-done.4 = f32[32,1,128]{2,1,0:T(1,128)S(1)} async-done(((f32[32,1,128]{2,1,0:T(1,128)}), f32[32,1,128]{2,1,0:T(1,128)S(1)}, u32[]{:S(2)}, u32[]{:S(2)}) %all-to-all-start.4) | async-done | bytes 16416 | tf_op jit(solution)/shard_map/camera/all_to_all | solution.py:695
  100.7 0.6 reduce_sum.11
  (12 shorter events, 0.0 us)
Async XLA Ops:
  21.5 16.9 %copy-start.9 = (bf16[1,2,3,256]{3,1,2,0:T(2,128)(2,1)S(1)}, bf16[1,2,3,256]{3,1,2,0:T(2,128)(2,1)}, u32[]{:S(2)}) copy-start(bf16[1,2,3,256]{3,1,2,0:T(2,128)(2,1)} %param.17) | copy-start | bytes 9220
  32.6 7.4 %collective-permute-start = (f32[32,9,4,128]{3,2,1,0:T(4,128)S(1)}, f32[32,9,4,128]{3,2,1,0:T(4,128)S(1)}, u32[]{:S(2)}, u32[]{:S(2)}) collective-permute-start(f32[32,9,4,128]{3,2,1,0:T(4,128)S(1)} %bitcast.14), channel_id=1, source_target_pairs={{0,8},{8,0},{16,24},{24,16},{32,40},{40,32},{48,56},{56,48},{64,72... | collective-permute-start | bytes 1769480 | tf_op jit(solution)/shard_map/gather/ppermute | solution.py:655
  38.4 1.6 %copy-start.3 = (f32[4,128]{1,0:T(4,128)S(1)}, f32[4,128]{1,0:T(4,128)}, u32[]{:S(2)}) copy-start(f32[4,128]{1,0:T(4,128)} %get-tuple-element.15.extra_ref) | copy-start | bytes 6148
  38.4 1.6 %copy-start.8 = (s32[1,2]{1,0:T(1,128)S(1)}, s32[1,2]{1,0:T(1,128)}, u32[]{:S(2)}) copy-start(s32[1,2]{1,0:T(1,128)} %tile_ref.1) | copy-start | bytes 28
  38.4 1.6 %copy-start.6 = (s32[1,2,4]{2,1,0:T(2,128)S(1)}, s32[1,2,4]{2,1,0:T(2,128)}, u32[]{:S(2)}) copy-start(s32[1,2,4]{2,1,0:T(2,128)} %order_ref.1) | copy-start | bytes 100
  38.4 1.6 %copy-start.7 = (s32[1,2]{1,0:T(1,128)S(1)}, s32[1,2]{1,0:T(1,128)}, u32[]{:S(2)}) copy-start(s32[1,2]{1,0:T(1,128)} %length_ref.1) | copy-start | bytes 28
  45.2 3.9 %collective-permute-start.1 = (f32[144,8,128]{2,1,0:T(8,128)S(1)}, f32[144,8,128]{2,1,0:T(8,128)S(1)}, u32[]{:S(2)}, u32[]{:S(2)}) collective-permute-start(f32[144,8,128]{2,1,0:T(8,128)S(1)} %get-tuple-element.17), channel_id=1, source_target_pairs={{0,8},{8,0},{16,24},{24,16},{32,40},{40,32},{48,56},{56,48},{64,72... | collective-permute-start | bytes 1769480 | tf_op jit(solution)/shard_map/scatter/ppermute | solution.py:668
  68.0 7.7 %copy-start = (f32[8,59,256]{2,0,1:T(8,128)S(1)}, f32[8,59,256]{2,0,1:T(8,128)}, u32[]{:S(2)}) copy-start(f32[8,59,256]{2,0,1:T(8,128)} %param.9) | copy-start | bytes 1449988
  68.7 7.0 %copy-start.4 = (s32[1,2]{1,0:T(1,128)S(1)}, s32[1,2]{1,0:T(1,128)}, u32[]{:S(2)}) copy-start(s32[1,2]{1,0:T(1,128)} %refs_0_.3) | copy-start | bytes 28
  68.7 7.0 %copy-start.5 = (f32[1,6]{1,0:T(1,128)S(1)}, f32[1,6]{1,0:T(1,128)}, u32[]{:S(2)}) copy-start(f32[1,6]{1,0:T(1,128)} %refs_1_.3) | copy-start | bytes 76
  68.7 16.3 %all-to-all-start.3 = ((f32[8,10,4,128]{3,2,1,0:T(4,128)}), f32[8,10,4,128]{3,2,1,0:T(4,128)S(1)}, u32[]{:S(2)}, u32[]{:S(2)}) async-start(f32[8,10,4,128]{3,2,1,0:T(4,128)} %collect.1.own_ref), calls=%async_computation.3 | async-start | bytes 327680 | tf_op jit(solution)/shard_map/collect/all_to_all | solution.py:680
  75.7 16.4 %copy-start.1 = (f32[8,59,256]{2,0,1:T(8,128)S(1)}, f32[8,59,256]{2,0,1:T(8,128)}, u32[]{:S(2)}) copy-start(f32[8,59,256]{2,0,1:T(8,128)} %param.10) | copy-start | bytes 1449988
  75.7 16.4 %copy-start.2 = (f32[8,59,256]{2,0,1:T(8,128)S(1)}, f32[8,59,256]{2,0,1:T(8,128)}, u32[]{:S(2)}) copy-start(f32[8,59,256]{2,0,1:T(8,128)} %param.11) | copy-start | bytes 1449988
  78.0 6.4 %collective-permute-start.2 = (f32[32,1,128]{2,1,0:T(1,128)S(1)}, f32[32,1,128]{2,1,0:T(1,128)S(1)}, u32[]{:S(2)}, u32[]{:S(2)}) collective-permute-start(f32[32,1,128]{2,1,0:T(1,128)S(1)} %pose.1), channel_id=1, source_target_pairs={{0,8},{8,0},{16,24},{24,16},{32,40},{40,32},{48,56},{56,48},{64,72... | collective-permute-start | bytes 49160 | tf_op jit(solution)/shard_map/camera/ppermute | solution.py:693
  85.0 15.7 %all-to-all-start.4 = ((f32[32,1,128]{2,1,0:T(1,128)}), f32[32,1,128]{2,1,0:T(1,128)S(1)}, u32[]{:S(2)}, u32[]{:S(2)}) async-start(f32[32,1,128]{2,1,0:T(1,128)} %add.7), calls=%async_computation.4 | async-start | bytes 32768 | tf_op jit(solution)/shard_map/camera/all_to_all | solution.py:695

commit v7 on v6

--- a/solution.py
+++ b/solution.py
@@ -186,6 +186,7 @@
     visible_ref,
     camera_ref,
     gauss_ref,
+    basis_scr,
     small_done,
     large_done,
 ):
@@ -216,12 +217,22 @@
     for i, value in enumerate(values):
         extra = jnp.where(place == i, value, extra)
     extra_ref[...] = extra
-    for copy in large:
-        copy.wait()
-    features = features_of(halves_of(gauss_ref), camera_rows(camera_ref), focal)
+    large[0].wait()
+    whole = halves_of(gauss_ref)
     picked = pick(visible_ref, owned)
-    for f in range(FEATURES):
-        out_ref[0, f] = jnp.concatenate(picked(features[f]), axis=0)
+    frame = [
+        jnp.broadcast_to(entry, (HALVES * owned, LANES))
+        for entry in camera_frame(camera_rows(camera_ref))
+    ]
+    factor = shape_factor([whole(3 + i) for i in range(3)], [whole(6 + i) for i in range(4)])
+    seen = view_of([whole(i) for i in range(3)], factor, frame, *focal)
+    basis_scr[...] = jnp.stack(seen[5:])
+    for f, feature in enumerate(seen[:5] + [sigmoid(whole(10))]):
+        out_ref[0, f] = jnp.concatenate(picked(feature), axis=0)
+    for channel in range(3):
+        large[1 + channel].wait()
+        summed = colour_sum(basis_scr, lambda c, k: whole(11 + 16 * c + k), channel)
+        out_ref[0, 6 + channel] = jnp.concatenate(picked(jnp.maximum(summed, 0.0)), axis=0)
     message = out_ref[0]
     for i in range(1, out_ref.shape[0]):
         out_ref[i] = message
@@ -616,6 +627,7 @@
                 pltpu.SMEM(visible_blocks.shape, jnp.int32),
                 pltpu.SMEM(cameras.shape, F32),
                 pltpu.VMEM(gaussians.shape, F32),
+                pltpu.VMEM((15, HALVES * owned, LANES), F32),
                 pltpu.SemaphoreType.DMA((2,)),
                 pltpu.SemaphoreType.DMA((4,)),
             ],

time: 103 us -> 103 us (level)
  no operation moved by 1% of the time
where the time goes in v7:
time: 103 us; the launch traced here: 101 us
  blocking collectives  48.7 us (47%)
  starting transfers between devices  27.6 us (27%)
  Pallas kernels  15.1 us (15%)
  waiting for transfers between devices  7.49 us (7%)
  other arithmetic  1.24 us (1%)
    all_to_all x1, blocking collectives, shards(): lax.all_to_all(pair.reshape(near.shape), 'cell', 0, 0, axis_index_groups=...  18.8 us
    all_to_all x1, blocking collectives, shards(): lax.all_to_all(message, 'cell', 0, 0, axis_index_groups=z_groups, tiled=T...  18.8 us
    all_to_all x1, blocking collectives, shards(): lax.all_to_all(columns, 'cell', 0, 0, axis_index_groups=x_groups, tiled=T...  11.1 us
    all_to_all x1, starting transfers between devices, shards(): lax.all_to_all(camera_copies, 'cell', 0, 0, axis_index_groups=same_core,...  7.04 us
    all_to_all x1, starting transfers between devices, shards(): every = lax.all_to_all(own, 'view', 0, 0, tiled=True)  6.95 us
    ppermute x1, starting transfers between devices, shards(): far = lax.ppermute(near, 'cell', swap)  5.76 us
    ppermute x1, starting transfers between devices, shards(): camera_copies = camera_part + lax.ppermute(camera_part, 'cell', swap)  5.6 us
    pallas_call x1, Pallas kernels, shards(): pl.pallas_call(render_kernel, out_shape=[pairs, pairs, jax.ShapeDtypeStru...  5.21 us
  transfers between devices with their start and end apart: 5, of which 4 were waited for; matrix products, arithmetic and copies ran while one was open for 1% of the time, Pallas kernels for 7%

profile of v7, /device:TPU:1, one launch (start us, length us, event | category | flops | bytes accessed | tf_op | source)
XLA Modules:
  0.0 101.1 jit_solution(13935369327781246998)
XLA Ops:
  0.6 1.8 %project.1 = (f32[8,9,4,128]{3,2,1,0:T(4,128)}, f32[4,128]{1,0:T(4,128)}) custom-call(s32[1,2]{1,0:T(1,128)} %refs_0_.3, f32[1,6]{1,0:T(1,128)} %refs_1_.3, f32[59,8,256]{2,1,0:T(8,128)} %bitcast.11), custom_call_target="tpu_custom_call" | custom-call | tf_op jit(solution)/shard_map/project/project/pallas_call | solution.py:618
  2.5 18.8 %all_to_all.25 = f32[8,9,4,128]{3,2,1,0:T(4,128)S(1)} all-to-all(f32[8,9,4,128]{3,2,1,0:T(4,128)} %get-tuple-element.14), channel_id=1, replica_groups={{0,16,32,48,64,80,96,112},{8,24,40,56,72,88,104,120},{128,144,160,176,1..., dimensions={0} | all-to-all | bytes 294912 | tf_op jit(solution)/shard_map/gather/all_to_all | solution.py:660
  21.3 0.1 broadcast_in_dim.3
  21.3 0.0 copy-start.9
  21.4 11.1 %all_to_all.26 = f32[4,8,9,4,128]{4,3,2,1,0:T(4,128)S(1)} all-to-all(f32[4,8,9,4,128]{4,3,2,1,0:T(4,128)S(1)} %broadcast_in_dim.3), channel_id=1, replica_groups={{0,128,256,384},{8,136,264,392},{16,144,272,400},{24,152,280,408},{32,1..., dimensions={0} | all-to-all | bytes 1179648 | tf_op jit(solution)/shard_map/gather/all_to_all | solution.py:664
  32.5 5.8 %collective-permute-start = (f32[32,9,4,128]{3,2,1,0:T(4,128)S(1)}, f32[32,9,4,128]{3,2,1,0:T(4,128)S(1)}, u32[]{:S(2)}, u32[]{:S(2)}) collective-permute-start(f32[32,9,4,128]{3,2,1,0:T(4,128)S(1)} %bitcast.14), channel_id=1, source_target_pairs={{0,8},{8,0},{16,24},{24,16},{32,40},{40,32},{48,56},{56,48},{64,72... | collective-permute-start | bytes 1769480 | tf_op jit(solution)/shard_map/gather/ppermute | solution.py:667
  38.2 0.0 copy-start.3
  38.3 0.0 copy-start.8
  38.3 0.0 copy-start.6
  38.3 0.0 copy-start.7
  38.3 1.5 %collective-permute-done.far_ref = f32[32,9,4,128]{3,2,1,0:T(4,128)S(1)} collective-permute-done((f32[32,9,4,128]{3,2,1,0:T(4,128)S(1)}, f32[32,9,4,128]{3,2,1,0:T(4,128)S(1)}, u32[]{:S(2)}, u32[]{:S(2)}) %collective-permute-start) | collective-permute-done | bytes 589856 | tf_op jit(solution)/shard_map/gather/ppermute | solution.py:667
  39.9 5.2 %render.1 = (f32[144,8,128]{2,1,0:T(8,128)S(1)}, f32[144,8,128]{2,1,0:T(8,128)S(1)}, f32[4,128]{1,0:T(4,128)S(1)}) custom-call(s32[1,2,4]{2,1,0:T(2,128)S(1)} %copy-done.6, s32[1,2]{1,0:T(1,128)S(1)} %copy-done.7, s32[1,2]{1,0:T(1,128)S(1)} %copy-done.8, bf16[1,2,3,256]{3,2,1,0:T(4,128)(2,1)S(1)} %copy.13.target_ref, f32[32,9,4,128]{3,2,1,0:T(4,128)S(1)} %bitcast.15, ...), custom_call_target="tpu_custom_call" | custom-call | tf_op jit(solution)/shard_map/render/render/pallas_call | solution.py:670
  45.1 2.3 %collective-permute-start.1 = (f32[144,8,128]{2,1,0:T(8,128)S(1)}, f32[144,8,128]{2,1,0:T(8,128)S(1)}, u32[]{:S(2)}, u32[]{:S(2)}) collective-permute-start(f32[144,8,128]{2,1,0:T(8,128)S(1)} %get-tuple-element.17), channel_id=1, source_target_pairs={{0,8},{8,0},{16,24},{24,16},{32,40},{40,32},{48,56},{56,48},{64,72... | collective-permute-start | bytes 1769480 | tf_op jit(solution)/shard_map/scatter/ppermute | solution.py:680
  47.4 1.6 %collective-permute-done.1 = f32[144,8,128]{2,1,0:T(8,128)S(1)} collective-permute-done((f32[144,8,128]{2,1,0:T(8,128)S(1)}, f32[144,8,128]{2,1,0:T(8,128)S(1)}, u32[]{:S(2)}, u32[]{:S(2)}) %collective-permute-start.1) | collective-permute-done | bytes 589856 | tf_op jit(solution)/shard_map/scatter/ppermute | solution.py:680
  49.0 0.1 add.6
  49.0 18.8 %all_to_all.27 = f32[32,9,4,128]{3,2,1,0:T(4,128)S(1)} all-to-all(f32[32,9,4,128]{3,2,1,0:T(4,128)S(1)} %bitcast.19), channel_id=1, replica_groups={{0,16,32,48,64,80,96,112,128,144,160,176,192,208,224,240,256,272,288,30..., dimensions={0} | all-to-all | bytes 1179648 | tf_op jit(solution)/shard_map/scatter/all_to_all | solution.py:681
  67.9 0.7 collect.1.own_ref
  68.6 7.0 %all-to-all-start.3 = ((f32[8,10,4,128]{3,2,1,0:T(4,128)}), f32[8,10,4,128]{3,2,1,0:T(4,128)S(1)}, u32[]{:S(2)}, u32[]{:S(2)}) async-start(f32[8,10,4,128]{3,2,1,0:T(4,128)} %collect.1.own_ref), calls=%async_computation.3 | async-start | bytes 327680 | tf_op jit(solution)/shard_map/collect/all_to_all | solution.py:692
  75.6 0.0 copy-start.1
  75.6 0.0 copy-start.2
  75.6 1.2 %slope.1.slope_ref = f32[6,9,4,128]{3,2,1,0:T(4,128)S(1)} custom-call(s32[1,2]{1,0:T(1,128)S(1)} %copy-done.4, f32[1,6]{1,0:T(1,128)S(1)} %copy-done.5, f32[59,8,256]{2,1,0:T(8,128)S(1)} %bitcast.12), custom_call_target="tpu_custom_call" | custom-call | flops 4000000 | bytes 200000 | tf_op jit(solution)/shard_map/project/slope/pallas_call | solution.py:637
  76.8 1.0 %pose.1 = f32[32,1,128]{2,1,0:T(1,128)S(1)} custom-call(f32[8,10,4,128]{3,2,1,0:T(4,128)} %collect.1.own_ref, f32[6,9,4,128]{3,2,1,0:T(4,128)S(1)} %slope.1.slope_ref), custom_call_target="tpu_custom_call" | custom-call | flops 100000 | bytes 250000 | tf_op jit(solution)/shard_map/camera/pose/pallas_call | solution.py:694
  77.8 5.6 %collective-permute-start.2 = (f32[32,1,128]{2,1,0:T(1,128)S(1)}, f32[32,1,128]{2,1,0:T(1,128)S(1)}, u32[]{:S(2)}, u32[]{:S(2)}) collective-permute-start(f32[32,1,128]{2,1,0:T(1,128)S(1)} %pose.1), channel_id=1, source_target_pairs={{0,8},{8,0},{16,24},{24,16},{32,40},{40,32},{48,56},{56,48},{64,72... | collective-permute-start | bytes 49160 | tf_op jit(solution)/shard_map/camera/ppermute | solution.py:705
  83.4 0.8 collective-permute-done.2
  84.2 0.6 add.7
  84.9 0.0 all-to-all-done.3.refs_0_
  84.9 7.0 %all-to-all-start.4 = ((f32[32,1,128]{2,1,0:T(1,128)}), f32[32,1,128]{2,1,0:T(1,128)S(1)}, u32[]{:S(2)}, u32[]{:S(2)}) async-start(f32[32,1,128]{2,1,0:T(1,128)} %add.7), calls=%async_computation.4 | async-start | bytes 32768 | tf_op jit(solution)/shard_map/camera/all_to_all | solution.py:707
  91.9 0.0 copy-done.1
  91.9 0.0 copy-done.2
  91.9 5.1 %update.1 = (f32[59,8,256]{2,1,0:T(8,128)}, f32[59,8,256]{2,1,0:T(8,128)}, f32[59,8,256]{2,1,0:T(8,128)}) custom-call(f32[8,10,4,128]{3,2,1,0:T(4,128)S(1)} %all-to-all-done.3.refs_0_, f32[59,8,256]{2,1,0:T(8,128)S(1)} %bitcast.13, f32[59,8,256]{2,1,0:T(8,128)S(1)} %bitcast.17, f32[59,8,256]{2,1,0:T(8,128)S(1)} %bitcast.18), custom_call_target="tpu_custom_call" | custom-call | tf_op jit(solution)/shard_map/update/update/pallas_call | solution.py:712
  97.0 3.5 %all-to-all-done.4 = f32[32,1,128]{2,1,0:T(1,128)S(1)} async-done(((f32[32,1,128]{2,1,0:T(1,128)}), f32[32,1,128]{2,1,0:T(1,128)S(1)}, u32[]{:S(2)}, u32[]{:S(2)}) %all-to-all-start.4) | async-done | bytes 16416 | tf_op jit(solution)/shard_map/camera/all_to_all | solution.py:707
  100.5 0.6 reduce_sum.11
  (12 shorter events, 0.0 us)
Async XLA Ops:
  21.3 16.9 %copy-start.9 = (bf16[1,2,3,256]{3,1,2,0:T(2,128)(2,1)S(1)}, bf16[1,2,3,256]{3,1,2,0:T(2,128)(2,1)}, u32[]{:S(2)}) copy-start(bf16[1,2,3,256]{3,1,2,0:T(2,128)(2,1)} %param.17) | copy-start | bytes 9220
  32.5 7.4 %collective-permute-start = (f32[32,9,4,128]{3,2,1,0:T(4,128)S(1)}, f32[32,9,4,128]{3,2,1,0:T(4,128)S(1)}, u32[]{:S(2)}, u32[]{:S(2)}) collective-permute-start(f32[32,9,4,128]{3,2,1,0:T(4,128)S(1)} %bitcast.14), channel_id=1, source_target_pairs={{0,8},{8,0},{16,24},{24,16},{32,40},{40,32},{48,56},{56,48},{64,72... | collective-permute-start | bytes 1769480 | tf_op jit(solution)/shard_map/gather/ppermute | solution.py:667
  38.2 1.6 %copy-start.3 = (f32[4,128]{1,0:T(4,128)S(1)}, f32[4,128]{1,0:T(4,128)}, u32[]{:S(2)}) copy-start(f32[4,128]{1,0:T(4,128)} %get-tuple-element.15.extra_ref) | copy-start | bytes 6148
  38.3 1.6 %copy-start.8 = (s32[1,2]{1,0:T(1,128)S(1)}, s32[1,2]{1,0:T(1,128)}, u32[]{:S(2)}) copy-start(s32[1,2]{1,0:T(1,128)} %tile_ref.1) | copy-start | bytes 28
  38.3 1.6 %copy-start.6 = (s32[1,2,4]{2,1,0:T(2,128)S(1)}, s32[1,2,4]{2,1,0:T(2,128)}, u32[]{:S(2)}) copy-start(s32[1,2,4]{2,1,0:T(2,128)} %order_ref.1) | copy-start | bytes 100
  38.3 1.6 %copy-start.7 = (s32[1,2]{1,0:T(1,128)S(1)}, s32[1,2]{1,0:T(1,128)}, u32[]{:S(2)}) copy-start(s32[1,2]{1,0:T(1,128)} %length_ref.1) | copy-start | bytes 28
  45.1 3.9 %collective-permute-start.1 = (f32[144,8,128]{2,1,0:T(8,128)S(1)}, f32[144,8,128]{2,1,0:T(8,128)S(1)}, u32[]{:S(2)}, u32[]{:S(2)}) collective-permute-start(f32[144,8,128]{2,1,0:T(8,128)S(1)} %get-tuple-element.17), channel_id=1, source_target_pairs={{0,8},{8,0},{16,24},{24,16},{32,40},{40,32},{48,56},{56,48},{64,72... | collective-permute-start | bytes 1769480 | tf_op jit(solution)/shard_map/scatter/ppermute | solution.py:680
  67.8 7.7 %copy-start = (f32[8,59,256]{2,0,1:T(8,128)S(1)}, f32[8,59,256]{2,0,1:T(8,128)}, u32[]{:S(2)}) copy-start(f32[8,59,256]{2,0,1:T(8,128)} %param.9) | copy-start | bytes 1449988
  68.6 7.0 %copy-start.4 = (s32[1,2]{1,0:T(1,128)S(1)}, s32[1,2]{1,0:T(1,128)}, u32[]{:S(2)}) copy-start(s32[1,2]{1,0:T(1,128)} %refs_0_.3) | copy-start | bytes 28
  68.6 7.0 %copy-start.5 = (f32[1,6]{1,0:T(1,128)S(1)}, f32[1,6]{1,0:T(1,128)}, u32[]{:S(2)}) copy-start(f32[1,6]{1,0:T(1,128)} %refs_1_.3) | copy-start | bytes 76
  68.6 16.3 %all-to-all-start.3 = ((f32[8,10,4,128]{3,2,1,0:T(4,128)}), f32[8,10,4,128]{3,2,1,0:T(4,128)S(1)}, u32[]{:S(2)}, u32[]{:S(2)}) async-start(f32[8,10,4,128]{3,2,1,0:T(4,128)} %collect.1.own_ref), calls=%async_computation.3 | async-start | bytes 327680 | tf_op jit(solution)/shard_map/collect/all_to_all | solution.py:692
  75.6 16.4 %copy-start.1 = (f32[8,59,256]{2,0,1:T(8,128)S(1)}, f32[8,59,256]{2,0,1:T(8,128)}, u32[]{:S(2)}) copy-start(f32[8,59,256]{2,0,1:T(8,128)} %param.10) | copy-start | bytes 1449988
  75.6 16.4 %copy-start.2 = (f32[8,59,256]{2,0,1:T(8,128)S(1)}, f32[8,59,256]{2,0,1:T(8,128)}, u32[]{:S(2)}) copy-start(f32[8,59,256]{2,0,1:T(8,128)} %param.11) | copy-start | bytes 1449988
  77.8 6.4 %collective-permute-start.2 = (f32[32,1,128]{2,1,0:T(1,128)S(1)}, f32[32,1,128]{2,1,0:T(1,128)S(1)}, u32[]{:S(2)}, u32[]{:S(2)}) collective-permute-start(f32[32,1,128]{2,1,0:T(1,128)S(1)} %pose.1), channel_id=1, source_target_pairs={{0,8},{8,0},{16,24},{24,16},{32,40},{40,32},{48,56},{56,48},{64,72... | collective-permute-start | bytes 49160 | tf_op jit(solution)/shard_map/camera/ppermute | solution.py:705
  84.9 15.7 %all-to-all-start.4 = ((f32[32,1,128]{2,1,0:T(1,128)}), f32[32,1,128]{2,1,0:T(1,128)S(1)}, u32[]{:S(2)}, u32[]{:S(2)}) async-start(f32[32,1,128]{2,1,0:T(1,128)} %add.7), calls=%async_computation.4 | async-start | bytes 32768 | tf_op jit(solution)/shard_map/camera/all_to_all | solution.py:707
